TPU v7x, 512 devices: a whole 4x8x8 slice. The times are simulated.
512 devices in a mesh: band: 32 (over z_hi, x, core), grid: 16 (over y, z_lo).
Axes of the slice: x: 4, y: 8, z: 8 (z_hi: 4, z_lo: 2; z = z_hi * 2 + z_lo), core: 2. Of those that a mesh axis runs over, the one named last changes fastest.
Arguments:
- orbitals: bfloat16 [32, 96, 9216], P('band', 'grid'), may hold values from -6 to 6
Outputs:
- exchanged: float32 [32, 96, 9216], P('band', 'grid')
All inputs are finite; a program needn't handle non-finite values.
Results may differ from a plain program's by a relative error of at most 0.0003.
Values may be sent and summed in bfloat16 or wider, within the bound.
No kernel may reach another device: no remote copies, remote signals or barrier semaphores. Data moves between devices by JAX's collectives and lax.ppermute only.
A program may use at most 64 MiB of HBM per device.

v0:
```python
import math

import jax
import jax.numpy as jnp
from jax import lax
from jax.sharding import PartitionSpec as P

MIXING = 0.25
SPACING = 0.31
SCREENING = 0.106


def shifted(array, axis, by):
    peers = lax.axis_size(axis)
    return lax.ppermute(array, axis, [(i, (i + by) % peers) for i in range(peers)])


def kernel_values(index_x, index_y, index_z, length):

    def wavenumber(positions):
        signed = jnp.where(positions * 2 < length, positions, positions - length).astype(
            jnp.float32
        )
        return signed * (2.0 * math.pi / (length * SPACING))

    wave_x = wavenumber(index_x)[:, None, None]
    wave_y = wavenumber(index_y)[None, :, None]
    wave_z = wavenumber(index_z)[None, None, :]
    square = wave_x * wave_x + wave_y * wave_y + wave_z * wave_z
    safe_square = jnp.where(square > 0, square, 1.0)
    values = (
        4.0 * math.pi * (1.0 - jnp.exp(-safe_square / (4.0 * SCREENING * SCREENING))) / safe_square
    )
    return jnp.where(square > 0, values, 0.0)


def hartley_table(length):
    row_index = jnp.arange(length, dtype=jnp.int32)
    product_index = row_index[:, None] * row_index[None, :] % length
    phases = product_index.astype(jnp.float32) * (2.0 * math.pi / length)
    return jnp.cos(phases) + jnp.sin(phases)


def plane_transform(field_cells, cas_table):
    section = jnp.einsum("pxyz,kz->pxyk", field_cells, cas_table, precision=lax.Precision.HIGHEST)
    return jnp.einsum("pxyz,ky->pxkz", section, cas_table, precision=lax.Precision.HIGHEST)


def potentials(own_bands, visitors, cas_table, kernel_local):
    left_count = own_bands.shape[0]
    right_count = visitors.shape[0]
    slab_rows = own_bands.shape[1]
    length = cas_table.shape[0]
    density = own_bands.astype(jnp.float32)[:, None] * visitors.astype(jnp.float32)[None]
    density = density.reshape(left_count * right_count, slab_rows, length, length)
    spectrum = plane_transform(density, cas_table)
    moved = jnp.einsum(
        "pxyz,kx->pkyz",
        lax.all_to_all(spectrum, "grid", split_axis=2, concat_axis=1, tiled=True),
        cas_table,
        precision=lax.Precision.HIGHEST,
    )
    moved = moved * kernel_local[None]
    moved = jnp.einsum("pkyz,kx->pxyz", moved, cas_table, precision=lax.Precision.HIGHEST)
    potential = lax.all_to_all(moved, "grid", split_axis=1, concat_axis=2, tiled=True)
    potential = plane_transform(potential, cas_table)
    return potential.reshape(left_count, right_count, slab_rows, length * length)


def own_update(potential, visitors):
    return jnp.einsum(
        "acxg,cxg->axg", potential, visitors.astype(jnp.float32), precision=lax.Precision.HIGHEST
    )


def visitor_update(potential, own_bands):
    return jnp.einsum(
        "acxg,axg->cxg", potential, own_bands.astype(jnp.float32), precision=lax.Precision.HIGHEST
    )


def body(orbitals):
    slab_rows = orbitals.shape[1]
    length = slab_rows * lax.axis_size("grid")
    cas_table = hartley_table(length)
    offset = lax.axis_index("grid") * slab_rows
    span_index = jnp.arange(length, dtype=jnp.int32)
    slab_index = offset + jnp.arange(slab_rows, dtype=jnp.int32)
    kernel_local = kernel_values(span_index, slab_index, span_index, length) / float(length) ** 3
    cycle_size = lax.axis_size("band")
    half_cycle = cycle_size // 2
    own_terms = own_update(potentials(orbitals, orbitals, cas_table, kernel_local), orbitals)
    empty_terms = jnp.zeros(orbitals.shape, jnp.float32)

    def advance(cycle_state, offset_step):
        visitor, carried, gathered = cycle_state
        visitor = shifted(visitor, "band", 1)
        carried = shifted(carried, "band", 1)
        potential = potentials(orbitals, visitor, cas_table, kernel_local)
        gathered = gathered + own_update(potential, visitor)
        keep_mask = jnp.where(2 * offset_step == cycle_size, 0.0, 1.0)
        carried = carried + keep_mask * visitor_update(potential, orbitals)
        return ((visitor, carried, gathered), None)

    cycle_state, unused_rows = lax.scan(
        advance, (orbitals, empty_terms, own_terms), jnp.arange(1, half_cycle + 1, dtype=jnp.int32)
    )
    carried = cycle_state[1]
    own_terms = cycle_state[2]
    returned = shifted(carried, "band", half_cycle)
    return -MIXING * (own_terms + returned)


def solution(mesh):
    placed = (P("band", "grid", None),)
    return jax.shard_map(
        body, mesh=mesh, in_specs=placed, out_specs=P("band", "grid", None), check_vma=False
    )
```

profile of v0, /device:TPU:64, one launch (start us, length us, event | category | flops | bytes accessed | tf_op | source)
XLA Modules:
  0.0 938.7 jit_solution(7458069854812363606)
XLA Ops:
  12.0 11.1 %all-to-all-done.2 = f32[1,6,96,96]{3,0,1,2:T(1,128)S(1)} async-done(((f32[1,6,96,96]{3,0,1,2:T(1,128)}), f32[1,6,96,96]{3,0,1,2:T(1,128)S(1)}, u32[]{:S(2)}, u32[]{:S(2)}) %all-to-all-start.2) | async-done | bytes 221216 | tf_op jit(solution)/shard_map/all_to_all | solution.py:59
  30.9 10.1 %all-to-all-done.3 = f32[1,96,6,96]{3,0,2,1:T(1,128)S(1)} async-done(((f32[1,96,6,96]{3,0,2,1:T(1,128)}), f32[1,96,6,96]{3,0,2,1:T(1,128)S(1)}, u32[]{:S(2)}, u32[]{:S(2)}) %all-to-all-start.3) | async-done | bytes 221216 | tf_op jit(solution)/shard_map/all_to_all | solution.py:65
  42.6 874.7 %while.16 = (s32[]{:T(128)}, bf16[1,6,9216]{2,1,0:T(8,128)(2,1)S(1)}, f32[1,6,9216]{2,1,0:T(8,128)S(1)}, f32[1,6,9216]{2,1,0:T(8,128)S(1)}, s32[16]{0:T(128)S(1)...) while((s32[]{:T(128)}, ...), condition=%wide.region_1.2_spmd.clone.clone, body=%wide.region_0.1_spmd.clone.clone.sunk | while | flops 383975424 | bytes 12463057 | solution.py:105
  44.5 11.0 %collective-permute-done = bf16[1,6,9216]{2,1,0:T(8,128)(2,1)S(1)} collective-permute-done((bf16[1,6,9216]{2,1,0:T(8,128)(2,1)S(1)}, bf16[1,6,9216]{2,1,0:T(8,128)(2,1)S(1)}, u32[]{:S(2)}, u32[]{:S(2)}) %collective-permute-start) | collective-permute-done | bytes 110624 | tf_op jit(solution)/shard_map/while/body/eval_jaxpr/ppermute | solution.py:15
  63.5 10.1 %all-to-all-done = f32[1,6,96,96]{3,0,1,2:T(1,128)S(1)} async-done(((f32[1,6,96,96]{3,0,1,2:T(1,128)}), f32[1,6,96,96]{3,0,1,2:T(1,128)S(1)}, u32[]{:S(2)}, u32[]{:S(2)}) %all-to-all-start) | async-done | bytes 221216 | tf_op jit(solution)/shard_map/while/body/eval_jaxpr/all_to_all | solution.py:59
  117.8 10.1 %all-to-all-done = f32[1,6,96,96]{3,0,1,2:T(1,128)S(1)} async-done(((f32[1,6,96,96]{3,0,1,2:T(1,128)}), f32[1,6,96,96]{3,0,1,2:T(1,128)S(1)}, u32[]{:S(2)}, u32[]{:S(2)}) %all-to-all-start) | async-done | bytes 221216 | tf_op jit(solution)/shard_map/while/body/eval_jaxpr/all_to_all | solution.py:59
  172.1 10.1 %all-to-all-done = f32[1,6,96,96]{3,0,1,2:T(1,128)S(1)} async-done(((f32[1,6,96,96]{3,0,1,2:T(1,128)}), f32[1,6,96,96]{3,0,1,2:T(1,128)S(1)}, u32[]{:S(2)}, u32[]{:S(2)}) %all-to-all-start) | async-done | bytes 221216 | tf_op jit(solution)/shard_map/while/body/eval_jaxpr/all_to_all | solution.py:59
  225.5 10.1 %all-to-all-done = f32[1,6,96,96]{3,0,1,2:T(1,128)S(1)} async-done(((f32[1,6,96,96]{3,0,1,2:T(1,128)}), f32[1,6,96,96]{3,0,1,2:T(1,128)S(1)}, u32[]{:S(2)}, u32[]{:S(2)}) %all-to-all-start) | async-done | bytes 221216 | tf_op jit(solution)/shard_map/while/body/eval_jaxpr/all_to_all | solution.py:59
  260.2 10.4 %collective-permute-done = bf16[1,6,9216]{2,1,0:T(8,128)(2,1)S(1)} collective-permute-done((bf16[1,6,9216]{2,1,0:T(8,128)(2,1)S(1)}, bf16[1,6,9216]{2,1,0:T(8,128)(2,1)S(1)}, u32[]{:S(2)}, u32[]{:S(2)}) %collective-permute-start) | collective-permute-done | bytes 110624 | tf_op jit(solution)/shard_map/while/body/eval_jaxpr/ppermute | solution.py:15
  281.1 10.1 %all-to-all-done = f32[1,6,96,96]{3,0,1,2:T(1,128)S(1)} async-done(((f32[1,6,96,96]{3,0,1,2:T(1,128)}), f32[1,6,96,96]{3,0,1,2:T(1,128)S(1)}, u32[]{:S(2)}, u32[]{:S(2)}) %all-to-all-start) | async-done | bytes 221216 | tf_op jit(solution)/shard_map/while/body/eval_jaxpr/all_to_all | solution.py:59
  335.4 10.1 %all-to-all-done = f32[1,6,96,96]{3,0,1,2:T(1,128)S(1)} async-done(((f32[1,6,96,96]{3,0,1,2:T(1,128)}), f32[1,6,96,96]{3,0,1,2:T(1,128)S(1)}, u32[]{:S(2)}, u32[]{:S(2)}) %all-to-all-start) | async-done | bytes 221216 | tf_op jit(solution)/shard_map/while/body/eval_jaxpr/all_to_all | solution.py:59
  390.6 10.1 %all-to-all-done = f32[1,6,96,96]{3,0,1,2:T(1,128)S(1)} async-done(((f32[1,6,96,96]{3,0,1,2:T(1,128)}), f32[1,6,96,96]{3,0,1,2:T(1,128)S(1)}, u32[]{:S(2)}, u32[]{:S(2)}) %all-to-all-start) | async-done | bytes 221216 | tf_op jit(solution)/shard_map/while/body/eval_jaxpr/all_to_all | solution.py:59
  425.0 9.9 %collective-permute-done = bf16[1,6,9216]{2,1,0:T(8,128)(2,1)S(1)} collective-permute-done((bf16[1,6,9216]{2,1,0:T(8,128)(2,1)S(1)}, bf16[1,6,9216]{2,1,0:T(8,128)(2,1)S(1)}, u32[]{:S(2)}, u32[]{:S(2)}) %collective-permute-start) | collective-permute-done | bytes 110624 | tf_op jit(solution)/shard_map/while/body/eval_jaxpr/ppermute | solution.py:15
  445.2 10.1 %all-to-all-done = f32[1,6,96,96]{3,0,1,2:T(1,128)S(1)} async-done(((f32[1,6,96,96]{3,0,1,2:T(1,128)}), f32[1,6,96,96]{3,0,1,2:T(1,128)S(1)}, u32[]{:S(2)}, u32[]{:S(2)}) %all-to-all-start) | async-done | bytes 221216 | tf_op jit(solution)/shard_map/while/body/eval_jaxpr/all_to_all | solution.py:59
  500.2 10.1 %all-to-all-done = f32[1,6,96,96]{3,0,1,2:T(1,128)S(1)} async-done(((f32[1,6,96,96]{3,0,1,2:T(1,128)}), f32[1,6,96,96]{3,0,1,2:T(1,128)S(1)}, u32[]{:S(2)}, u32[]{:S(2)}) %all-to-all-start) | async-done | bytes 221216 | tf_op jit(solution)/shard_map/while/body/eval_jaxpr/all_to_all | solution.py:59
  555.5 10.1 %all-to-all-done = f32[1,6,96,96]{3,0,1,2:T(1,128)S(1)} async-done(((f32[1,6,96,96]{3,0,1,2:T(1,128)}), f32[1,6,96,96]{3,0,1,2:T(1,128)S(1)}, u32[]{:S(2)}, u32[]{:S(2)}) %all-to-all-start) | async-done | bytes 221216 | tf_op jit(solution)/shard_map/while/body/eval_jaxpr/all_to_all | solution.py:59
  610.5 10.1 %all-to-all-done = f32[1,6,96,96]{3,0,1,2:T(1,128)S(1)} async-done(((f32[1,6,96,96]{3,0,1,2:T(1,128)}), f32[1,6,96,96]{3,0,1,2:T(1,128)S(1)}, u32[]{:S(2)}, u32[]{:S(2)}) %all-to-all-start) | async-done | bytes 221216 | tf_op jit(solution)/shard_map/while/body/eval_jaxpr/all_to_all | solution.py:59
  666.7 10.1 %all-to-all-done = f32[1,6,96,96]{3,0,1,2:T(1,128)S(1)} async-done(((f32[1,6,96,96]{3,0,1,2:T(1,128)}), f32[1,6,96,96]{3,0,1,2:T(1,128)S(1)}, u32[]{:S(2)}, u32[]{:S(2)}) %all-to-all-start) | async-done | bytes 221216 | tf_op jit(solution)/shard_map/while/body/eval_jaxpr/all_to_all | solution.py:59
  721.3 10.1 %all-to-all-done = f32[1,6,96,96]{3,0,1,2:T(1,128)S(1)} async-done(((f32[1,6,96,96]{3,0,1,2:T(1,128)}), f32[1,6,96,96]{3,0,1,2:T(1,128)S(1)}, u32[]{:S(2)}, u32[]{:S(2)}) %all-to-all-start) | async-done | bytes 221216 | tf_op jit(solution)/shard_map/while/body/eval_jaxpr/all_to_all | solution.py:59
  776.3 10.1 %all-to-all-done = f32[1,6,96,96]{3,0,1,2:T(1,128)S(1)} async-done(((f32[1,6,96,96]{3,0,1,2:T(1,128)}), f32[1,6,96,96]{3,0,1,2:T(1,128)S(1)}, u32[]{:S(2)}, u32[]{:S(2)}) %all-to-all-start) | async-done | bytes 221216 | tf_op jit(solution)/shard_map/while/body/eval_jaxpr/all_to_all | solution.py:59
  810.9 9.5 %collective-permute-done = bf16[1,6,9216]{2,1,0:T(8,128)(2,1)S(1)} collective-permute-done((bf16[1,6,9216]{2,1,0:T(8,128)(2,1)S(1)}, bf16[1,6,9216]{2,1,0:T(8,128)(2,1)S(1)}, u32[]{:S(2)}, u32[]{:S(2)}) %collective-permute-start) | collective-permute-done | bytes 110624 | tf_op jit(solution)/shard_map/while/body/eval_jaxpr/ppermute | solution.py:15
  830.5 10.1 %all-to-all-done = f32[1,6,96,96]{3,0,1,2:T(1,128)S(1)} async-done(((f32[1,6,96,96]{3,0,1,2:T(1,128)}), f32[1,6,96,96]{3,0,1,2:T(1,128)S(1)}, u32[]{:S(2)}, u32[]{:S(2)}) %all-to-all-start) | async-done | bytes 221216 | tf_op jit(solution)/shard_map/while/body/eval_jaxpr/all_to_all | solution.py:59
  884.8 10.1 %all-to-all-done = f32[1,6,96,96]{3,0,1,2:T(1,128)S(1)} async-done(((f32[1,6,96,96]{3,0,1,2:T(1,128)}), f32[1,6,96,96]{3,0,1,2:T(1,128)S(1)}, u32[]{:S(2)}, u32[]{:S(2)}) %all-to-all-start) | async-done | bytes 221216 | tf_op jit(solution)/shard_map/while/body/eval_jaxpr/all_to_all | solution.py:59
  917.5 16.3 %collective-permute-start.2 = (f32[1,6,9216]{2,0,1:T(1,128)S(1)}, f32[1,6,9216]{2,0,1:T(1,128)S(1)}, u32[]{:S(2)}, u32[]{:S(2)}) collective-permute-start(f32[1,6,9216]{2,0,1:T(1,128)S(1)} %copy.48), channel_id=1, source_target_pairs={{0,256},{16,272},{32,288},{48,304},{64,320},{80,336},{96,352},{112... | collective-permute-start | bytes 663560 | tf_op jit(solution)/shard_map/ppermute | solution.py:15
  (474 shorter events, 685.6 us)
Async XLA Ops:
  3.3 19.8 %all-to-all-start.2 = ((f32[1,6,96,96]{3,0,1,2:T(1,128)}), f32[1,6,96,96]{3,0,1,2:T(1,128)S(1)}, u32[]{:S(2)}, u32[]{:S(2)}) async-start(f32[1,6,96,96]{3,0,1,2:T(1,128)} %copy.42), calls=%async_computation.2 | async-start | bytes 589824 | tf_op jit(solution)/shard_map/all_to_all | solution.py:59
  58.1 15.5 %all-to-all-start = ((f32[1,6,96,96]{3,0,1,2:T(1,128)}), f32[1,6,96,96]{3,0,1,2:T(1,128)S(1)}, u32[]{:S(2)}, u32[]{:S(2)}) async-start(f32[1,6,96,96]{3,0,1,2:T(1,128)} %copy.64), calls=%async_computation | async-start | bytes 589824 | tf_op jit(solution)/shard_map/while/body/eval_jaxpr/all_to_all | solution.py:59
  80.7 15.4 %collective-permute-start.1 = (f32[1,6,9216]{2,1,0:T(8,128)S(1)}, f32[1,6,9216]{2,1,0:T(8,128)S(1)}, u32[]{:S(2)}, u32[]{:S(2)}) collective-permute-start(f32[1,6,9216]{2,1,0:T(8,128)S(1)} %broadcast_select_fusion.2), channel_id=1, source_target_pairs={{0,16},{16,32},{32,48},{48,64},{64,80},{80,96},{96,112},{112,128},... | collective-permute-start | bytes 663560 | tf_op jit(solution)/shard_map/while/body/eval_jaxpr/ppermute | solution.py:15
  109.6 18.3 %all-to-all-start = ((f32[1,6,96,96]{3,0,1,2:T(1,128)}), f32[1,6,96,96]{3,0,1,2:T(1,128)S(1)}, u32[]{:S(2)}, u32[]{:S(2)}) async-start(f32[1,6,96,96]{3,0,1,2:T(1,128)} %copy.64), calls=%async_computation | async-start | bytes 589824 | tf_op jit(solution)/shard_map/while/body/eval_jaxpr/all_to_all | solution.py:59
  163.6 18.6 %all-to-all-start = ((f32[1,6,96,96]{3,0,1,2:T(1,128)}), f32[1,6,96,96]{3,0,1,2:T(1,128)S(1)}, u32[]{:S(2)}, u32[]{:S(2)}) async-start(f32[1,6,96,96]{3,0,1,2:T(1,128)} %copy.64), calls=%async_computation | async-start | bytes 589824 | tf_op jit(solution)/shard_map/while/body/eval_jaxpr/all_to_all | solution.py:59
  216.2 19.4 %all-to-all-start = ((f32[1,6,96,96]{3,0,1,2:T(1,128)}), f32[1,6,96,96]{3,0,1,2:T(1,128)S(1)}, u32[]{:S(2)}, u32[]{:S(2)}) async-start(f32[1,6,96,96]{3,0,1,2:T(1,128)} %copy.64), calls=%async_computation | async-start | bytes 589824 | tf_op jit(solution)/shard_map/while/body/eval_jaxpr/all_to_all | solution.py:59
  273.2 18.0 %all-to-all-start = ((f32[1,6,96,96]{3,0,1,2:T(1,128)}), f32[1,6,96,96]{3,0,1,2:T(1,128)S(1)}, u32[]{:S(2)}, u32[]{:S(2)}) async-start(f32[1,6,96,96]{3,0,1,2:T(1,128)} %copy.64), calls=%async_computation | async-start | bytes 589824 | tf_op jit(solution)/shard_map/while/body/eval_jaxpr/all_to_all | solution.py:59
  327.2 18.3 %all-to-all-start = ((f32[1,6,96,96]{3,0,1,2:T(1,128)}), f32[1,6,96,96]{3,0,1,2:T(1,128)S(1)}, u32[]{:S(2)}, u32[]{:S(2)}) async-start(f32[1,6,96,96]{3,0,1,2:T(1,128)} %copy.64), calls=%async_computation | async-start | bytes 589824 | tf_op jit(solution)/shard_map/while/body/eval_jaxpr/all_to_all | solution.py:59
  381.2 19.4 %all-to-all-start = ((f32[1,6,96,96]{3,0,1,2:T(1,128)}), f32[1,6,96,96]{3,0,1,2:T(1,128)S(1)}, u32[]{:S(2)}, u32[]{:S(2)}) async-start(f32[1,6,96,96]{3,0,1,2:T(1,128)} %copy.64), calls=%async_computation | async-start | bytes 589824 | tf_op jit(solution)/shard_map/while/body/eval_jaxpr/all_to_all | solution.py:59
  437.5 17.8 %all-to-all-start = ((f32[1,6,96,96]{3,0,1,2:T(1,128)}), f32[1,6,96,96]{3,0,1,2:T(1,128)S(1)}, u32[]{:S(2)}, u32[]{:S(2)}) async-start(f32[1,6,96,96]{3,0,1,2:T(1,128)} %copy.64), calls=%async_computation | async-start | bytes 589824 | tf_op jit(solution)/shard_map/while/body/eval_jaxpr/all_to_all | solution.py:59
  491.1 19.1 %all-to-all-start = ((f32[1,6,96,96]{3,0,1,2:T(1,128)}), f32[1,6,96,96]{3,0,1,2:T(1,128)S(1)}, u32[]{:S(2)}, u32[]{:S(2)}) async-start(f32[1,6,96,96]{3,0,1,2:T(1,128)} %copy.64), calls=%async_computation | async-start | bytes 589824 | tf_op jit(solution)/shard_map/while/body/eval_jaxpr/all_to_all | solution.py:59
  517.3 16.4 %collective-permute-start.1 = (f32[1,6,9216]{2,1,0:T(8,128)S(1)}, f32[1,6,9216]{2,1,0:T(8,128)S(1)}, u32[]{:S(2)}, u32[]{:S(2)}) collective-permute-start(f32[1,6,9216]{2,1,0:T(8,128)S(1)} %broadcast_select_fusion.2), channel_id=1, source_target_pairs={{0,16},{16,32},{32,48},{48,64},{64,80},{80,96},{96,112},{112,128},... | collective-permute-start | bytes 663560 | tf_op jit(solution)/shard_map/while/body/eval_jaxpr/ppermute | solution.py:15
  547.2 18.4 %all-to-all-start = ((f32[1,6,96,96]{3,0,1,2:T(1,128)}), f32[1,6,96,96]{3,0,1,2:T(1,128)S(1)}, u32[]{:S(2)}, u32[]{:S(2)}) async-start(f32[1,6,96,96]{3,0,1,2:T(1,128)} %copy.64), calls=%async_computation | async-start | bytes 589824 | tf_op jit(solution)/shard_map/while/body/eval_jaxpr/all_to_all | solution.py:59
  572.7 16.0 %collective-permute-start.1 = (f32[1,6,9216]{2,1,0:T(8,128)S(1)}, f32[1,6,9216]{2,1,0:T(8,128)S(1)}, u32[]{:S(2)}, u32[]{:S(2)}) collective-permute-start(f32[1,6,9216]{2,1,0:T(8,128)S(1)} %broadcast_select_fusion.2), channel_id=1, source_target_pairs={{0,16},{16,32},{32,48},{48,64},{64,80},{80,96},{96,112},{112,128},... | collective-permute-start | bytes 663560 | tf_op jit(solution)/shard_map/while/body/eval_jaxpr/ppermute | solution.py:15
  602.2 18.4 %all-to-all-start = ((f32[1,6,96,96]{3,0,1,2:T(1,128)}), f32[1,6,96,96]{3,0,1,2:T(1,128)S(1)}, u32[]{:S(2)}, u32[]{:S(2)}) async-start(f32[1,6,96,96]{3,0,1,2:T(1,128)} %copy.64), calls=%async_computation | async-start | bytes 589824 | tf_op jit(solution)/shard_map/while/body/eval_jaxpr/all_to_all | solution.py:59
  627.8 15.8 %collective-permute-start.1 = (f32[1,6,9216]{2,1,0:T(8,128)S(1)}, f32[1,6,9216]{2,1,0:T(8,128)S(1)}, u32[]{:S(2)}, u32[]{:S(2)}) collective-permute-start(f32[1,6,9216]{2,1,0:T(8,128)S(1)} %broadcast_select_fusion.2), channel_id=1, source_target_pairs={{0,16},{16,32},{32,48},{48,64},{64,80},{80,96},{96,112},{112,128},... | collective-permute-start | bytes 663560 | tf_op jit(solution)/shard_map/while/body/eval_jaxpr/ppermute | solution.py:15
  657.5 19.4 %all-to-all-start = ((f32[1,6,96,96]{3,0,1,2:T(1,128)}), f32[1,6,96,96]{3,0,1,2:T(1,128)S(1)}, u32[]{:S(2)}, u32[]{:S(2)}) async-start(f32[1,6,96,96]{3,0,1,2:T(1,128)} %copy.64), calls=%async_computation | async-start | bytes 589824 | tf_op jit(solution)/shard_map/while/body/eval_jaxpr/all_to_all | solution.py:59
  683.9 16.3 %collective-permute-start.1 = (f32[1,6,9216]{2,1,0:T(8,128)S(1)}, f32[1,6,9216]{2,1,0:T(8,128)S(1)}, u32[]{:S(2)}, u32[]{:S(2)}) collective-permute-start(f32[1,6,9216]{2,1,0:T(8,128)S(1)} %broadcast_select_fusion.2), channel_id=1, source_target_pairs={{0,16},{16,32},{32,48},{48,64},{64,80},{80,96},{96,112},{112,128},... | collective-permute-start | bytes 663560 | tf_op jit(solution)/shard_map/while/body/eval_jaxpr/ppermute | solution.py:15
  713.8 17.6 %all-to-all-start = ((f32[1,6,96,96]{3,0,1,2:T(1,128)}), f32[1,6,96,96]{3,0,1,2:T(1,128)S(1)}, u32[]{:S(2)}, u32[]{:S(2)}) async-start(f32[1,6,96,96]{3,0,1,2:T(1,128)} %copy.64), calls=%async_computation | async-start | bytes 589824 | tf_op jit(solution)/shard_map/while/body/eval_jaxpr/all_to_all | solution.py:59
  738.5 15.8 %collective-permute-start.1 = (f32[1,6,9216]{2,1,0:T(8,128)S(1)}, f32[1,6,9216]{2,1,0:T(8,128)S(1)}, u32[]{:S(2)}, u32[]{:S(2)}) collective-permute-start(f32[1,6,9216]{2,1,0:T(8,128)S(1)} %broadcast_select_fusion.2), channel_id=1, source_target_pairs={{0,16},{16,32},{32,48},{48,64},{64,80},{80,96},{96,112},{112,128},... | collective-permute-start | bytes 663560 | tf_op jit(solution)/shard_map/while/body/eval_jaxpr/ppermute | solution.py:15
  767.9 18.4 %all-to-all-start = ((f32[1,6,96,96]{3,0,1,2:T(1,128)}), f32[1,6,96,96]{3,0,1,2:T(1,128)S(1)}, u32[]{:S(2)}, u32[]{:S(2)}) async-start(f32[1,6,96,96]{3,0,1,2:T(1,128)} %copy.64), calls=%async_computation | async-start | bytes 589824 | tf_op jit(solution)/shard_map/while/body/eval_jaxpr/all_to_all | solution.py:59
  823.0 17.6 %all-to-all-start = ((f32[1,6,96,96]{3,0,1,2:T(1,128)}), f32[1,6,96,96]{3,0,1,2:T(1,128)S(1)}, u32[]{:S(2)}, u32[]{:S(2)}) async-start(f32[1,6,96,96]{3,0,1,2:T(1,128)} %copy.64), calls=%async_computation | async-start | bytes 589824 | tf_op jit(solution)/shard_map/while/body/eval_jaxpr/all_to_all | solution.py:59
  876.9 17.9 %all-to-all-start = ((f32[1,6,96,96]{3,0,1,2:T(1,128)}), f32[1,6,96,96]{3,0,1,2:T(1,128)S(1)}, u32[]{:S(2)}, u32[]{:S(2)}) async-start(f32[1,6,96,96]{3,0,1,2:T(1,128)} %copy.64), calls=%async_computation | async-start | bytes 589824 | tf_op jit(solution)/shard_map/while/body/eval_jaxpr/all_to_all | solution.py:59
  917.5 20.2 %collective-permute-start.2 = (f32[1,6,9216]{2,0,1:T(1,128)S(1)}, f32[1,6,9216]{2,0,1:T(1,128)S(1)}, u32[]{:S(2)}, u32[]{:S(2)}) collective-permute-start(f32[1,6,9216]{2,0,1:T(1,128)S(1)} %copy.48), channel_id=1, source_target_pairs={{0,256},{16,272},{32,288},{48,304},{64,320},{80,336},{96,352},{112... | collective-permute-start | bytes 663560 | tf_op jit(solution)/shard_map/ppermute | solution.py:15
  (44 other events, 580.6 us)
where the time goes:
time: 943 us; the launch traced here: 939 us
  waiting for transfers between devices  494 us (52%)
  starting transfers between devices  293 us (31%)
  matrix products  75.3 us (8%)
  local copies, waits for them, and re-layouts  57 us (6%)
  loops' own time  13.5 us (1%)
    ppermute x33, waiting for transfers between devices, shifted(): lax.ppermute(array, axis, [(i, (i + by) % peers) for i in range(peers)])  203 us
    all_to_all x17, waiting for transfers between devices, potentials(): lax.all_to_all(spectrum, 'grid', split_axis=2, concat_axis=1, tiled=True)  172 us
    all_to_all x17, starting transfers between devices, potentials(): lax.all_to_all(spectrum, 'grid', split_axis=2, concat_axis=1, tiled=True)  139 us
    all_to_all x17, waiting for transfers between devices, potentials(): lax.all_to_all(moved, 'grid', split_axis=1, concat_axis=2, tiled=True)  118 us
    ppermute x33, starting transfers between devices, shifted(): lax.ppermute(array, axis, [(i, (i + by) % peers) for i in range(peers)])  77.8 us
    all_to_all x17, starting transfers between devices, potentials(): lax.all_to_all(moved, 'grid', split_axis=1, concat_axis=2, tiled=True)  75.4 us
    dot_general x34, matrix products, plane_transform(): jnp.einsum('pxyz,kz->pxyk', field_cells, cas_table, precision=lax.Precisi...  31.5 us
    dot_general x34, matrix products, plane_transform(): jnp.einsum('pxyz,ky->pxkz', section, cas_table, precision=lax.Precision.H...  20.5 us
  transfers between devices with their start and end apart: 67, of which 67 were waited for; matrix products, arithmetic and copies ran while one was open for 5% of the time, Pallas kernels for 0%

commit v1 on v0

v1 whole, which is shorter than its diff:
```python
import math

import jax
import jax.numpy as jnp
import numpy as np
from jax import lax
from jax.experimental import pallas as pl
from jax.experimental.pallas import tpu as pltpu
from jax.sharding import Mesh
from jax.sharding import PartitionSpec as P

MIXING = 0.25
SPACING = 0.31
SCREENING = 0.106

NG = 96
LANES = 128
SLAB = 6
BF16 = jnp.bfloat16
F32 = jnp.float32
AXES = ("zh", "x", "core", "y", "zl")
SIZES = (4, 4, 2, 8, 2)
BAND = ("zh", "x", "core")
GRID = ("y", "zl")
X_BLOCK = 8
KY_BLOCK = 8


def cas_halves():
    index = np.arange(NG)
    phases = (index[:, None] * index[None, :] % NG) * (2.0 * math.pi / NG)
    table = np.cos(phases) + np.sin(phases)
    high = table.astype(BF16)
    low = (table - high.astype(np.float64)).astype(BF16)
    return high, low


def right_table():
    high, low = cas_halves()
    table = np.zeros((2 * LANES, 2 * LANES), BF16)
    for row in (0, LANES):
        table[row : row + NG, 0:NG] = high
        table[row : row + NG, LANES : LANES + NG] = low
    return table


def left_table():
    high, low = cas_halves()
    return np.concatenate(
        [np.concatenate([high, high], axis=1), np.concatenate([low, low], axis=1)], axis=0
    )


def kernel_table():
    index = jnp.arange(NG, dtype=jnp.int32)
    signed = jnp.where(index * 2 < NG, index, index - NG).astype(F32)
    wave = signed * (2.0 * math.pi / (NG * SPACING))
    wave_z = jnp.pad(wave, (0, LANES - NG))
    square = (
        (wave * wave)[:, None, None] + (wave * wave)[None, :, None] + (wave_z * wave_z)[None, None, :]
    )
    safe = jnp.where(square > 0, square, 1.0)
    values = 4.0 * math.pi * (1.0 - jnp.exp(-safe / (4.0 * SCREENING * SCREENING))) / safe
    return jnp.where(square > 0, values, 0.0) * (-MIXING / float(NG) ** 3)


def halves(values):
    high = values.astype(BF16)
    low = (values - high.astype(F32)).astype(BF16)
    return high, low


def left_transform(table, columns):
    high, low = halves(columns)
    both = jnp.dot(table, jnp.concatenate([high, low], axis=0), preferred_element_type=F32)
    return both[:NG] + both[NG:]


def right_transform(rows, table):
    high, low = halves(rows)
    both = jnp.dot(jnp.concatenate([high, low], axis=1), table, preferred_element_type=F32)
    return both[:, :LANES] + both[:, LANES:]


def padded(plane):
    return jnp.concatenate([plane, jnp.zeros((plane.shape[0], LANES - NG), plane.dtype)], axis=1)


def forward_kernel(own_ref, first_ref, second_ref, right_ref, left_ref, out_ref):
    for at in range(X_BLOCK):
        own = own_ref[at].astype(F32)
        first = own * first_ref[at].astype(F32)
        second = own * second_ref[at].astype(F32)
        rows = jnp.concatenate([padded(first), padded(second)], axis=0)
        rows = right_transform(rows, right_ref[...])
        columns = jnp.concatenate([rows[:NG], rows[NG:]], axis=1)
        out_ref[at] = left_transform(left_ref[...], columns)


def middle_kernel(field_ref, kernel_ref, left_ref, out_ref):
    for at in range(KY_BLOCK):
        columns = left_transform(left_ref[...], field_ref[:, at, :])
        weight = kernel_ref[at]
        columns = columns * jnp.concatenate([weight, weight], axis=1)
        out_ref[:, at, :] = left_transform(left_ref[...], columns)


def backward_kernel(field_ref, first_ref, second_ref, right_ref, left_ref, out_ref):
    for at in range(X_BLOCK):
        columns = left_transform(left_ref[...], field_ref[at])
        rows = jnp.concatenate([columns[:, :LANES], columns[:, LANES:]], axis=0)
        rows = right_transform(rows, right_ref[...])
        first = rows[:NG, :NG] * first_ref[at].astype(F32)
        second = rows[NG:, :NG] * second_ref[at].astype(F32)
        out_ref[at] = first + second


PARAMS = pltpu.CompilerParams(vmem_limit_bytes=48 * 1024 * 1024)
CUBE = (NG, NG, NG)
WIDE = (NG, NG, 2 * LANES)
RIGHT_SPEC = pl.BlockSpec((2 * LANES, 2 * LANES), lambda i: (0, 0))
LEFT_SPEC = pl.BlockSpec((2 * NG, 2 * NG), lambda i: (0, 0))


def forward(own, first, second, right, left):
    orbital = pl.BlockSpec((X_BLOCK, NG, NG), lambda i: (i, 0, 0))
    return pl.pallas_call(
        forward_kernel,
        grid=(NG // X_BLOCK,),
        in_specs=[orbital, orbital, orbital, RIGHT_SPEC, LEFT_SPEC],
        out_specs=pl.BlockSpec((X_BLOCK, NG, 2 * LANES), lambda i: (i, 0, 0)),
        out_shape=jax.ShapeDtypeStruct(WIDE, F32),
        compiler_params=PARAMS,
    )(own, first, second, right, left)


def middle(field, kernel, left):
    block = pl.BlockSpec((NG, KY_BLOCK, 2 * LANES), lambda i: (0, i, 0))
    return pl.pallas_call(
        middle_kernel,
        grid=(NG // KY_BLOCK,),
        in_specs=[block, pl.BlockSpec((KY_BLOCK, NG, LANES), lambda i: (i, 0, 0)), LEFT_SPEC],
        out_specs=block,
        out_shape=jax.ShapeDtypeStruct(WIDE, F32),
        compiler_params=PARAMS,
    )(field, kernel, left)


def backward(field, first, second, right, left):
    orbital = pl.BlockSpec((X_BLOCK, NG, NG), lambda i: (i, 0, 0))
    return pl.pallas_call(
        backward_kernel,
        grid=(NG // X_BLOCK,),
        in_specs=[
            pl.BlockSpec((X_BLOCK, NG, 2 * LANES), lambda i: (i, 0, 0)),
            orbital,
            orbital,
            RIGHT_SPEC,
            LEFT_SPEC,
        ],
        out_specs=orbital,
        out_shape=jax.ShapeDtypeStruct(CUBE, F32),
        compiler_params=PARAMS,
    )(field, first, second, right, left)


def exchanged_slabs(slab):
    pairs = []
    for pair in range(16):
        for core in range(2):
            for place in range(16):
                pairs.append(((pair * 2 + core) * 16 + place, (place * 2 + core) * 16 + pair))
    return lax.ppermute(slab, AXES, pairs)


def body(orbitals):
    slab = orbitals.reshape(SLAB * NG * NG // LANES, LANES)
    right = jnp.asarray(right_table())
    left = jnp.asarray(left_table())
    kernel = kernel_table()
    first = lax.all_gather(exchanged_slabs(slab), ("zh", "x"), axis=0, tiled=True).reshape(CUBE)
    second = lax.ppermute(first, "core", [(0, 1), (1, 0)])
    own = lax.all_gather(slab, GRID, axis=0, tiled=True).reshape(CUBE)
    field = forward(own, first, second, right, left)
    field = middle(field, kernel, left)
    terms = backward(field, first, second, right, left).reshape(NG * NG * NG // LANES, LANES)
    total = lax.psum_scatter(terms, GRID, scatter_dimension=0, tiled=True)
    return total.reshape(orbitals.shape)


def solution(mesh):
    fine = Mesh(mesh.devices.reshape(SIZES), AXES)
    placed = P(BAND, GRID, None)
    return jax.shard_map(
        body, mesh=fine, in_specs=(placed,), out_specs=placed, check_vma=False
    )
```

time: 943 us -> 350 us (0.37)
  the two profiles are of different devices: /device:TPU:64 before, /device:TPU:1 now
where the time goes in v1:
time: 350 us; the launch traced here: 348 us
  waiting for transfers between devices  243 us (69%)
  Pallas kernels  65.5 us (19%)
  local copies, waits for them, and re-layouts  17.6 us (5%)
  between operations  13.2 us (4%)
  starting transfers between devices  4.82 us (1%)
  other arithmetic  3.82 us (1%)
    reduce_scatter x1, waiting for transfers between devices, body(): total = lax.psum_scatter(terms, GRID, scatter_dimension=0, tiled=True)  96.7 us
    all_gather x1, waiting for transfers between devices, body(): lax.all_gather(exchanged_slabs(slab), ('zh', 'x'), axis=0, tiled=True)  91.1 us
    all_gather x1, waiting for transfers between devices, body(): own = lax.all_gather(slab, GRID, axis=0, tiled=True).reshape(CUBE)  54.4 us
    pallas_call x1, Pallas kernels, middle(): pl.pallas_call(middle_kernel, grid=(NG // KY_BLOCK,), in_specs=[block, pl...  37.3 us
    pallas_call x1, Pallas kernels, forward(): pl.pallas_call(forward_kernel, grid=(NG // X_BLOCK,), in_specs=[orbital,...  14.3 us
    pallas_call x1, Pallas kernels, backward(): pl.pallas_call(backward_kernel, grid=(NG // X_BLOCK,), in_specs=[pl.Block...  13.8 us
  transfers between devices with their start and end apart: 5, of which 3 were waited for; matrix products, arithmetic and copies ran while one was open for 3% of the time, Pallas kernels for 0%

profile of v1, /device:TPU:1, one launch (start us, length us, event | category | flops | bytes accessed | tf_op | source)
XLA Modules:
  0.0 347.8 jit_solution(9831701691777934938)
XLA Ops:
  6.5 1.1 reshape.72
  7.6 0.0 copy-start.4
  7.6 0.7 collective-permute-start
  8.3 0.6 copy-done.5
  9.0 0.0 all-gather.5.cloned.1.call-update
  9.0 0.0 all-gather.3.cloned.1.call-start
  9.0 0.7 all-gather.3.cloned.1.call-update
  9.7 0.0 reduce-scatter.2.cloned.1.call-start
  9.8 91.1 %all-gather.5.cloned.1.call-done = bf16[6912,128]{1,0:T(8,128)(2,1)} async-done(((bf16[432,128]{1,0:T(8,128)(2,1)}), bf16[6912,128]{1,0:T(8,128)(2,1)}) %all-gather.5.cloned.1.call-update) | async-done | bytes 1769488 | tf_op jit(solution)/shard_map/all_gather | solution.py:181
  100.9 3.4 reshape.74.first_ref
  104.3 0.0 copy-start.2
  104.3 0.0 copy-start.3
  104.3 4.1 %collective-permute-start.1 = (bf16[96,96,96]{2,1,0:T(8,128)(2,1)S(1)}, bf16[96,96,96]{2,1,0:T(8,128)(2,1)}, u32[]{:S(2)}, u32[]{:S(2)}) collective-permute-start(bf16[96,96,96]{2,1,0:T(8,128)(2,1)S(1)} %reshape.74.first_ref), channel_id=1, source_target_pairs={{0,16},{16,0},{1,17},{17,1},{2,18},{18,2},{3,19},{19,3},{4,20},{20... | collective-permute-start | bytes 5308424 | tf_op jit(solution)/shard_map/ppermute | solution.py:182
  108.4 0.1 broadcast_add_fusion
  108.5 3.7 %fusion.3.kernel_ref = f32[96,96,128]{2,1,0:T(8,128)} fusion(f32[128]{0:T(128)S(1)} %pad_multiply_fusion, f32[96,96]{1,0:T(8,128)S(1)} %broadcast_add_fusion), kind=kLoop, calls=%fused_computation.5 | loop fusion | flops 11796480 | bytes 4755968 | tf_op jit(solution)/shard_map/mul | solution.py:64
  112.2 54.4 %all-gather.3.cloned.1.call-done = bf16[6912,128]{1,0:T(8,128)(2,1)} async-done(((bf16[432,128]{1,0:T(8,128)(2,1)}), bf16[6912,128]{1,0:T(8,128)(2,1)}) %all-gather.3.cloned.1.call-update) | async-done | bytes 1769488 | tf_op jit(solution)/shard_map/all_gather | solution.py:183
  166.6 4.6 %reshape.73.own_ref = bf16[96,96,96]{2,1,0:T(8,128)(2,1)} reshape(bf16[6912,128]{1,0:T(8,128)(2,1)} %all-gather.3.cloned.1.call-done) | data formatting | bytes 3538944 | tf_op jit(solution)/shard_map/reshape | solution.py:183
  171.2 1.8 copy-done.1
  173.0 14.3 %shard_map.37.field_ref = f32[96,96,256]{2,1,0:T(8,128)} custom-call(bf16[96,96,96]{2,1,0:T(8,128)(2,1)S(1)} %copy-done.1, bf16[96,96,96]{2,1,0:T(8,128)(2,1)S(1)} %reshape.74.first_ref, bf16[96,96,96]{2,1,0:T(8,128)(2,1)} %collective-permute-done.1.second_ref, bf16[256,256]{1,0:T(8,128)(2,1)S(1)} %copy-done.3, bf16[192,192]{1,0:T(8,128)(2,1)S(1)} %copy-done.2), custom_call_target="tpu_custom_call" | custom-call | tf_op jit(solution)/shard_map/pallas_call | solution.py:127
  187.3 37.3 %shard_map.38.field_ref = f32[96,96,256]{2,1,0:T(8,128)} custom-call(f32[96,96,256]{2,1,0:T(8,128)} %shard_map.37.field_ref, f32[96,96,128]{2,1,0:T(8,128)S(1)} %copy-done, bf16[192,192]{1,0:T(8,128)(2,1)S(1)} %copy-done.2), custom_call_target="tpu_custom_call" | custom-call | tf_op jit(solution)/shard_map/pallas_call | solution.py:139
  224.6 13.8 %shard_map.39 = f32[96,96,96]{2,1,0:T(8,128)} custom-call(f32[96,96,256]{2,1,0:T(8,128)} %shard_map.38.field_ref, bf16[96,96,96]{2,1,0:T(8,128)(2,1)S(1)} %reshape.74.first_ref, bf16[96,96,96]{2,1,0:T(8,128)(2,1)} %collective-permute-done.1.second_ref, bf16[256,256]{1,0:T(8,128)(2,1)S(1)} %copy-done.3, bf16[192,192]{1,0:T(8,128)(2,1)S(1)} %copy-done.2), custom_call_target="tpu_custom_call" | custom-call | tf_op jit(solution)/shard_map/pallas_call | solution.py:151
  238.5 6.1 %reshape.75 = f32[6912,128]{1,0:T(8,128)} reshape(f32[96,96,96]{2,1,0:T(8,128)} %shard_map.39) | data formatting | bytes 7077888 | tf_op jit(solution)/shard_map/reshape | solution.py:186
  244.6 0.0 reduce-scatter.2.cloned.1.call-update
  244.6 96.7 %reduce-scatter.2.cloned.1.call-done = f32[432,128]{1,0:T(8,128)} async-done(((f32[6912,128]{1,0:T(8,128)}), f32[432,128]{1,0:T(8,128)}) %reduce-scatter.2.cloned.1.call-update) | async-done | bytes 221200 | tf_op jit(solution)/shard_map/reduce_scatter | solution.py:187
  (13 shorter events, 0.0 us)
Async XLA Ops:
  6.5 94.3 %all-gather.5.cloned.1.call-start = ((), (), s32[]{:S(2)}) async-start(), calls=%async_computation.2 | async-start | bytes 1880064 | tf_op jit(solution)/shard_map/all_gather | solution.py:181
  7.6 1.4 copy-start.4
  7.6 0.7 collective-permute-start
  8.3 0.6 copy-start.5
  9.0 157.6 %all-gather.3.cloned.1.call-start = ((), (), s32[]{:S(2)}) async-start(), calls=%async_computation.1 | async-start | bytes 1880064 | tf_op jit(solution)/shard_map/all_gather | solution.py:183
  9.7 331.6 %reduce-scatter.2.cloned.1.call-start = ((), (), s32[]{:S(2)}) async-start(), calls=%async_computation.3 | async-start | bytes 3760128 | tf_op jit(solution)/shard_map/reduce_scatter | solution.py:187
  104.3 66.9 %copy-start.2 = (bf16[192,192]{1,0:T(8,128)(2,1)S(1)}, bf16[192,192]{1,0:T(8,128)(2,1)}, u32[]{:S(2)}) copy-start(bf16[192,192]{1,0:T(8,128)(2,1)} %constant.28.clone.left_ref) | copy-start | bytes 221188
  104.3 66.9 %copy-start.3 = (bf16[256,256]{1,0:T(8,128)(2,1)S(1)}, bf16[256,256]{1,0:T(8,128)(2,1)}, u32[]{:S(2)}) copy-start(bf16[256,256]{1,0:T(8,128)(2,1)} %constant.27.clone.right_ref) | copy-start | bytes 393220
  104.3 66.8 %collective-permute-start.1 = (bf16[96,96,96]{2,1,0:T(8,128)(2,1)S(1)}, bf16[96,96,96]{2,1,0:T(8,128)(2,1)}, u32[]{:S(2)}, u32[]{:S(2)}) collective-permute-start(bf16[96,96,96]{2,1,0:T(8,128)(2,1)S(1)} %reshape.74.first_ref), channel_id=1, source_target_pairs={{0,16},{16,0},{1,17},{17,1},{2,18},{18,2},{3,19},{19,3},{4,20},{20... | collective-permute-start | bytes 5308424 | tf_op jit(solution)/shard_map/ppermute | solution.py:182
  171.1 16.2 %copy-start = (f32[96,96,128]{2,1,0:T(8,128)S(1)}, f32[96,96,128]{2,1,0:T(8,128)}, u32[]{:S(2)}) copy-start(f32[96,96,128]{2,1,0:T(8,128)} %fusion.3.kernel_ref) | copy-start | bytes 14155780
  171.2 1.8 copy-start.1
Sparse Core Ops, SparseCore 0:
  10.4 90.4 all-gather.4
  102.9 63.6 all-gather.2
  244.7 96.5 reduce-scatter.1

commit v2 on v1

--- a/solution.py
+++ b/solution.py
@@ -82,60 +82,104 @@
     return both[:, :LANES] + both[:, LANES:]
 
 
-def padded(plane):
-    return jnp.concatenate([plane, jnp.zeros((plane.shape[0], LANES - NG), plane.dtype)], axis=1)
+PACKED = NG * NG // LANES
+TAIL = NG - PACKED
+REST = LANES - NG
+
+
+def pack(planes):
+    tail = planes[:, PACKED:]
+    thirds = [tail[:, :, REST * at : REST * (at + 1)] for at in range(NG // REST)]
+    return jnp.concatenate([planes[:, :PACKED], jnp.concatenate(thirds, axis=1)], axis=2)
+
+
+def unpack(packed):
+    side = packed[:, :, NG:]
+    thirds = [side[:, TAIL * at : TAIL * (at + 1)] for at in range(NG // REST)]
+    return jnp.concatenate([packed[:, :, :NG], jnp.concatenate(thirds, axis=2)], axis=1)
+
+
+def lane_mask(rows, low, high):
+    lane = lax.broadcasted_iota(jnp.int32, (rows, LANES), 1)
+    return (lane >= low) & (lane < high)
+
+
+def unpack_plane(packed):
+    top = jnp.where(lane_mask(PACKED, 0, NG), packed, 0.0)
+    tail = jnp.zeros((TAIL, LANES), packed.dtype)
+    for at in range(NG // REST):
+        rolled = pltpu.roll(packed[TAIL * at : TAIL * (at + 1)], REST * (at + 1), 1)
+        tail = jnp.where(lane_mask(TAIL, REST * at, REST * (at + 1)), rolled, tail)
+    return jnp.concatenate([top, tail], axis=0)
+
+
+def pack_plane(plane):
+    tail = plane[PACKED:]
+    sides = [pltpu.roll(tail, LANES - REST * (at + 1), 1) for at in range(NG // REST)]
+    return jnp.where(lane_mask(PACKED, 0, NG), plane[:PACKED], jnp.concatenate(sides, axis=0))
 
 
 def forward_kernel(own_ref, first_ref, second_ref, right_ref, left_ref, out_ref):
     for at in range(X_BLOCK):
         own = own_ref[at].astype(F32)
-        first = own * first_ref[at].astype(F32)
-        second = own * second_ref[at].astype(F32)
-        rows = jnp.concatenate([padded(first), padded(second)], axis=0)
-        rows = right_transform(rows, right_ref[...])
+        first = unpack_plane(own * first_ref[at].astype(F32))
+        second = unpack_plane(own * second_ref[at].astype(F32))
+        rows = right_transform(jnp.concatenate([first, second], axis=0), right_ref[...])
         columns = jnp.concatenate([rows[:NG], rows[NG:]], axis=1)
-        out_ref[at] = left_transform(left_ref[...], columns)
+        columns = left_transform(left_ref[...], columns)
+        out_ref[0, at] = columns[:, :LANES]
+        out_ref[1, at] = columns[:, LANES:]
 
 
 def middle_kernel(field_ref, kernel_ref, left_ref, out_ref):
+    field = field_ref.reshape(2 * NG * KY_BLOCK, LANES)
+    out = out_ref.reshape(2 * NG * KY_BLOCK, LANES)
     for at in range(KY_BLOCK):
-        columns = left_transform(left_ref[...], field_ref[:, at, :])
+        first = pl.ds(at, NG, stride=KY_BLOCK)
+        second = pl.ds(NG * KY_BLOCK + at, NG, stride=KY_BLOCK)
+        columns = jnp.concatenate([field[first, :], field[second, :]], axis=1)
+        columns = left_transform(left_ref[...], columns)
         weight = kernel_ref[at]
         columns = columns * jnp.concatenate([weight, weight], axis=1)
-        out_ref[:, at, :] = left_transform(left_ref[...], columns)
+        columns = left_transform(left_ref[...], columns)
+        out[first, :] = columns[:, :LANES]
+        out[second, :] = columns[:, LANES:]
 
 
 def backward_kernel(field_ref, first_ref, second_ref, right_ref, left_ref, out_ref):
     for at in range(X_BLOCK):
-        columns = left_transform(left_ref[...], field_ref[at])
+        columns = jnp.concatenate([field_ref[0, at], field_ref[1, at]], axis=1)
+        columns = left_transform(left_ref[...], columns)
         rows = jnp.concatenate([columns[:, :LANES], columns[:, LANES:]], axis=0)
         rows = right_transform(rows, right_ref[...])
-        first = rows[:NG, :NG] * first_ref[at].astype(F32)
-        second = rows[NG:, :NG] * second_ref[at].astype(F32)
+        first = pack_plane(rows[:NG]) * first_ref[at].astype(F32)
+        second = pack_plane(rows[NG:]) * second_ref[at].astype(F32)
         out_ref[at] = first + second
 
 
 PARAMS = pltpu.CompilerParams(vmem_limit_bytes=48 * 1024 * 1024)
-CUBE = (NG, NG, NG)
-WIDE = (NG, NG, 2 * LANES)
+CUBE = (NG, PACKED, LANES)
+WIDE = (2, NG, NG, LANES)
 RIGHT_SPEC = pl.BlockSpec((2 * LANES, 2 * LANES), lambda i: (0, 0))
 LEFT_SPEC = pl.BlockSpec((2 * NG, 2 * NG), lambda i: (0, 0))
+ORBITAL_SPEC = pl.BlockSpec((X_BLOCK, PACKED, LANES), lambda i: (i, 0, 0))
+FIELD_SPEC = pl.BlockSpec((2, X_BLOCK, NG, LANES), lambda i: (0, i, 0, 0))
 
 
 def forward(own, first, second, right, left):
-    orbital = pl.BlockSpec((X_BLOCK, NG, NG), lambda i: (i, 0, 0))
     return pl.pallas_call(
         forward_kernel,
         grid=(NG // X_BLOCK,),
-        in_specs=[orbital, orbital, orbital, RIGHT_SPEC, LEFT_SPEC],
-        out_specs=pl.BlockSpec((X_BLOCK, NG, 2 * LANES), lambda i: (i, 0, 0)),
+        in_specs=[ORBITAL_SPEC, ORBITAL_SPEC, ORBITAL_SPEC, RIGHT_SPEC, LEFT_SPEC],
+        out_specs=FIELD_SPEC,
         out_shape=jax.ShapeDtypeStruct(WIDE, F32),
         compiler_params=PARAMS,
+        name="forward",
     )(own, first, second, right, left)
 
 
 def middle(field, kernel, left):
-    block = pl.BlockSpec((NG, KY_BLOCK, 2 * LANES), lambda i: (0, i, 0))
+    block = pl.BlockSpec((2, NG, KY_BLOCK, LANES), lambda i: (0, 0, i, 0))
     return pl.pallas_call(
         middle_kernel,
         grid=(NG // KY_BLOCK,),
@@ -143,24 +187,19 @@
         out_specs=block,
         out_shape=jax.ShapeDtypeStruct(WIDE, F32),
         compiler_params=PARAMS,
+        name="middle",
     )(field, kernel, left)
 
 
 def backward(field, first, second, right, left):
-    orbital = pl.BlockSpec((X_BLOCK, NG, NG), lambda i: (i, 0, 0))
     return pl.pallas_call(
         backward_kernel,
         grid=(NG // X_BLOCK,),
-        in_specs=[
-            pl.BlockSpec((X_BLOCK, NG, 2 * LANES), lambda i: (i, 0, 0)),
-            orbital,
-            orbital,
-            RIGHT_SPEC,
-            LEFT_SPEC,
-        ],
-        out_specs=orbital,
+        in_specs=[FIELD_SPEC, ORBITAL_SPEC, ORBITAL_SPEC, RIGHT_SPEC, LEFT_SPEC],
+        out_specs=ORBITAL_SPEC,
         out_shape=jax.ShapeDtypeStruct(CUBE, F32),
         compiler_params=PARAMS,
+        name="backward",
     )(field, first, second, right, left)
 
 
@@ -173,19 +212,35 @@
     return lax.ppermute(slab, AXES, pairs)
 
 
+def gathered(block, axis):
+    return lax.all_gather(block, axis, axis=0, tiled=True)
+
+
 def body(orbitals):
-    slab = orbitals.reshape(SLAB * NG * NG // LANES, LANES)
+    slab = pack(orbitals.reshape(SLAB, NG, NG)).reshape(SLAB * PACKED, LANES)
     right = jnp.asarray(right_table())
     left = jnp.asarray(left_table())
     kernel = kernel_table()
-    first = lax.all_gather(exchanged_slabs(slab), ("zh", "x"), axis=0, tiled=True).reshape(CUBE)
+    visiting = exchanged_slabs(slab)
+    pair = gathered(slab, "zl")
+    pair, visiting = lax.optimization_barrier((pair, visiting))
+    own = gathered(pair, "y").reshape(CUBE)
+    over_zh = gathered(visiting[None], "zh")
+    half = SLAB * PACKED // 2
+    parts = [gathered(over_zh[None, :, at * half : (at + 1) * half], "x") for at in range(2)]
+    first = jnp.stack(parts, axis=2)
+    first = first.transpose(1, 0, 2, 3, 4).reshape(CUBE)
     second = lax.ppermute(first, "core", [(0, 1), (1, 0)])
-    own = lax.all_gather(slab, GRID, axis=0, tiled=True).reshape(CUBE)
     field = forward(own, first, second, right, left)
     field = middle(field, kernel, left)
-    terms = backward(field, first, second, right, left).reshape(NG * NG * NG // LANES, LANES)
-    total = lax.psum_scatter(terms, GRID, scatter_dimension=0, tiled=True)
-    return total.reshape(orbitals.shape)
+    terms = backward(field, first, second, right, left).reshape(NG * PACKED, LANES)
+    both = lax.psum_scatter(terms, "y", scatter_dimension=0, tiled=True)
+    rows = SLAB * PACKED
+    place = lax.axis_index("zl")
+    mine = lax.dynamic_slice_in_dim(both, place * rows, rows)
+    other = lax.dynamic_slice_in_dim(both, (1 - place) * rows, rows)
+    total = mine + lax.ppermute(other, "zl", [(0, 1), (1, 0)])
+    return unpack(total.reshape(SLAB, PACKED, LANES)).reshape(orbitals.shape)
 
 
 def solution(mesh):

time: 350 us -> 204 us (0.58)
  waiting for transfers between devices: 243 us -> 55.2 us
  blocking collectives: 0 us -> 67.5 us
  Pallas kernels: 65.5 us -> 41 us
  local copies, waits for them, and re-layouts: 17.6 us -> 6.68 us
  starting transfers between devices: 4.82 us -> 13.8 us
    all_gather x2 -> x1, waiting for transfers between devices: 145 us -> 0.01 us  [gathered(): return lax.all_gather(block, axis, axis=0, tiled=True)]
    all_gather x0 -> x4, blocking collectives: none -> 67.5 us  [gathered(): return lax.all_gather(block, axis, axis=0, tiled=True)]
    reduce_scatter x1, waiting for transfers between devices: 96.7 us -> 50.2 us  [body(): both = lax.psum_scatter(terms, 'y', scatter_dimension=0, tiled=True)]
    pallas_call x1, Pallas kernels: 37.3 us -> 14.8 us  [middle(): pl.pallas_call(middle_kernel, grid=(NG // KY_BLOCK,), in_specs=[block, pl...]
    reshape x4 -> x2, local copies, waits for them, and re-layouts: 15.2 us -> 2.09 us  [the longest x1 1.08 us: body(): slab = pack(orbitals.reshape(SLAB, NG, NG)).reshape(SLAB * PACKED, LANES)]
    ppermute x1, starting transfers between devices: 4.07 us -> 9.87 us  [body(): second = lax.ppermute(first, 'core', [(0, 1), (1, 0)])]
    ppermute x0 -> x1, waiting for transfers between devices: none -> 4.96 us  [body(): total = mine + lax.ppermute(other, 'zl', [(0, 1), (1, 0)])]
  transfers between devices with their start and end apart: 5 -> 5, of which waited for: 3 -> 2; matrix products, arithmetic and copies ran while one was open for 3% -> 2% of each run, Pallas kernels for 0% -> 0%
where the time goes in v2:
time: 204 us; the launch traced here: 203 us
  blocking collectives  67.5 us (33%)
  waiting for transfers between devices  55.2 us (27%)
  Pallas kernels  41 us (20%)
  starting transfers between devices  13.8 us (7%)
  between operations  13.5 us (7%)
  local copies, waits for them, and re-layouts  6.68 us (3%)
  other arithmetic  5.14 us (3%)
    all_gather x4, blocking collectives, gathered(): return lax.all_gather(block, axis, axis=0, tiled=True)  67.5 us
    reduce_scatter x1, waiting for transfers between devices, body(): both = lax.psum_scatter(terms, 'y', scatter_dimension=0, tiled=True)  50.2 us
    pallas_call x1, Pallas kernels, middle(): pl.pallas_call(middle_kernel, grid=(NG // KY_BLOCK,), in_specs=[block, pl...  14.8 us
    pallas_call x1, Pallas kernels, backward(): pl.pallas_call(backward_kernel, grid=(NG // X_BLOCK,), in_specs=[FIELD_SP...  13.9 us
    pallas_call x1, Pallas kernels, forward(): pl.pallas_call(forward_kernel, grid=(NG // X_BLOCK,), in_specs=[ORBITAL_S...  12.4 us
    ppermute x1, starting transfers between devices, body(): second = lax.ppermute(first, 'core', [(0, 1), (1, 0)])  9.87 us
    ppermute x1, waiting for transfers between devices, body(): total = mine + lax.ppermute(other, 'zl', [(0, 1), (1, 0)])  4.96 us
  transfers between devices with their start and end apart: 5, of which 2 were waited for; matrix products, arithmetic and copies ran while one was open for 2% of the time, Pallas kernels for 0%

profile of v2, /device:TPU:1, one launch (start us, length us, event | category | flops | bytes accessed | tf_op | source)
XLA Modules:
  0.0 202.9 jit_solution(16602120301685733139)
XLA Ops:
  6.5 1.1 reshape.78
  7.8 0.7 collective-permute-start
  8.5 11.7 %all_gather.15 = bf16[864,128]{1,0:T(8,128)(2,1)} all-gather(bf16[432,128]{1,0:T(8,128)(2,1)S(1)} %bitcast.22), channel_id=1, replica_groups=mesh['zh'=4,'x'=4,'core'=2,'y'=8,'zl'=2] {'zl'}, dimensions={0}, use_global_device_ids=true | all-gather | bytes 331776 | tf_op jit(solution)/shard_map/all_gather | solution.py:216
  20.4 26.9 %all-gather = bf16[1728,128]{1,0:T(8,128)(2,1)S(1)} all-gather(bf16[432,128]{1,0:T(8,128)(2,1)S(1)} %collective-permute-done), channel_id=2, replica_groups=mesh['zh'=4,'x'=4,'core'=2,'y'=8,'zl'=2] {'zh'}, dimensions={0}, use_global_device_ids=true | all-gather | bytes 552960 | tf_op jit(solution)/shard_map/all_gather | solution.py:216
  47.3 15.7 %all-gather.1 = bf16[16,216,128]{2,1,0:T(8,128)(2,1)S(1)} all-gather(bf16[4,216,128]{2,1,0:T(8,128)(2,1)S(1)} %get-tuple-element.9), channel_id=3, replica_groups=mesh['zh'=4,'x'=4,'core'=2,'y'=8,'zl'=2] {'x'}, dimensions={0}, use_global_device_ids=true | all-gather | bytes 1105920 | tf_op jit(solution)/shard_map/all_gather | solution.py:216
  63.0 13.1 %all-gather.2 = bf16[16,216,128]{2,1,0:T(8,128)(2,1)S(1)} all-gather(bf16[4,216,128]{2,1,0:T(8,128)(2,1)S(1)} %get-tuple-element.10), channel_id=4, replica_groups=mesh['zh'=4,'x'=4,'core'=2,'y'=8,'zl'=2] {'x'}, dimensions={0}, use_global_device_ids=true | all-gather | bytes 1105920 | tf_op jit(solution)/shard_map/all_gather | solution.py:216
  76.2 0.2 maximum_bitcast_fusion
  76.3 0.1 copy.11
  76.5 9.9 %collective-permute-start.1 = (bf16[96,72,128]{2,1,0:T(8,128)(2,1)S(1)}, bf16[96,72,128]{2,1,0:T(8,128)(2,1)S(1)}, u32[]{:S(2)}, u32[]{:S(2)}) collective-permute-start(bf16[96,72,128]{2,1,0:T(8,128)(2,1)S(1)} %bitcast.11), channel_id=1, source_target_pairs={{0,16},{16,0},{1,17},{17,1},{2,18},{18,2},{3,19},{19,3},{4,20},{20... | collective-permute-start | bytes 5308424 | tf_op jit(solution)/shard_map/ppermute | solution.py:233
  86.4 3.7 %fusion.3.kernel_ref = f32[96,96,128]{2,1,0:T(8,128)} fusion(f32[128]{0:T(128)S(1)} %pad_multiply_fusion, f32[96,96]{1,0:T(8,128)S(1)} %broadcast_add_fusion), kind=kLoop, calls=%fused_computation.5 | loop fusion | flops 11796480 | bytes 4755968 | tf_op jit(solution)/shard_map/mul | solution.py:64
  90.2 1.5 copy-done.1
  91.6 0.9 copy-done.2
  92.5 0.9 copy-done.3
  93.4 12.4 %forward.1.field_ref = f32[2,96,96,128]{3,2,1,0:T(8,128)} custom-call(bf16[96,72,128]{2,1,0:T(8,128)(2,1)S(1)} %bitcast.14, bf16[96,72,128]{2,1,0:T(8,128)(2,1)S(1)} %bitcast.12, bf16[96,72,128]{2,1,0:T(8,128)(2,1)S(1)} %collective-permute-done.1.second_ref, bf16[256,256]{1,0:T(8,128)(2,1)S(1)} %copy-done.3, bf16[192,192]{1,0:T(8,128)(2,1)S(1)} %copy-done.2), custom_call_target="tpu_custom_call" | custom-call | tf_op jit(solution)/shard_map/forward/pallas_call | solution.py:170
  105.8 14.8 %middle.1.field_ref = f32[2,96,96,128]{3,2,1,0:T(8,128)} custom-call(f32[2,96,96,128]{3,2,1,0:T(8,128)} %forward.1.field_ref, f32[96,96,128]{2,1,0:T(8,128)S(1)} %copy-done, bf16[192,192]{1,0:T(8,128)(2,1)S(1)} %copy-done.2), custom_call_target="tpu_custom_call" | custom-call | tf_op jit(solution)/shard_map/middle/pallas_call | solution.py:183
  120.6 13.9 %backward.1 = f32[96,72,128]{2,1,0:T(8,128)} custom-call(f32[2,96,96,128]{3,2,1,0:T(8,128)} %middle.1.field_ref, bf16[96,72,128]{2,1,0:T(8,128)(2,1)S(1)} %bitcast.13, bf16[96,72,128]{2,1,0:T(8,128)(2,1)S(1)} %collective-permute-done.1.second_ref, bf16[256,256]{1,0:T(8,128)(2,1)S(1)} %copy-done.3, bf16[192,192]{1,0:T(8,128)(2,1)S(1)} %copy-done.2), custom_call_target="tpu_custom_call" | custom-call | tf_op jit(solution)/shard_map/backward/pallas_call | solution.py:195
  134.5 50.2 %reduce-scatter.2.cloned.1.call-done = f32[864,128]{1,0:T(8,128)} async-done(((f32[6912,128]{1,0:T(8,128)}), f32[864,128]{1,0:T(8,128)}) %reduce-scatter.2.cloned.1.call-update) | async-done | bytes 442384 | tf_op jit(solution)/shard_map/reduce_scatter | solution.py:237
  184.7 0.9 constant_dynamic-slice_fusion
  185.7 3.3 %collective-permute-start.2 = (f32[432,128]{1,0:T(8,128)S(1)}, f32[432,128]{1,0:T(8,128)S(1)}, u32[]{:S(2)}, u32[]{:S(2)}) collective-permute-start(f32[432,128]{1,0:T(8,128)S(1)} %constant_dynamic-slice_fusion), channel_id=1, source_target_pairs={{0,1},{1,0},{2,3},{3,2},{4,5},{5,4},{6,7},{7,6},{8,9},{9,8},{10,11... | collective-permute-start | bytes 663560 | tf_op jit(solution)/shard_map/ppermute | solution.py:242
  188.9 5.0 %collective-permute-done.2 = f32[432,128]{1,0:T(8,128)S(1)} collective-permute-done((f32[432,128]{1,0:T(8,128)S(1)}, f32[432,128]{1,0:T(8,128)S(1)}, u32[]{:S(2)}, u32[]{:S(2)}) %collective-permute-start.2) | collective-permute-done | bytes 221216 | tf_op jit(solution)/shard_map/ppermute | solution.py:242
  193.9 1.0 dynamic-slice_add_fusion
  194.9 0.1 fusion.12
  195.0 0.1 maximum_maximum_fusion
  195.1 1.0 reshape.84
  (20 shorter events, 0.4 us)
Async XLA Ops:
  6.5 83.6 %all-gather.5.cloned.1.call-start = ((), (), s32[]{:S(2)}) async-start(), calls=%async_computation.1 | async-start | bytes 1990656 | tf_op jit(solution)/shard_map/all_gather | solution.py:216
  7.8 12.4 %collective-permute-start = (bf16[432,128]{1,0:T(8,128)(2,1)S(1)}, bf16[432,128]{1,0:T(8,128)(2,1)S(1)}, u32[]{:S(2)}, u32[]{:S(2)}) collective-permute-start(bf16[432,128]{1,0:T(8,128)(2,1)S(1)} %bitcast.21), channel_id=1, source_target_pairs={{0,0},{1,32},{2,64},{3,96},{4,128},{5,160},{6,192},{7,224},{8,256}... | collective-permute-start | bytes 331784 | tf_op jit(solution)/shard_map/ppermute | solution.py:212
  20.3 164.4 %reduce-scatter.2.cloned.1.call-start = ((), (), s32[]{:S(2)}) async-start(), calls=%async_computation.2 | async-start | bytes 3981312 | tf_op jit(solution)/shard_map/reduce_scatter | solution.py:237
  76.5 13.7 %collective-permute-start.1 = (bf16[96,72,128]{2,1,0:T(8,128)(2,1)S(1)}, bf16[96,72,128]{2,1,0:T(8,128)(2,1)S(1)}, u32[]{:S(2)}, u32[]{:S(2)}) collective-permute-start(bf16[96,72,128]{2,1,0:T(8,128)(2,1)S(1)} %bitcast.11), channel_id=1, source_target_pairs={{0,16},{16,0},{1,17},{17,1},{2,18},{18,2},{3,19},{19,3},{4,20},{20... | collective-permute-start | bytes 5308424 | tf_op jit(solution)/shard_map/ppermute | solution.py:233
  90.1 1.5 copy-start.1
  91.6 0.9 copy-start.2
  92.5 0.9 copy-start.3
  93.4 12.4 %copy-start = (f32[96,96,128]{2,1,0:T(8,128)S(1)}, f32[96,96,128]{2,1,0:T(8,128)}, u32[]{:S(2)}) copy-start(f32[96,96,128]{2,1,0:T(8,128)} %fusion.3.kernel_ref) | copy-start | bytes 14155780
  185.7 8.2 %collective-permute-start.2 = (f32[432,128]{1,0:T(8,128)S(1)}, f32[432,128]{1,0:T(8,128)S(1)}, u32[]{:S(2)}, u32[]{:S(2)}) collective-permute-start(f32[432,128]{1,0:T(8,128)S(1)} %constant_dynamic-slice_fusion), channel_id=1, source_target_pairs={{0,1},{1,0},{2,3},{3,2},{4,5},{5,4},{6,7},{7,6},{8,9},{9,8},{10,11... | collective-permute-start | bytes 663560 | tf_op jit(solution)/shard_map/ppermute | solution.py:242
Sparse Core Ops, SparseCore 0:
  20.4 57.9 all-gather.4
  134.6 50.0 reduce-scatter.1

commit v3 on v2

--- a/solution.py
+++ b/solution.py
@@ -22,8 +22,10 @@
 SIZES = (4, 4, 2, 8, 2)
 BAND = ("zh", "x", "core")
 GRID = ("y", "zl")
-X_BLOCK = 8
-KY_BLOCK = 8
+BLOCK = 24
+BATCH = 24
+PITCH = NG + 8
+UNROLL = 1
 
 
 def cas_halves():
@@ -119,88 +121,114 @@
     return jnp.where(lane_mask(PACKED, 0, NG), plane[:PACKED], jnp.concatenate(sides, axis=0))
 
 
-def forward_kernel(own_ref, first_ref, second_ref, right_ref, left_ref, out_ref):
-    for at in range(X_BLOCK):
-        own = own_ref[at].astype(F32)
-        first = unpack_plane(own * first_ref[at].astype(F32))
-        second = unpack_plane(own * second_ref[at].astype(F32))
-        rows = right_transform(jnp.concatenate([first, second], axis=0), right_ref[...])
-        columns = jnp.concatenate([rows[:NG], rows[NG:]], axis=1)
-        columns = left_transform(left_ref[...], columns)
-        out_ref[0, at] = columns[:, :LANES]
-        out_ref[1, at] = columns[:, LANES:]
-
-
-def middle_kernel(field_ref, kernel_ref, left_ref, out_ref):
-    field = field_ref.reshape(2 * NG * KY_BLOCK, LANES)
-    out = out_ref.reshape(2 * NG * KY_BLOCK, LANES)
-    for at in range(KY_BLOCK):
-        first = pl.ds(at, NG, stride=KY_BLOCK)
-        second = pl.ds(NG * KY_BLOCK + at, NG, stride=KY_BLOCK)
-        columns = jnp.concatenate([field[first, :], field[second, :]], axis=1)
-        columns = left_transform(left_ref[...], columns)
-        weight = kernel_ref[at]
-        columns = columns * jnp.concatenate([weight, weight], axis=1)
-        columns = left_transform(left_ref[...], columns)
-        out[first, :] = columns[:, :LANES]
-        out[second, :] = columns[:, LANES:]
-
-
-def backward_kernel(field_ref, first_ref, second_ref, right_ref, left_ref, out_ref):
-    for at in range(X_BLOCK):
-        columns = jnp.concatenate([field_ref[0, at], field_ref[1, at]], axis=1)
-        columns = left_transform(left_ref[...], columns)
-        rows = jnp.concatenate([columns[:, :LANES], columns[:, LANES:]], axis=0)
-        rows = right_transform(rows, right_ref[...])
-        first = pack_plane(rows[:NG]) * first_ref[at].astype(F32)
-        second = pack_plane(rows[NG:]) * second_ref[at].astype(F32)
-        out_ref[at] = first + second
-
-
-PARAMS = pltpu.CompilerParams(vmem_limit_bytes=48 * 1024 * 1024)
+def place(pair, plane):
+    return pl.ds(pl.multiple_of((pair * NG + plane) * PITCH, 8), NG)
+
+
+def line(pair, ky):
+    return pl.ds(pair * NG * PITCH + ky, NG, stride=PITCH)
+
+
+def side_by_side(tiles):
+    return jnp.concatenate(tiles, axis=1)
+
+
+def stacked(tiles):
+    return jnp.concatenate(tiles, axis=0)
+
+
+def lane_tiles(wide):
+    return [wide[:, at : at + LANES] for at in range(0, wide.shape[1], LANES)]
+
+
+def row_tiles(tall):
+    return [tall[at : at + NG] for at in range(0, tall.shape[0], NG)]
+
+
+def pairs_kernel(own_ref, first_ref, second_ref, kernel_ref, right_ref, left_ref, out_ref, field):
+    step = pl.program_id(0)
+    steps = NG // BLOCK
+    right = right_ref[...]
+    left = left_ref[...]
+
+    @pl.when(step < steps)
+    def forward():
+        @pl.loop(0, BLOCK // BATCH, unroll=UNROLL)
+        def _(group):
+            rows = []
+            for at in range(BATCH):
+                plane = group * BATCH + at
+                own = own_ref[plane].astype(F32)
+                rows.append(unpack_plane(own * first_ref[plane].astype(F32)))
+                rows.append(unpack_plane(own * second_ref[plane].astype(F32)))
+            rows = right_transform(stacked(rows), right)
+            columns = left_transform(left, side_by_side(row_tiles(rows)))
+            for at, tile in enumerate(lane_tiles(columns)):
+                plane = step * BLOCK + group * BATCH + at // 2
+                field[place(at % 2, plane), :] = tile
+
+    @pl.when((step >= steps) & (step < 2 * steps))
+    def middle():
+        @pl.loop(0, BLOCK // BATCH, unroll=UNROLL)
+        def _(group):
+            base = (step - steps) * BLOCK + group * BATCH
+            lines = [line(at % 2, base + at // 2) for at in range(2 * BATCH)]
+            columns = left_transform(left, side_by_side([field[at, :] for at in lines]))
+            weights = [kernel_ref[group * BATCH + at // 2] for at in range(2 * BATCH)]
+            columns = left_transform(left, columns * side_by_side(weights))
+            for at, tile in zip(lines, lane_tiles(columns), strict=True):
+                field[at, :] = tile
+
+    @pl.when(step >= 2 * steps)
+    def backward():
+        @pl.loop(0, BLOCK // BATCH, unroll=UNROLL)
+        def _(group):
+            base = (step - 2 * steps) * BLOCK + group * BATCH
+            tiles = [field[place(at % 2, base + at // 2), :] for at in range(2 * BATCH)]
+            columns = left_transform(left, side_by_side(tiles))
+            tiles = row_tiles(right_transform(stacked(lane_tiles(columns)), right))
+            for at in range(BATCH):
+                plane = group * BATCH + at
+                first = pack_plane(tiles[2 * at]) * first_ref[plane].astype(F32)
+                second = pack_plane(tiles[2 * at + 1]) * second_ref[plane].astype(F32)
+                out_ref[plane] = first + second
+
+
 CUBE = (NG, PACKED, LANES)
-WIDE = (2, NG, NG, LANES)
-RIGHT_SPEC = pl.BlockSpec((2 * LANES, 2 * LANES), lambda i: (0, 0))
-LEFT_SPEC = pl.BlockSpec((2 * NG, 2 * NG), lambda i: (0, 0))
-ORBITAL_SPEC = pl.BlockSpec((X_BLOCK, PACKED, LANES), lambda i: (i, 0, 0))
-FIELD_SPEC = pl.BlockSpec((2, X_BLOCK, NG, LANES), lambda i: (0, i, 0, 0))
-
-
-def forward(own, first, second, right, left):
+
+
+def pair_terms(own, first, second, kernel, right, left):
+    steps = NG // BLOCK
+
+    def clipped(i, low):
+        return jnp.clip(i - low, 0, steps - 1)
+
+    def both(i):
+        return jnp.where(i < steps, i, clipped(i, 2 * steps))
+
+    def planes(place_of):
+        return pl.BlockSpec((BLOCK, PACKED, LANES), lambda i: (place_of(i), 0, 0))
+
     return pl.pallas_call(
-        forward_kernel,
-        grid=(NG // X_BLOCK,),
-        in_specs=[ORBITAL_SPEC, ORBITAL_SPEC, ORBITAL_SPEC, RIGHT_SPEC, LEFT_SPEC],
-        out_specs=FIELD_SPEC,
-        out_shape=jax.ShapeDtypeStruct(WIDE, F32),
-        compiler_params=PARAMS,
-        name="forward",
-    )(own, first, second, right, left)
-
-
-def middle(field, kernel, left):
-    block = pl.BlockSpec((2, NG, KY_BLOCK, LANES), lambda i: (0, 0, i, 0))
-    return pl.pallas_call(
-        middle_kernel,
-        grid=(NG // KY_BLOCK,),
-        in_specs=[block, pl.BlockSpec((KY_BLOCK, NG, LANES), lambda i: (i, 0, 0)), LEFT_SPEC],
-        out_specs=block,
-        out_shape=jax.ShapeDtypeStruct(WIDE, F32),
-        compiler_params=PARAMS,
-        name="middle",
-    )(field, kernel, left)
-
-
-def backward(field, first, second, right, left):
-    return pl.pallas_call(
-        backward_kernel,
-        grid=(NG // X_BLOCK,),
-        in_specs=[FIELD_SPEC, ORBITAL_SPEC, ORBITAL_SPEC, RIGHT_SPEC, LEFT_SPEC],
-        out_specs=ORBITAL_SPEC,
+        pairs_kernel,
+        grid=(3 * steps,),
+        in_specs=[
+            planes(lambda i: clipped(i, 0)),
+            planes(both),
+            planes(both),
+            pl.BlockSpec((BLOCK, NG, LANES), lambda i: (clipped(i, steps), 0, 0)),
+            pl.BlockSpec((2 * LANES, 2 * LANES), lambda i: (0, 0)),
+            pl.BlockSpec((2 * NG, 2 * NG), lambda i: (0, 0)),
+        ],
+        out_specs=planes(lambda i: clipped(i, 2 * steps)),
         out_shape=jax.ShapeDtypeStruct(CUBE, F32),
-        compiler_params=PARAMS,
-        name="backward",
-    )(field, first, second, right, left)
+        scratch_shapes=[pltpu.VMEM((2 * NG * PITCH, LANES), F32)],
+        compiler_params=pltpu.CompilerParams(vmem_limit_bytes=58 * 1024 * 1024),
+        cost_estimate=pl.CostEstimate(
+            flops=2 * 6 * 2 * NG * NG * 256 * 256, bytes_accessed=17_000_000, transcendentals=0
+        ),
+        name="pair_terms",
+    )(own, first, second, kernel, right, left)
 
 
 def exchanged_slabs(slab):
@@ -231,9 +259,7 @@
     first = jnp.stack(parts, axis=2)
     first = first.transpose(1, 0, 2, 3, 4).reshape(CUBE)
     second = lax.ppermute(first, "core", [(0, 1), (1, 0)])
-    field = forward(own, first, second, right, left)
-    field = middle(field, kernel, left)
-    terms = backward(field, first, second, right, left).reshape(NG * PACKED, LANES)
+    terms = pair_terms(own, first, second, kernel, right, left).reshape(NG * PACKED, LANES)
     both = lax.psum_scatter(terms, "y", scatter_dimension=0, tiled=True)
     rows = SLAB * PACKED
     place = lax.axis_index("zl")

time: 204 us -> 183 us (0.90)
  Pallas kernels: 41 us -> 22.9 us
    pallas_call x3 -> x1, Pallas kernels: 41 us -> 22.9 us  [pair_terms(): pl.pallas_call(pairs_kernel, grid=(3 * steps,), in_specs=[planes(lambda i...]
where the time goes in v3:
time: 183 us
  blocking collectives  67.5 us (37%)
  waiting for transfers between devices  55.2 us (30%)
  Pallas kernels  22.9 us (13%)
  starting transfers between devices  13.8 us (8%)
  between operations  13.5 us (7%)
  other arithmetic  5.14 us (3%)
  local copies, waits for them, and re-layouts  4.7 us (3%)
    all_gather x4, blocking collectives, gathered(): return lax.all_gather(block, axis, axis=0, tiled=True)  67.5 us
    reduce_scatter x1, waiting for transfers between devices, body(): both = lax.psum_scatter(terms, 'y', scatter_dimension=0, tiled=True)  50.2 us
    pallas_call x1, Pallas kernels, pair_terms(): pl.pallas_call(pairs_kernel, grid=(3 * steps,), in_specs=[planes(lambda i...  22.9 us
    ppermute x1, starting transfers between devices, body(): second = lax.ppermute(first, 'core', [(0, 1), (1, 0)])  9.87 us
    ppermute x1, waiting for transfers between devices, body(): total = mine + lax.ppermute(other, 'zl', [(0, 1), (1, 0)])  4.96 us
    mul x1, other arithmetic, kernel_table(): return jnp.where(square > 0, values, 0.0) * (-MIXING / float(NG) ** 3)  3.7 us
  transfers between devices with their start and end apart: 5, of which 2 were waited for; matrix products, arithmetic and copies ran while one was open for 2% of the time, Pallas kernels for 0%

profile of v3, /device:TPU:1, one launch (start us, length us, event | category | flops | bytes accessed | tf_op | source)
XLA Modules:
  0.0 182.8 jit_solution(12155790216590079834)
XLA Ops:
  6.5 1.1 reshape.78
  7.6 0.1 fusion.13
  7.7 0.1 maximum_maximum_fusion.1
  7.8 0.7 collective-permute-start
  8.5 11.7 %all_gather.15 = bf16[864,128]{1,0:T(8,128)(2,1)} all-gather(bf16[432,128]{1,0:T(8,128)(2,1)S(1)} %bitcast.20), channel_id=1, replica_groups=mesh['zh'=4,'x'=4,'core'=2,'y'=8,'zl'=2] {'zl'}, dimensions={0}, use_global_device_ids=true | all-gather | bytes 331776 | tf_op jit(solution)/shard_map/all_gather | solution.py:244
  20.3 0.0 reduce-scatter.2.cloned.1.call-start
  20.4 26.9 %all-gather = bf16[1728,128]{1,0:T(8,128)(2,1)S(1)} all-gather(bf16[432,128]{1,0:T(8,128)(2,1)S(1)} %collective-permute-done), channel_id=2, replica_groups=mesh['zh'=4,'x'=4,'core'=2,'y'=8,'zl'=2] {'zh'}, dimensions={0}, use_global_device_ids=true | all-gather | bytes 552960 | tf_op jit(solution)/shard_map/all_gather | solution.py:244
  47.3 15.7 %all-gather.1 = bf16[16,216,128]{2,1,0:T(8,128)(2,1)S(1)} all-gather(bf16[4,216,128]{2,1,0:T(8,128)(2,1)S(1)} %get-tuple-element.9), channel_id=3, replica_groups=mesh['zh'=4,'x'=4,'core'=2,'y'=8,'zl'=2] {'x'}, dimensions={0}, use_global_device_ids=true | all-gather | bytes 1105920 | tf_op jit(solution)/shard_map/all_gather | solution.py:244
  63.0 13.1 %all-gather.2 = bf16[16,216,128]{2,1,0:T(8,128)(2,1)S(1)} all-gather(bf16[4,216,128]{2,1,0:T(8,128)(2,1)S(1)} %get-tuple-element.10), channel_id=4, replica_groups=mesh['zh'=4,'x'=4,'core'=2,'y'=8,'zl'=2] {'x'}, dimensions={0}, use_global_device_ids=true | all-gather | bytes 1105920 | tf_op jit(solution)/shard_map/all_gather | solution.py:244
  76.2 0.2 maximum_bitcast_fusion
  76.3 0.1 copy.11
  76.5 9.9 %collective-permute-start.1 = (bf16[96,72,128]{2,1,0:T(8,128)(2,1)S(1)}, bf16[96,72,128]{2,1,0:T(8,128)(2,1)S(1)}, u32[]{:S(2)}, u32[]{:S(2)}) collective-permute-start(bf16[96,72,128]{2,1,0:T(8,128)(2,1)S(1)} %bitcast.16), channel_id=1, source_target_pairs={{0,16},{16,0},{1,17},{17,1},{2,18},{18,2},{3,19},{19,3},{4,20},{20... | collective-permute-start | bytes 5308424 | tf_op jit(solution)/shard_map/ppermute | solution.py:261
  86.4 0.1 broadcast_add_fusion
  86.5 3.7 %fusion.3.kernel_ref = f32[96,96,128]{2,1,0:T(8,128)} fusion(f32[128]{0:T(128)S(1)} %pad_multiply_fusion, f32[96,96]{1,0:T(8,128)S(1)} %broadcast_add_fusion), kind=kLoop, calls=%fused_computation.5 | loop fusion | flops 11796480 | bytes 4755968 | tf_op jit(solution)/shard_map/mul | solution.py:66
  90.2 1.3 copy-done.1
  91.5 22.9 %pair_terms.1 = f32[96,72,128]{2,1,0:T(8,128)} custom-call(bf16[96,72,128]{2,1,0:T(8,128)(2,1)} %bitcast.21, bf16[96,72,128]{2,1,0:T(8,128)(2,1)} %bitcast.17, bf16[96,72,128]{2,1,0:T(8,128)(2,1)} %copy-done.1, f32[96,96,128]{2,1,0:T(8,128)} %fusion.3.kernel_ref, bf16[256,256]{1,0:T(8,128)(2,1)} %constant.38.clone.right_ref, ...), custom_call_target="tpu_custom_call" | custom-call | flops 14495514624 | bytes 17000000 | tf_op jit(solution)/shard_map/pair_terms/pallas_call | solution.py:212
  114.4 50.2 %reduce-scatter.2.cloned.1.call-done = f32[864,128]{1,0:T(8,128)} async-done(((f32[6912,128]{1,0:T(8,128)}), f32[864,128]{1,0:T(8,128)}) %reduce-scatter.2.cloned.1.call-update) | async-done | bytes 442384 | tf_op jit(solution)/shard_map/reduce_scatter | solution.py:263
  164.6 0.9 constant_dynamic-slice_fusion
  165.5 3.3 %collective-permute-start.2 = (f32[432,128]{1,0:T(8,128)S(1)}, f32[432,128]{1,0:T(8,128)S(1)}, u32[]{:S(2)}, u32[]{:S(2)}) collective-permute-start(f32[432,128]{1,0:T(8,128)S(1)} %constant_dynamic-slice_fusion), channel_id=1, source_target_pairs={{0,1},{1,0},{2,3},{3,2},{4,5},{5,4},{6,7},{7,6},{8,9},{9,8},{10,11... | collective-permute-start | bytes 663560 | tf_op jit(solution)/shard_map/ppermute | solution.py:268
  168.8 5.0 %collective-permute-done.2 = f32[432,128]{1,0:T(8,128)S(1)} collective-permute-done((f32[432,128]{1,0:T(8,128)S(1)}, f32[432,128]{1,0:T(8,128)S(1)}, u32[]{:S(2)}, u32[]{:S(2)}) %collective-permute-start.2) | collective-permute-done | bytes 221216 | tf_op jit(solution)/shard_map/ppermute | solution.py:268
  173.8 1.0 dynamic-slice_add_fusion
  174.8 0.1 fusion.12
  174.9 0.1 maximum_maximum_fusion
  175.0 1.0 reshape.84
  (14 shorter events, 0.1 us)
Async XLA Ops:
  6.5 83.6 %all-gather.5.cloned.1.call-start = ((), (), s32[]{:S(2)}) async-start(), calls=%async_computation.1 | async-start | bytes 1990656 | tf_op jit(solution)/shard_map/all_gather | solution.py:244
  7.8 12.4 %collective-permute-start = (bf16[432,128]{1,0:T(8,128)(2,1)S(1)}, bf16[432,128]{1,0:T(8,128)(2,1)S(1)}, u32[]{:S(2)}, u32[]{:S(2)}) collective-permute-start(bf16[432,128]{1,0:T(8,128)(2,1)S(1)} %bitcast.19), channel_id=1, source_target_pairs={{0,0},{1,32},{2,64},{3,96},{4,128},{5,160},{6,192},{7,224},{8,256}... | collective-permute-start | bytes 331784 | tf_op jit(solution)/shard_map/ppermute | solution.py:240
  20.3 144.3 %reduce-scatter.2.cloned.1.call-start = ((), (), s32[]{:S(2)}) async-start(), calls=%async_computation.2 | async-start | bytes 3981312 | tf_op jit(solution)/shard_map/reduce_scatter | solution.py:263
  76.5 13.7 %copy-start = (bf16[4,4,2,216,128]{4,3,2,1,0:T(8,128)(2,1)}, bf16[4,4,2,216,128]{4,3,2,1,0:T(8,128)(2,1)S(1)}, u32[]{:S(2)}) copy-start(bf16[4,4,2,216,128]{4,3,2,1,0:T(8,128)(2,1)S(1)} %copy.11) | copy-start | bytes 5308420
  76.5 13.7 %collective-permute-start.1 = (bf16[96,72,128]{2,1,0:T(8,128)(2,1)S(1)}, bf16[96,72,128]{2,1,0:T(8,128)(2,1)S(1)}, u32[]{:S(2)}, u32[]{:S(2)}) collective-permute-start(bf16[96,72,128]{2,1,0:T(8,128)(2,1)S(1)} %bitcast.16), channel_id=1, source_target_pairs={{0,16},{16,0},{1,17},{17,1},{2,18},{18,2},{3,19},{19,3},{4,20},{20... | collective-permute-start | bytes 5308424 | tf_op jit(solution)/shard_map/ppermute | solution.py:261
  90.2 1.3 copy-start.1
  165.5 8.2 %collective-permute-start.2 = (f32[432,128]{1,0:T(8,128)S(1)}, f32[432,128]{1,0:T(8,128)S(1)}, u32[]{:S(2)}, u32[]{:S(2)}) collective-permute-start(f32[432,128]{1,0:T(8,128)S(1)} %constant_dynamic-slice_fusion), channel_id=1, source_target_pairs={{0,1},{1,0},{2,3},{3,2},{4,5},{5,4},{6,7},{7,6},{8,9},{9,8},{10,11... | collective-permute-start | bytes 663560 | tf_op jit(solution)/shard_map/ppermute | solution.py:268
Sparse Core Ops, SparseCore 0:
  20.4 57.9 all-gather.4
  114.5 50.0 reduce-scatter.1

commit v4 on v3

--- a/solution.py
+++ b/solution.py
@@ -1,3 +1,4 @@
+import functools
 import math
 
 import jax
@@ -22,8 +23,9 @@
 SIZES = (4, 4, 2, 8, 2)
 BAND = ("zh", "x", "core")
 GRID = ("y", "zl")
-BLOCK = 24
 BATCH = 24
+SLABS = BATCH // SLAB
+VMEM_MIB = 58
 PITCH = NG + 8
 UNROLL = 1
 
@@ -53,8 +55,7 @@
     )
 
 
-def kernel_table():
-    index = jnp.arange(NG, dtype=jnp.int32)
+def kernel_table(index):
     signed = jnp.where(index * 2 < NG, index, index - NG).astype(F32)
     wave = signed * (2.0 * math.pi / (NG * SPACING))
     wave_z = jnp.pad(wave, (0, LANES - NG))
@@ -145,60 +146,54 @@
     return [tall[at : at + NG] for at in range(0, tall.shape[0], NG)]
 
 
-def pairs_kernel(own_ref, first_ref, second_ref, kernel_ref, right_ref, left_ref, out_ref, field):
+def pairs_kernel(order_ref, own_ref, *refs):
+    *visitor_refs, kernel_ref, right_ref, left_ref, out_ref, field = refs
     step = pl.program_id(0)
-    steps = NG // BLOCK
+    steps = NG // BATCH
     right = right_ref[...]
     left = left_ref[...]
 
+    def visitor(pair, plane):
+        slab = lax.rem(plane // SLAB + order_ref[pair, steps], SLABS)
+        return visitor_refs[pair][slab * SLAB + plane % SLAB].astype(F32)
+
     @pl.when(step < steps)
     def forward():
-        @pl.loop(0, BLOCK // BATCH, unroll=UNROLL)
-        def _(group):
-            rows = []
-            for at in range(BATCH):
-                plane = group * BATCH + at
-                own = own_ref[plane].astype(F32)
-                rows.append(unpack_plane(own * first_ref[plane].astype(F32)))
-                rows.append(unpack_plane(own * second_ref[plane].astype(F32)))
-            rows = right_transform(stacked(rows), right)
-            columns = left_transform(left, side_by_side(row_tiles(rows)))
-            for at, tile in enumerate(lane_tiles(columns)):
-                plane = step * BLOCK + group * BATCH + at // 2
-                field[place(at % 2, plane), :] = tile
+        rows = []
+        for at in range(BATCH):
+            own = own_ref[at].astype(F32)
+            rows += [unpack_plane(own * visitor(pair, at)) for pair in range(2)]
+        rows = right_transform(stacked(rows), right)
+        columns = left_transform(left, side_by_side(row_tiles(rows)))
+        for at, tile in enumerate(lane_tiles(columns)):
+            field[place(at % 2, step * BATCH + at // 2), :] = tile
 
     @pl.when((step >= steps) & (step < 2 * steps))
     def middle():
-        @pl.loop(0, BLOCK // BATCH, unroll=UNROLL)
-        def _(group):
-            base = (step - steps) * BLOCK + group * BATCH
-            lines = [line(at % 2, base + at // 2) for at in range(2 * BATCH)]
-            columns = left_transform(left, side_by_side([field[at, :] for at in lines]))
-            weights = [kernel_ref[group * BATCH + at // 2] for at in range(2 * BATCH)]
-            columns = left_transform(left, columns * side_by_side(weights))
-            for at, tile in zip(lines, lane_tiles(columns), strict=True):
-                field[at, :] = tile
+        first = (step - steps) * BATCH
+        lines = [line(at % 2, first + at // 2) for at in range(2 * BATCH)]
+        columns = left_transform(left, side_by_side([field[at, :] for at in lines]))
+        columns = columns * side_by_side([kernel_ref[at // 2] for at in range(2 * BATCH)])
+        columns = left_transform(left, columns)
+        for at, tile in zip(lines, lane_tiles(columns), strict=True):
+            field[at, :] = tile
 
     @pl.when(step >= 2 * steps)
     def backward():
-        @pl.loop(0, BLOCK // BATCH, unroll=UNROLL)
-        def _(group):
-            base = (step - 2 * steps) * BLOCK + group * BATCH
-            tiles = [field[place(at % 2, base + at // 2), :] for at in range(2 * BATCH)]
-            columns = left_transform(left, side_by_side(tiles))
-            tiles = row_tiles(right_transform(stacked(lane_tiles(columns)), right))
-            for at in range(BATCH):
-                plane = group * BATCH + at
-                first = pack_plane(tiles[2 * at]) * first_ref[plane].astype(F32)
-                second = pack_plane(tiles[2 * at + 1]) * second_ref[plane].astype(F32)
-                out_ref[plane] = first + second
+        first = (step - 2 * steps) * BATCH
+        tiles = [field[place(at % 2, first + at // 2), :] for at in range(2 * BATCH)]
+        columns = left_transform(left, side_by_side(tiles))
+        tiles = row_tiles(right_transform(stacked(lane_tiles(columns)), right))
+        for at in range(BATCH):
+            terms = [pack_plane(tiles[2 * at + pair]) * visitor(pair, at) for pair in range(2)]
+            out_ref[at] = terms[0] + terms[1]
 
 
 CUBE = (NG, PACKED, LANES)
 
 
-def pair_terms(own, first, second, kernel, right, left):
-    steps = NG // BLOCK
+def pair_terms(order, own, first, second, kernel, right, left):
+    steps = NG // BATCH
 
     def clipped(i, low):
         return jnp.clip(i - low, 0, steps - 1)
@@ -206,38 +201,74 @@
     def both(i):
         return jnp.where(i < steps, i, clipped(i, 2 * steps))
 
-    def planes(place_of):
-        return pl.BlockSpec((BLOCK, PACKED, LANES), lambda i: (place_of(i), 0, 0))
+    def planes(count, place_of):
+        return pl.BlockSpec((count, PACKED, LANES), lambda i, order: (place_of(i, order), 0, 0))
+
+    def visitor(pair):
+        return planes(BATCH, lambda i, order: order[pair, both(i)])
 
     return pl.pallas_call(
         pairs_kernel,
-        grid=(3 * steps,),
-        in_specs=[
-            planes(lambda i: clipped(i, 0)),
-            planes(both),
-            planes(both),
-            pl.BlockSpec((BLOCK, NG, LANES), lambda i: (clipped(i, steps), 0, 0)),
-            pl.BlockSpec((2 * LANES, 2 * LANES), lambda i: (0, 0)),
-            pl.BlockSpec((2 * NG, 2 * NG), lambda i: (0, 0)),
-        ],
-        out_specs=planes(lambda i: clipped(i, 2 * steps)),
+        grid_spec=pltpu.PrefetchScalarGridSpec(
+            num_scalar_prefetch=1,
+            grid=(3 * steps,),
+            in_specs=[
+                planes(BATCH, lambda i, order: clipped(i, 0)),
+                visitor(0),
+                visitor(1),
+                pl.BlockSpec((BATCH, NG, LANES), lambda i, order: (clipped(i, steps), 0, 0)),
+                pl.BlockSpec((2 * LANES, 2 * LANES), lambda i, order: (0, 0)),
+                pl.BlockSpec((2 * NG, 2 * NG), lambda i, order: (0, 0)),
+            ],
+            out_specs=planes(BATCH, lambda i, order: clipped(i, 2 * steps)),
+            scratch_shapes=[pltpu.VMEM((2 * NG * PITCH, LANES), F32)],
+        ),
         out_shape=jax.ShapeDtypeStruct(CUBE, F32),
-        scratch_shapes=[pltpu.VMEM((2 * NG * PITCH, LANES), F32)],
-        compiler_params=pltpu.CompilerParams(vmem_limit_bytes=58 * 1024 * 1024),
+        compiler_params=pltpu.CompilerParams(vmem_limit_bytes=VMEM_MIB * 1024 * 1024),
         cost_estimate=pl.CostEstimate(
-            flops=2 * 6 * 2 * NG * NG * 256 * 256, bytes_accessed=17_000_000, transcendentals=0
+            flops=4 * 6 * NG * NG * 256 * 256, bytes_accessed=17_000_000, transcendentals=0
         ),
         name="pair_terms",
-    )(own, first, second, kernel, right, left)
+    )(order, own, first, second, kernel, right, left)
+
+
+def meeting_place(zh, x, core):
+    return (zh + 4 * ((x % 2 + core) % 2)) % 8, x // 2
+
+
+def landing(zh, x, y, zl, meeting_y):
+    apart = (y - meeting_y // 2 * 2) % 8
+    return (zh + 2 * (apart % 2) + zl) % 4, (x + apart // 2) % 4
 
 
 def exchanged_slabs(slab):
     pairs = []
-    for pair in range(16):
-        for core in range(2):
-            for place in range(16):
-                pairs.append(((pair * 2 + core) * 16 + place, (place * 2 + core) * 16 + pair))
+    for zh, x, core, y, zl in np.ndindex(*SIZES):
+        there_y, there_zl = meeting_place(zh, x, core)
+        there_zh, there_x = landing(zh, x, y, zl, there_y)
+        target = (there_zh, there_x, core, there_y, there_zl)
+        pairs.append(
+            (int(np.ravel_multi_index((zh, x, core, y, zl), SIZES)), int(np.ravel_multi_index(target, SIZES)))
+        )
     return lax.ppermute(slab, AXES, pairs)
+
+
+def visiting_order(core):
+    y, zl = lax.axis_index("y"), lax.axis_index("zl")
+    zh = y % 4
+    x = 2 * zl + (y // 4 + core) % 2
+    block = jnp.arange(4, dtype=jnp.int32)
+    apart = (x + block - y // 2 - lax.axis_index("x")) % 4
+    place = jnp.where(apart == 3, 1, jnp.where(apart == 0, 0, apart + 1))
+    return jnp.concatenate([place, zh[None]]).astype(jnp.int32)
+
+
+def gathered_x(block):
+    def shifted(part, by):
+        return lax.ppermute(part, "x", [(at, (at + by) % 4) for at in range(4)])
+
+    before, after = shifted(block, 1), shifted(block, 3)
+    return [block, before, after, shifted(before[:2], 1), shifted(after[2:], 3)]
 
 
 def gathered(block, axis):
@@ -248,19 +279,20 @@
     slab = pack(orbitals.reshape(SLAB, NG, NG)).reshape(SLAB * PACKED, LANES)
     right = jnp.asarray(right_table())
     left = jnp.asarray(left_table())
-    kernel = kernel_table()
     visiting = exchanged_slabs(slab)
     pair = gathered(slab, "zl")
     pair, visiting = lax.optimization_barrier((pair, visiting))
     own = gathered(pair, "y").reshape(CUBE)
-    over_zh = gathered(visiting[None], "zh")
-    half = SLAB * PACKED // 2
-    parts = [gathered(over_zh[None, :, at * half : (at + 1) * half], "x") for at in range(2)]
-    first = jnp.stack(parts, axis=2)
-    first = first.transpose(1, 0, 2, 3, 4).reshape(CUBE)
+    blocks = gathered_x(gathered(visiting[None], "zh"))
+    index = jnp.arange(NG, dtype=jnp.int32)
+    own, index, *blocks = lax.optimization_barrier((own, index, *blocks))
+    kernel = kernel_table(index)
+    first = jnp.concatenate(blocks).reshape(CUBE)
     second = lax.ppermute(first, "core", [(0, 1), (1, 0)])
-    terms = pair_terms(own, first, second, kernel, right, left).reshape(NG * PACKED, LANES)
-    both = lax.psum_scatter(terms, "y", scatter_dimension=0, tiled=True)
+    core = lax.axis_index("core")
+    order = jnp.stack([visiting_order(core), visiting_order(1 - core)])
+    terms = pair_terms(order, own, first, second, kernel, right, left)
+    both = lax.psum_scatter(terms.reshape(NG * PACKED, LANES), "y", scatter_dimension=0, tiled=True)
     rows = SLAB * PACKED
     place = lax.axis_index("zl")
     mine = lax.dynamic_slice_in_dim(both, place * rows, rows)

time: 183 us -> 174 us (0.951)
  blocking collectives: 67.5 us -> 22.1 us
  starting transfers between devices: 13.8 us -> 36.5 us
  waiting for transfers between devices: 55.2 us -> 67.7 us
    all_gather x4 -> x2, blocking collectives: 67.5 us -> 22.1 us  [gathered(): return lax.all_gather(block, axis, axis=0, tiled=True)]
    ppermute x0 -> x4, starting transfers between devices: none -> 16.3 us  [shifted(): return lax.ppermute(part, 'x', [(at, (at + by) % 4) for at in range(4)])]
    ppermute x1, starting transfers between devices: 0.67 us -> 10.7 us  [exchanged_slabs(): return lax.ppermute(slab, AXES, pairs)]
    ppermute x0 -> x4, waiting for transfers between devices: none -> 8.57 us  [shifted(): return lax.ppermute(part, 'x', [(at, (at + by) % 4) for at in range(4)])]
    all_gather x1, waiting for transfers between devices: 0.01 us -> 4.1 us  [gathered(): return lax.all_gather(block, axis, axis=0, tiled=True)]
    ppermute x1, starting transfers between devices: 9.87 us -> 6.15 us  [body(): second = lax.ppermute(first, 'core', [(0, 1), (1, 0)])]
  transfers between devices with their start and end apart: 5 -> 9, of which waited for: 2 -> 6; matrix products, arithmetic and copies ran while one was open for 2% -> 3% of each run, Pallas kernels for 0% -> 0%
where the time goes in v4:
time: 174 us; the launch traced here: 173 us
  waiting for transfers between devices  67.7 us (39%)
  starting transfers between devices  36.5 us (21%)
  Pallas kernels  23.9 us (14%)
  blocking collectives  22.1 us (13%)
  between operations  13.7 us (8%)
  other arithmetic  5.72 us (3%)
  local copies, waits for them, and re-layouts  3.5 us (2%)
    reduce_scatter x1, waiting for transfers between devices, body(): lax.psum_scatter(terms.reshape(NG * PACKED, LANES), 'y', scatter_dimensio...  50 us
    pallas_call x1, Pallas kernels, pair_terms(): pl.pallas_call(pairs_kernel, grid_spec=pltpu.PrefetchScalarGridSpec(num_s...  23.9 us
    all_gather x2, blocking collectives, gathered(): return lax.all_gather(block, axis, axis=0, tiled=True)  22.1 us
    ppermute x4, starting transfers between devices, shifted(): return lax.ppermute(part, 'x', [(at, (at + by) % 4) for at in range(4)])  16.3 us
    ppermute x1, starting transfers between devices, exchanged_slabs(): return lax.ppermute(slab, AXES, pairs)  10.7 us
    ppermute x4, waiting for transfers between devices, shifted(): return lax.ppermute(part, 'x', [(at, (at + by) % 4) for at in range(4)])  8.57 us
    ppermute x1, starting transfers between devices, body(): second = lax.ppermute(first, 'core', [(0, 1), (1, 0)])  6.15 us
    ppermute x1, waiting for transfers between devices, body(): total = mine + lax.ppermute(other, 'zl', [(0, 1), (1, 0)])  5 us
  transfers between devices with their start and end apart: 9, of which 6 were waited for; matrix products, arithmetic and copies ran while one was open for 3% of the time, Pallas kernels for 0%

profile of v4, /device:TPU:1, one launch (start us, length us, event | category | flops | bytes accessed | tf_op | source)
XLA Modules:
  0.0 173.2 jit_solution(14575359170043934300)
XLA Ops:
  6.5 1.1 reshape.54
  7.8 10.7 %collective-permute-start = (bf16[432,128]{1,0:T(8,128)(2,1)S(1)}, bf16[432,128]{1,0:T(8,128)(2,1)S(1)}, u32[]{:S(2)}, u32[]{:S(2)}) collective-permute-start(bf16[432,128]{1,0:T(8,128)(2,1)S(1)} %bitcast.18), channel_id=1, source_target_pairs={{0,0},{1,128},{2,256},{3,384},{4,32},{5,160},{6,288},{7,416},{8,64... | collective-permute-start | bytes 331784 | tf_op jit(solution)/shard_map/ppermute | solution.py:253
  18.6 8.7 %all_gather.9 = bf16[864,128]{1,0:T(8,128)(2,1)} all-gather(bf16[432,128]{1,0:T(8,128)(2,1)S(1)} %bitcast.19), channel_id=1, replica_groups=mesh['zh'=4,'x'=4,'core'=2,'y'=8,'zl'=2] {'zl'}, dimensions={0}, use_global_device_ids=true | all-gather | bytes 331776 | tf_op jit(solution)/shard_map/all_gather | solution.py:275
  27.4 13.5 %all-gather = bf16[1728,128]{1,0:T(8,128)(2,1)S(1)} all-gather(bf16[432,128]{1,0:T(8,128)(2,1)S(1)} %collective-permute-done), channel_id=2, replica_groups=mesh['zh'=4,'x'=4,'core'=2,'y'=8,'zl'=2] {'zh'}, dimensions={0}, use_global_device_ids=true | all-gather | bytes 552960 | tf_op jit(solution)/shard_map/all_gather | solution.py:275
  40.8 5.4 %collective-permute-start.1 = (bf16[4,432,128]{2,1,0:T(8,128)(2,1)S(1)}, bf16[4,432,128]{2,1,0:T(8,128)(2,1)S(1)}, u32[]{:S(2)}, u32[]{:S(2)}) collective-permute-start(bf16[4,432,128]{2,1,0:T(8,128)(2,1)S(1)} %bitcast.15), channel_id=1, source_target_pairs={{0,32},{32,64},{64,96},{96,0},{1,33},{33,65},{65,97},{97,1},{2,34}... | collective-permute-start | bytes 1327112 | tf_op jit(solution)/shard_map/ppermute | solution.py:268
  46.3 4.4 %collective-permute-start.2 = (bf16[4,432,128]{2,1,0:T(8,128)(2,1)S(1)}, bf16[4,432,128]{2,1,0:T(8,128)(2,1)S(1)}, u32[]{:S(2)}, u32[]{:S(2)}) collective-permute-start(bf16[4,432,128]{2,1,0:T(8,128)(2,1)S(1)} %bitcast.16), channel_id=1, source_target_pairs={{0,96},{32,0},{64,32},{96,64},{1,97},{33,1},{65,33},{97,65},{2,98}... | collective-permute-start | bytes 1327112 | tf_op jit(solution)/shard_map/ppermute | solution.py:268
  50.7 5.8 %collective-permute-done.1 = bf16[4,432,128]{2,1,0:T(8,128)(2,1)S(1)} collective-permute-done((bf16[4,432,128]{2,1,0:T(8,128)(2,1)S(1)}, bf16[4,432,128]{2,1,0:T(8,128)(2,1)S(1)}, u32[]{:S(2)}, u32[]{:S(2)}) %collective-permute-start.1) | collective-permute-done | bytes 442400 | tf_op jit(solution)/shard_map/ppermute | solution.py:268
  56.5 1.9 %collective-permute-start.3 = (bf16[2,432,128]{2,1,0:T(8,128)(2,1)S(1)}, bf16[2,432,128]{2,1,0:T(8,128)(2,1)S(1)}, u32[]{:S(2)}, u32[]{:S(2)}) collective-permute-start(bf16[2,432,128]{2,1,0:T(8,128)(2,1)S(1)} %slice.52), channel_id=1, source_target_pairs={{0,32},{32,64},{64,96},{96,0},{1,33},{33,65},{65,97},{97,1},{2,34}... | collective-permute-start | bytes 663560 | tf_op jit(solution)/shard_map/ppermute | solution.py:268
  58.4 4.6 %collective-permute-start.4 = (bf16[2,432,128]{2,1,0:T(8,128)(2,1)S(1)}, bf16[2,432,128]{2,1,0:T(8,128)(2,1)S(1)}, u32[]{:S(2)}, u32[]{:S(2)}) collective-permute-start(bf16[2,432,128]{2,1,0:T(8,128)(2,1)S(1)} %slice.53), channel_id=1, source_target_pairs={{0,96},{32,0},{64,32},{96,64},{1,97},{33,1},{65,33},{97,65},{2,98}... | collective-permute-start | bytes 663560 | tf_op jit(solution)/shard_map/ppermute | solution.py:268
  63.1 1.6 collective-permute-done.3
  64.7 1.2 collective-permute-done.4
  65.9 4.1 %all-gather.3.cloned.1.call-done = bf16[6912,128]{1,0:T(8,128)(2,1)} async-done(((bf16[864,128]{1,0:T(8,128)(2,1)}), bf16[6912,128]{1,0:T(8,128)(2,1)}) %all-gather.3.cloned.1.call-update) | async-done | bytes 1769488 | tf_op jit(solution)/shard_map/all_gather | solution.py:275
  70.2 6.1 %collective-permute-start.5 = (bf16[96,72,128]{2,1,0:T(8,128)(2,1)S(1)}, bf16[96,72,128]{2,1,0:T(8,128)(2,1)}, u32[]{:S(2)}, u32[]{:S(2)}) collective-permute-start(bf16[96,72,128]{2,1,0:T(8,128)(2,1)S(1)} %bitcast.20), channel_id=1, source_target_pairs={{0,16},{16,0},{1,17},{17,1},{2,18},{18,2},{3,19},{19,3},{4,20},{20... | collective-permute-start | bytes 5308424 | tf_op jit(solution)/shard_map/ppermute | solution.py:291
  76.6 0.6 pad_add_fusion.order_ref
  77.2 3.7 %fusion.3.refs_2_ = f32[96,96,128]{2,1,0:T(8,128)} fusion(f32[128]{0:T(128)S(1)} %pad_multiply_fusion, f32[96,96]{1,0:T(8,128)S(1)} %broadcast_add_fusion), kind=kLoop, calls=%fused_computation.5 | loop fusion | flops 11796480 | bytes 4755968 | tf_op jit(solution)/shard_map/mul | solution.py:67
  80.9 23.9 %pair_terms.1 = f32[96,72,128]{2,1,0:T(8,128)} custom-call(s32[2,5]{1,0:T(2,128)} %pad_add_fusion.order_ref, bf16[96,72,128]{2,1,0:T(8,128)(2,1)} %bitcast.22, bf16[96,72,128]{2,1,0:T(8,128)(2,1)} %bitcast.21, bf16[96,72,128]{2,1,0:T(8,128)(2,1)} %collective-permute-done.5.refs_1_, f32[96,96,128]{2,1,0:T(8,128)} %fusion.3.refs_2_, ...), custom_call_target="tpu_custom_call" | custom-call | flops 14495514624 | bytes 17000000 | tf_op jit(solution)/shard_map/pair_terms/pallas_call | solution.py:210
  104.9 50.0 %reduce-scatter.2.cloned.1.call-done = f32[864,128]{1,0:T(8,128)} async-done(((f32[6912,128]{1,0:T(8,128)}), f32[864,128]{1,0:T(8,128)}) %reduce-scatter.2.cloned.1.call-update) | async-done | bytes 442384 | tf_op jit(solution)/shard_map/reduce_scatter | solution.py:295
  154.9 0.9 constant_dynamic-slice_fusion
  155.9 3.3 %collective-permute-start.6 = (f32[432,128]{1,0:T(8,128)S(1)}, f32[432,128]{1,0:T(8,128)S(1)}, u32[]{:S(2)}, u32[]{:S(2)}) collective-permute-start(f32[432,128]{1,0:T(8,128)S(1)} %constant_dynamic-slice_fusion), channel_id=1, source_target_pairs={{0,1},{1,0},{2,3},{3,2},{4,5},{5,4},{6,7},{7,6},{8,9},{9,8},{10,11... | collective-permute-start | bytes 663560 | tf_op jit(solution)/shard_map/ppermute | solution.py:300
  159.1 5.0 %collective-permute-done.6 = f32[432,128]{1,0:T(8,128)S(1)} collective-permute-done((f32[432,128]{1,0:T(8,128)S(1)}, f32[432,128]{1,0:T(8,128)S(1)}, u32[]{:S(2)}, u32[]{:S(2)}) %collective-permute-start.6) | collective-permute-done | bytes 221216 | tf_op jit(solution)/shard_map/ppermute | solution.py:300
  164.1 1.0 dynamic-slice_add_fusion
  165.1 0.1 fusion.11
  165.2 0.1 maximum_maximum_fusion
  165.3 1.0 reshape.60
  (26 shorter events, 0.8 us)
Async XLA Ops:
  6.5 63.4 %all-gather.3.cloned.1.call-start = ((), (), s32[]{:S(2)}) async-start(), calls=%async_computation.1 | async-start | bytes 1990656 | tf_op jit(solution)/shard_map/all_gather | solution.py:275
  7.8 19.4 %collective-permute-start = (bf16[432,128]{1,0:T(8,128)(2,1)S(1)}, bf16[432,128]{1,0:T(8,128)(2,1)S(1)}, u32[]{:S(2)}, u32[]{:S(2)}) collective-permute-start(bf16[432,128]{1,0:T(8,128)(2,1)S(1)} %bitcast.18), channel_id=1, source_target_pairs={{0,0},{1,128},{2,256},{3,384},{4,32},{5,160},{6,288},{7,416},{8,64... | collective-permute-start | bytes 331784 | tf_op jit(solution)/shard_map/ppermute | solution.py:253
  27.3 127.6 %reduce-scatter.2.cloned.1.call-start = ((), (), s32[]{:S(2)}) async-start(), calls=%async_computation.2 | async-start | bytes 3981312 | tf_op jit(solution)/shard_map/reduce_scatter | solution.py:295
  40.8 15.6 %collective-permute-start.1 = (bf16[4,432,128]{2,1,0:T(8,128)(2,1)S(1)}, bf16[4,432,128]{2,1,0:T(8,128)(2,1)S(1)}, u32[]{:S(2)}, u32[]{:S(2)}) collective-permute-start(bf16[4,432,128]{2,1,0:T(8,128)(2,1)S(1)} %bitcast.15), channel_id=1, source_target_pairs={{0,32},{32,64},{64,96},{96,0},{1,33},{33,65},{65,97},{97,1},{2,34}... | collective-permute-start | bytes 1327112 | tf_op jit(solution)/shard_map/ppermute | solution.py:268
  46.3 12.1 %collective-permute-start.2 = (bf16[4,432,128]{2,1,0:T(8,128)(2,1)S(1)}, bf16[4,432,128]{2,1,0:T(8,128)(2,1)S(1)}, u32[]{:S(2)}, u32[]{:S(2)}) collective-permute-start(bf16[4,432,128]{2,1,0:T(8,128)(2,1)S(1)} %bitcast.16), channel_id=1, source_target_pairs={{0,96},{32,0},{64,32},{96,64},{1,97},{33,1},{65,33},{97,65},{2,98}... | collective-permute-start | bytes 1327112 | tf_op jit(solution)/shard_map/ppermute | solution.py:268
  56.5 8.2 %collective-permute-start.3 = (bf16[2,432,128]{2,1,0:T(8,128)(2,1)S(1)}, bf16[2,432,128]{2,1,0:T(8,128)(2,1)S(1)}, u32[]{:S(2)}, u32[]{:S(2)}) collective-permute-start(bf16[2,432,128]{2,1,0:T(8,128)(2,1)S(1)} %slice.52), channel_id=1, source_target_pairs={{0,32},{32,64},{64,96},{96,0},{1,33},{33,65},{65,97},{97,1},{2,34}... | collective-permute-start | bytes 663560 | tf_op jit(solution)/shard_map/ppermute | solution.py:268
  58.4 7.4 %collective-permute-start.4 = (bf16[2,432,128]{2,1,0:T(8,128)(2,1)S(1)}, bf16[2,432,128]{2,1,0:T(8,128)(2,1)S(1)}, u32[]{:S(2)}, u32[]{:S(2)}) collective-permute-start(bf16[2,432,128]{2,1,0:T(8,128)(2,1)S(1)} %slice.53), channel_id=1, source_target_pairs={{0,96},{32,0},{64,32},{96,64},{1,97},{33,1},{65,33},{97,65},{2,98}... | collective-permute-start | bytes 663560 | tf_op jit(solution)/shard_map/ppermute | solution.py:268
  70.2 10.7 %copy-start = (bf16[16,432,128]{2,1,0:T(8,128)(2,1)}, bf16[16,432,128]{2,1,0:T(8,128)(2,1)S(1)}, u32[]{:S(2)}) copy-start(bf16[16,432,128]{2,1,0:T(8,128)(2,1)S(1)} %constant_dynamic-update-slice_fusion) | copy-start | bytes 5308420
  70.2 10.7 %collective-permute-start.5 = (bf16[96,72,128]{2,1,0:T(8,128)(2,1)S(1)}, bf16[96,72,128]{2,1,0:T(8,128)(2,1)}, u32[]{:S(2)}, u32[]{:S(2)}) collective-permute-start(bf16[96,72,128]{2,1,0:T(8,128)(2,1)S(1)} %bitcast.20), channel_id=1, source_target_pairs={{0,16},{16,0},{1,17},{17,1},{2,18},{18,2},{3,19},{19,3},{4,20},{20... | collective-permute-start | bytes 5308424 | tf_op jit(solution)/shard_map/ppermute | solution.py:291
  155.9 8.3 %collective-permute-start.6 = (f32[432,128]{1,0:T(8,128)S(1)}, f32[432,128]{1,0:T(8,128)S(1)}, u32[]{:S(2)}, u32[]{:S(2)}) collective-permute-start(f32[432,128]{1,0:T(8,128)S(1)} %constant_dynamic-slice_fusion), channel_id=1, source_target_pairs={{0,1},{1,0},{2,3},{3,2},{4,5},{5,4},{6,7},{7,6},{8,9},{9,8},{10,11... | collective-permute-start | bytes 663560 | tf_op jit(solution)/shard_map/ppermute | solution.py:300
Sparse Core Ops, SparseCore 0:
  27.4 42.4 all-gather.2
  105.0 49.8 reduce-scatter.1

commit v5 on v4

--- a/solution.py
+++ b/solution.py
@@ -26,6 +26,8 @@
 BATCH = 24
 SLABS = BATCH // SLAB
 VMEM_MIB = 58
+NEAR = 4
+FAR = SLAB - NEAR
 PITCH = NG + 8
 UNROLL = 1
 
@@ -60,7 +62,7 @@
     wave = signed * (2.0 * math.pi / (NG * SPACING))
     wave_z = jnp.pad(wave, (0, LANES - NG))
     square = (
-        (wave * wave)[:, None, None] + (wave * wave)[None, :, None] + (wave_z * wave_z)[None, None, :]
+        (wave * wave)[: NG // 2 + 1, None, None] + (wave * wave)[None, :, None] + (wave_z * wave_z)[None, None, :]
     )
     safe = jnp.where(square > 0, square, 1.0)
     values = 4.0 * math.pi * (1.0 - jnp.exp(-safe / (4.0 * SCREENING * SCREENING))) / safe
@@ -147,7 +149,8 @@
 
 
 def pairs_kernel(order_ref, own_ref, *refs):
-    *visitor_refs, kernel_ref, right_ref, left_ref, out_ref, field = refs
+    *visitor_refs, right_ref, left_ref, kernel_ref, near_ref, far_ref, field, weights, arrived = refs
+    weights_copy = pltpu.make_async_copy(kernel_ref, weights, arrived)
     step = pl.program_id(0)
     steps = NG // BATCH
     right = right_ref[...]
@@ -156,6 +159,14 @@
     def visitor(pair, plane):
         slab = lax.rem(plane // SLAB + order_ref[pair, steps], SLABS)
         return visitor_refs[pair][slab * SLAB + plane % SLAB].astype(F32)
+
+    @pl.when(step == 0)
+    def fetch():
+        weights_copy.start()
+
+    @pl.when(step == steps)
+    def fetched():
+        weights_copy.wait()
 
     @pl.when(step < steps)
     def forward():
@@ -173,7 +184,8 @@
         first = (step - steps) * BATCH
         lines = [line(at % 2, first + at // 2) for at in range(2 * BATCH)]
         columns = left_transform(left, side_by_side([field[at, :] for at in lines]))
-        columns = columns * side_by_side([kernel_ref[at // 2] for at in range(2 * BATCH)])
+        rows = [jnp.minimum(first + at, NG - first - at) for at in range(BATCH)]
+        columns = columns * side_by_side([weights[rows[at // 2]] for at in range(2 * BATCH)])
         columns = left_transform(left, columns)
         for at, tile in zip(lines, lane_tiles(columns), strict=True):
             field[at, :] = tile
@@ -186,7 +198,11 @@
         tiles = row_tiles(right_transform(stacked(lane_tiles(columns)), right))
         for at in range(BATCH):
             terms = [pack_plane(tiles[2 * at + pair]) * visitor(pair, at) for pair in range(2)]
-            out_ref[at] = terms[0] + terms[1]
+            slab, plane = divmod(at, SLAB)
+            if plane < NEAR:
+                near_ref[slab * NEAR + plane] = terms[0] + terms[1]
+            else:
+                far_ref[slab * FAR + plane - NEAR] = terms[0] + terms[1]
 
 
 CUBE = (NG, PACKED, LANES)
@@ -216,20 +232,28 @@
                 planes(BATCH, lambda i, order: clipped(i, 0)),
                 visitor(0),
                 visitor(1),
-                pl.BlockSpec((BATCH, NG, LANES), lambda i, order: (clipped(i, steps), 0, 0)),
                 pl.BlockSpec((2 * LANES, 2 * LANES), lambda i, order: (0, 0)),
                 pl.BlockSpec((2 * NG, 2 * NG), lambda i, order: (0, 0)),
+                pl.BlockSpec(memory_space=pl.ANY),
             ],
-            out_specs=planes(BATCH, lambda i, order: clipped(i, 2 * steps)),
-            scratch_shapes=[pltpu.VMEM((2 * NG * PITCH, LANES), F32)],
+            out_specs=[
+                planes(count * SLABS, lambda i, order: clipped(i, 2 * steps)) for count in (NEAR, FAR)
+            ],
+            scratch_shapes=[
+                pltpu.VMEM((2 * NG * PITCH, LANES), F32),
+                pltpu.VMEM((NG // 2 + 1, NG, LANES), F32),
+                pltpu.SemaphoreType.DMA,
+            ],
         ),
-        out_shape=jax.ShapeDtypeStruct(CUBE, F32),
+        out_shape=[
+            jax.ShapeDtypeStruct((NG // SLAB * count, PACKED, LANES), F32) for count in (NEAR, FAR)
+        ],
         compiler_params=pltpu.CompilerParams(vmem_limit_bytes=VMEM_MIB * 1024 * 1024),
         cost_estimate=pl.CostEstimate(
             flops=4 * 6 * NG * NG * 256 * 256, bytes_accessed=17_000_000, transcendentals=0
         ),
         name="pair_terms",
-    )(order, own, first, second, kernel, right, left)
+    )(order, own, first, second, right, left, kernel)
 
 
 def meeting_place(zh, x, core):
@@ -273,6 +297,17 @@
 
 def gathered(block, axis):
     return lax.all_gather(block, axis, axis=0, tiled=True)
+
+
+def scattered(terms):
+    return lax.psum_scatter(terms, "y", scatter_dimension=0, tiled=True)
+
+
+def both_places(slabs):
+    place = lax.axis_index("zl")
+    mine = lax.dynamic_index_in_dim(slabs, place, keepdims=False)
+    other = lax.dynamic_index_in_dim(slabs, 1 - place, keepdims=False)
+    return mine + lax.ppermute(other, "zl", [(0, 1), (1, 0)])
 
 
 def body(orbitals):
@@ -291,14 +326,11 @@
     second = lax.ppermute(first, "core", [(0, 1), (1, 0)])
     core = lax.axis_index("core")
     order = jnp.stack([visiting_order(core), visiting_order(1 - core)])
-    terms = pair_terms(order, own, first, second, kernel, right, left)
-    both = lax.psum_scatter(terms.reshape(NG * PACKED, LANES), "y", scatter_dimension=0, tiled=True)
-    rows = SLAB * PACKED
-    place = lax.axis_index("zl")
-    mine = lax.dynamic_slice_in_dim(both, place * rows, rows)
-    other = lax.dynamic_slice_in_dim(both, (1 - place) * rows, rows)
-    total = mine + lax.ppermute(other, "zl", [(0, 1), (1, 0)])
-    return unpack(total.reshape(SLAB, PACKED, LANES)).reshape(orbitals.shape)
+    near, far = pair_terms(order, own, first, second, kernel, right, left)
+    near = scattered(near.reshape(-1, LANES)).reshape(2, NEAR, PACKED, LANES)
+    far = scattered(far.reshape(-1, 8 * LANES)).reshape(2, FAR, PACKED, LANES)
+    total = jnp.concatenate([both_places(near), both_places(far)])
+    return unpack(total).reshape(orbitals.shape)
 
 
 def solution(mesh):

time: 174 us -> 170 us (0.977)
  waiting for transfers between devices: 67.7 us -> 26 us
  blocking collectives: 22.1 us -> 48.1 us
  starting transfers between devices: 36.5 us -> 45 us
  local copies, waits for them, and re-layouts: 3.5 us -> 7.55 us
    reduce_scatter x1, waiting for transfers between devices: 50 us -> 8.36 us  [scattered(): return lax.psum_scatter(terms, 'y', scatter_dimension=0, tiled=True)]
    unnamed x0 -> x1, blocking collectives: none -> 26 us
    ppermute x1 -> x2, starting transfers between devices: 3.26 us -> 8.5 us  [both_places(): return mine + lax.ppermute(other, 'zl', [(0, 1), (1, 0)])]
    unnamed x6 -> x14, local copies, waits for them, and re-layouts: 0.18 us -> 4.16 us
    unnamed x0 -> x1, starting transfers between devices: none -> 3.25 us
    ppermute x1 -> x2, waiting for transfers between devices: 5 us -> 2.49 us  [both_places(): return mine + lax.ppermute(other, 'zl', [(0, 1), (1, 0)])]
    unnamed x2 -> x3, waiting for transfers between devices: 0.03 us -> 2.26 us
  transfers between devices with their start and end apart: 9 -> 11, of which waited for: 6 -> 8; matrix products, arithmetic and copies ran while one was open for 3% -> 19% of each run, Pallas kernels for 0% -> 0%
where the time goes in v5:
time: 170 us; the launch traced here: 169 us
  blocking collectives  48.1 us (28%)
  starting transfers between devices  45 us (26%)
  waiting for transfers between devices  26 us (15%)
  Pallas kernels  23.4 us (14%)
  between operations  14.4 us (8%)
  local copies, waits for them, and re-layouts  7.55 us (4%)
  other arithmetic  4.37 us (3%)
    unnamed x1, blocking collectives  26 us
    pallas_call x1, Pallas kernels, pair_terms(): pl.pallas_call(pairs_kernel, grid_spec=pltpu.PrefetchScalarGridSpec(num_s...  23.4 us
    all_gather x2, blocking collectives, gathered(): return lax.all_gather(block, axis, axis=0, tiled=True)  22.1 us
    ppermute x4, starting transfers between devices, shifted(): return lax.ppermute(part, 'x', [(at, (at + by) % 4) for at in range(4)])  16.3 us
    ppermute x1, starting transfers between devices, exchanged_slabs(): return lax.ppermute(slab, AXES, pairs)  10.7 us
    ppermute x4, waiting for transfers between devices, shifted(): return lax.ppermute(part, 'x', [(at, (at + by) % 4) for at in range(4)])  8.63 us
    ppermute x2, starting transfers between devices, both_places(): return mine + lax.ppermute(other, 'zl', [(0, 1), (1, 0)])  8.5 us
    reduce_scatter x1, waiting for transfers between devices, scattered(): return lax.psum_scatter(terms, 'y', scatter_dimension=0, tiled=True)  8.36 us
  transfers between devices with their start and end apart: 11, of which 8 were waited for; matrix products, arithmetic and copies ran while one was open for 19% of the time, Pallas kernels for 0%

profile of v5, /device:TPU:1, one launch (start us, length us, event | category | flops | bytes accessed | tf_op | source)
XLA Modules:
  0.0 168.8 jit_solution(7175591233295952278)
XLA Ops:
  7.8 10.7 %collective-permute-start = (bf16[432,128]{1,0:T(8,128)(2,1)S(1)}, bf16[432,128]{1,0:T(8,128)(2,1)S(1)}, u32[]{:S(2)}, u32[]{:S(2)}) collective-permute-start(bf16[432,128]{1,0:T(8,128)(2,1)S(1)} %bitcast.27), channel_id=1, source_target_pairs={{0,0},{1,128},{2,256},{3,384},{4,32},{5,160},{6,288},{7,416},{8,64... | collective-permute-start | bytes 331784 | tf_op jit(solution)/shard_map/ppermute | solution.py:277
  18.6 8.7 %all_gather.9 = bf16[864,128]{1,0:T(8,128)(2,1)} all-gather(bf16[432,128]{1,0:T(8,128)(2,1)S(1)} %bitcast.28), channel_id=1, replica_groups=mesh['zh'=4,'x'=4,'core'=2,'y'=8,'zl'=2] {'zl'}, dimensions={0}, use_global_device_ids=true | all-gather | bytes 331776 | tf_op jit(solution)/shard_map/all_gather | solution.py:299
  27.4 13.5 %all-gather = bf16[1728,128]{1,0:T(8,128)(2,1)S(1)} all-gather(bf16[432,128]{1,0:T(8,128)(2,1)S(1)} %collective-permute-done), channel_id=2, replica_groups=mesh['zh'=4,'x'=4,'core'=2,'y'=8,'zl'=2] {'zh'}, dimensions={0}, use_global_device_ids=true | all-gather | bytes 552960 | tf_op jit(solution)/shard_map/all_gather | solution.py:299
  40.8 5.4 %collective-permute-start.1 = (bf16[4,432,128]{2,1,0:T(8,128)(2,1)S(1)}, bf16[4,432,128]{2,1,0:T(8,128)(2,1)S(1)}, u32[]{:S(2)}, u32[]{:S(2)}) collective-permute-start(bf16[4,432,128]{2,1,0:T(8,128)(2,1)S(1)} %bitcast.24), channel_id=1, source_target_pairs={{0,32},{32,64},{64,96},{96,0},{1,33},{33,65},{65,97},{97,1},{2,34}... | collective-permute-start | bytes 1327112 | tf_op jit(solution)/shard_map/ppermute | solution.py:292
  46.3 4.4 %collective-permute-start.2 = (bf16[4,432,128]{2,1,0:T(8,128)(2,1)S(1)}, bf16[4,432,128]{2,1,0:T(8,128)(2,1)S(1)}, u32[]{:S(2)}, u32[]{:S(2)}) collective-permute-start(bf16[4,432,128]{2,1,0:T(8,128)(2,1)S(1)} %bitcast.25), channel_id=1, source_target_pairs={{0,96},{32,0},{64,32},{96,64},{1,97},{33,1},{65,33},{97,65},{2,98}... | collective-permute-start | bytes 1327112 | tf_op jit(solution)/shard_map/ppermute | solution.py:292
  50.7 5.8 %collective-permute-done.1 = bf16[4,432,128]{2,1,0:T(8,128)(2,1)S(1)} collective-permute-done((bf16[4,432,128]{2,1,0:T(8,128)(2,1)S(1)}, bf16[4,432,128]{2,1,0:T(8,128)(2,1)S(1)}, u32[]{:S(2)}, u32[]{:S(2)}) %collective-permute-start.1) | collective-permute-done | bytes 442400 | tf_op jit(solution)/shard_map/ppermute | solution.py:292
  56.5 1.9 %collective-permute-start.3 = (bf16[2,432,128]{2,1,0:T(8,128)(2,1)S(1)}, bf16[2,432,128]{2,1,0:T(8,128)(2,1)S(1)}, u32[]{:S(2)}, u32[]{:S(2)}) collective-permute-start(bf16[2,432,128]{2,1,0:T(8,128)(2,1)S(1)} %slice.56), channel_id=1, source_target_pairs={{0,32},{32,64},{64,96},{96,0},{1,33},{33,65},{65,97},{97,1},{2,34}... | collective-permute-start | bytes 663560 | tf_op jit(solution)/shard_map/ppermute | solution.py:292
  58.4 4.6 %collective-permute-start.4 = (bf16[2,432,128]{2,1,0:T(8,128)(2,1)S(1)}, bf16[2,432,128]{2,1,0:T(8,128)(2,1)S(1)}, u32[]{:S(2)}, u32[]{:S(2)}) collective-permute-start(bf16[2,432,128]{2,1,0:T(8,128)(2,1)S(1)} %slice.57), channel_id=1, source_target_pairs={{0,96},{32,0},{64,32},{96,64},{1,97},{33,1},{65,33},{97,65},{2,98}... | collective-permute-start | bytes 663560 | tf_op jit(solution)/shard_map/ppermute | solution.py:292
  63.0 1.7 %collective-permute-done.3 = bf16[2,432,128]{2,1,0:T(8,128)(2,1)S(1)} collective-permute-done((bf16[2,432,128]{2,1,0:T(8,128)(2,1)S(1)}, bf16[2,432,128]{2,1,0:T(8,128)(2,1)S(1)}, u32[]{:S(2)}, u32[]{:S(2)}) %collective-permute-start.3) | collective-permute-done | bytes 221216 | tf_op jit(solution)/shard_map/ppermute | solution.py:292
  64.7 1.2 collective-permute-done.4
  65.9 4.1 %all-gather.3.cloned.1.call-done = bf16[6912,128]{1,0:T(8,128)(2,1)} async-done(((bf16[864,128]{1,0:T(8,128)(2,1)}), bf16[6912,128]{1,0:T(8,128)(2,1)}) %all-gather.3.cloned.1.call-update) | async-done | bytes 1769488 | tf_op jit(solution)/shard_map/all_gather | solution.py:299
  70.2 6.1 %collective-permute-start.5 = (bf16[96,72,128]{2,1,0:T(8,128)(2,1)S(1)}, bf16[96,72,128]{2,1,0:T(8,128)(2,1)S(1)}, u32[]{:S(2)}, u32[]{:S(2)}) collective-permute-start(bf16[96,72,128]{2,1,0:T(8,128)(2,1)S(1)} %bitcast.31), channel_id=1, source_target_pairs={{0,16},{16,0},{1,17},{17,1},{2,18},{18,2},{3,19},{19,3},{4,20},{20... | collective-permute-start | bytes 5308424 | tf_op jit(solution)/shard_map/ppermute | solution.py:326
  77.3 2.3 %fusion.4.refs_4_ = f32[49,96,128]{2,1,0:T(8,128)} fusion(f32[128]{0:T(128)S(1)} %pad_multiply_fusion, f32[49,96]{1,0:T(8,128)S(1)} %broadcast_add_fusion), kind=kLoop, calls=%fused_computation.5 | loop fusion | flops 6021120 | bytes 2427776 | tf_op jit(solution)/shard_map/mul | solution.py:69
  79.7 1.3 copy-done.2
  80.9 23.4 %pair_terms.1 = (f32[64,72,128]{2,1,0:T(8,128)}, f32[32,72,128]{2,1,0:T(8,128)}) custom-call(s32[2,5]{1,0:T(2,128)} %pad_add_fusion.order_ref, bf16[96,72,128]{2,1,0:T(8,128)(2,1)} %bitcast.34, bf16[96,72,128]{2,1,0:T(8,128)(2,1)} %bitcast.32, bf16[96,72,128]{2,1,0:T(8,128)(2,1)} %copy-done.2, bf16[256,256]{1,0:T(8,128)(2,1)} %constant.126.clone.refs_2_, ...), custom_call_target="tpu_custom_call" | custom-call | flops 14495514624 | bytes 17000000 | tf_op jit(solution)/shard_map/pair_terms/pallas_call | solution.py:226
  104.4 1.2 copy-done
  105.8 26.0 %fusion = f32[40,1024]{1,0:T(8,128)S(1)} fusion(f32[288,1024]{1,0:T(8,128)S(1)} %reshape.66), kind=kCustom, calls=%all-reduce-scatter | all-reduce-scatter fusion | flops 327681 | bytes 1345536
  131.8 3.2 %collective-permute-start.8 = (f32[28,1024]{1,0:T(8,128)S(1)}, f32[28,1024]{1,0:T(8,128)S(1)}, u32[]{:S(2)}, u32[]{:S(2)}) collective-permute-start(f32[28,1024]{1,0:T(8,128)S(1)} %slice.64), channel_id=1, source_target_pairs={{0,2},{2,4},{4,6},{6,8},{8,10},{10,12},{12,14},{1,3},{3,5},{5,7},{... | collective-permute-start | bytes 344072
  135.0 1.3 dynamic-slice.4
  137.0 2.2 %collective-permute-done.8 = f32[28,1024]{1,0:T(8,128)S(1)} collective-permute-done((f32[28,1024]{1,0:T(8,128)S(1)}, f32[28,1024]{1,0:T(8,128)S(1)}, u32[]{:S(2)}, u32[]{:S(2)}) %collective-permute-start.8) | collective-permute-done | bytes 114720
  139.5 4.3 %collective-permute-start.7 = (f32[2,72,128]{2,1,0:T(8,128)S(1)}, f32[2,72,128]{2,1,0:T(8,128)S(1)}, u32[]{:S(2)}, u32[]{:S(2)}) collective-permute-start(f32[2,72,128]{2,1,0:T(8,128)S(1)} %dynamic-slice_bitcast_fusion.1), channel_id=1, source_target_pairs={{0,1},{1,0},{2,3},{3,2},{4,5},{5,4},{6,7},{7,6},{8,9},{9,8},{10,11... | collective-permute-start | bytes 221192 | tf_op jit(solution)/shard_map/ppermute | solution.py:310
  143.7 8.4 %reduce-scatter.4.cloned.1.call-done = f32[576,128]{1,0:T(8,128)} async-done(((f32[4608,128]{1,0:T(8,128)}), f32[576,128]{1,0:T(8,128)}) %reduce-scatter.4.cloned.1.call-update) | async-done | bytes 294928 | tf_op jit(solution)/shard_map/reduce_scatter | solution.py:303
  153.0 4.2 %collective-permute-start.6 = (f32[4,72,128]{2,1,0:T(8,128)S(1)}, f32[4,72,128]{2,1,0:T(8,128)S(1)}, u32[]{:S(2)}, u32[]{:S(2)}) collective-permute-start(f32[4,72,128]{2,1,0:T(8,128)S(1)} %dynamic-slice_bitcast_fusion), channel_id=1, source_target_pairs={{0,1},{1,0},{2,3},{3,2},{4,5},{5,4},{6,7},{7,6},{8,9},{9,8},{10,11... | collective-permute-start | bytes 442376 | tf_op jit(solution)/shard_map/ppermute | solution.py:310
  157.3 2.5 %collective-permute-done.6 = f32[4,72,128]{2,1,0:T(8,128)S(1)} collective-permute-done((f32[4,72,128]{2,1,0:T(8,128)S(1)}, f32[4,72,128]{2,1,0:T(8,128)S(1)}, u32[]{:S(2)}, u32[]{:S(2)}) %collective-permute-start.6) | collective-permute-done | bytes 147488 | tf_op jit(solution)/shard_map/ppermute | solution.py:310
  (44 shorter events, 6.1 us)
Async XLA Ops:
  6.5 63.4 %all-gather.3.cloned.1.call-start = ((), (), s32[]{:S(2)}) async-start(), calls=%async_computation.1 | async-start | bytes 1990656 | tf_op jit(solution)/shard_map/all_gather | solution.py:299
  7.8 19.4 %collective-permute-start = (bf16[432,128]{1,0:T(8,128)(2,1)S(1)}, bf16[432,128]{1,0:T(8,128)(2,1)S(1)}, u32[]{:S(2)}, u32[]{:S(2)}) collective-permute-start(bf16[432,128]{1,0:T(8,128)(2,1)S(1)} %bitcast.27), channel_id=1, source_target_pairs={{0,0},{1,128},{2,256},{3,384},{4,32},{5,160},{6,288},{7,416},{8,64... | collective-permute-start | bytes 331784 | tf_op jit(solution)/shard_map/ppermute | solution.py:277
  27.3 124.8 %reduce-scatter.4.cloned.1.call-start = ((), (), s32[]{:S(2)}) async-start(), calls=%async_computation.2 | async-start | bytes 2654208 | tf_op jit(solution)/shard_map/reduce_scatter | solution.py:303
  40.8 15.6 %collective-permute-start.1 = (bf16[4,432,128]{2,1,0:T(8,128)(2,1)S(1)}, bf16[4,432,128]{2,1,0:T(8,128)(2,1)S(1)}, u32[]{:S(2)}, u32[]{:S(2)}) collective-permute-start(bf16[4,432,128]{2,1,0:T(8,128)(2,1)S(1)} %bitcast.24), channel_id=1, source_target_pairs={{0,32},{32,64},{64,96},{96,0},{1,33},{33,65},{65,97},{97,1},{2,34}... | collective-permute-start | bytes 1327112 | tf_op jit(solution)/shard_map/ppermute | solution.py:292
  46.3 12.1 %collective-permute-start.2 = (bf16[4,432,128]{2,1,0:T(8,128)(2,1)S(1)}, bf16[4,432,128]{2,1,0:T(8,128)(2,1)S(1)}, u32[]{:S(2)}, u32[]{:S(2)}) collective-permute-start(bf16[4,432,128]{2,1,0:T(8,128)(2,1)S(1)} %bitcast.25), channel_id=1, source_target_pairs={{0,96},{32,0},{64,32},{96,64},{1,97},{33,1},{65,33},{97,65},{2,98}... | collective-permute-start | bytes 1327112 | tf_op jit(solution)/shard_map/ppermute | solution.py:292
  56.5 8.2 %collective-permute-start.3 = (bf16[2,432,128]{2,1,0:T(8,128)(2,1)S(1)}, bf16[2,432,128]{2,1,0:T(8,128)(2,1)S(1)}, u32[]{:S(2)}, u32[]{:S(2)}) collective-permute-start(bf16[2,432,128]{2,1,0:T(8,128)(2,1)S(1)} %slice.56), channel_id=1, source_target_pairs={{0,32},{32,64},{64,96},{96,0},{1,33},{33,65},{65,97},{97,1},{2,34}... | collective-permute-start | bytes 663560 | tf_op jit(solution)/shard_map/ppermute | solution.py:292
  58.4 7.4 %collective-permute-start.4 = (bf16[2,432,128]{2,1,0:T(8,128)(2,1)S(1)}, bf16[2,432,128]{2,1,0:T(8,128)(2,1)S(1)}, u32[]{:S(2)}, u32[]{:S(2)}) collective-permute-start(bf16[2,432,128]{2,1,0:T(8,128)(2,1)S(1)} %slice.57), channel_id=1, source_target_pairs={{0,96},{32,0},{64,32},{96,64},{1,97},{33,1},{65,33},{97,65},{2,98}... | collective-permute-start | bytes 663560 | tf_op jit(solution)/shard_map/ppermute | solution.py:292
  70.2 9.5 %copy-start.1 = (bf16[16,432,128]{2,1,0:T(8,128)(2,1)}, bf16[16,432,128]{2,1,0:T(8,128)(2,1)S(1)}, u32[]{:S(2)}) copy-start(bf16[16,432,128]{2,1,0:T(8,128)(2,1)S(1)} %constant_dynamic-update-slice_fusion) | copy-start | bytes 5308420
  70.2 9.5 %collective-permute-start.5 = (bf16[96,72,128]{2,1,0:T(8,128)(2,1)S(1)}, bf16[96,72,128]{2,1,0:T(8,128)(2,1)S(1)}, u32[]{:S(2)}, u32[]{:S(2)}) collective-permute-start(bf16[96,72,128]{2,1,0:T(8,128)(2,1)S(1)} %bitcast.31), channel_id=1, source_target_pairs={{0,16},{16,0},{1,17},{17,1},{2,18},{18,2},{3,19},{19,3},{4,20},{20... | collective-permute-start | bytes 5308424 | tf_op jit(solution)/shard_map/ppermute | solution.py:326
  79.7 1.3 copy-start.2
  104.3 1.3 copy-start
  131.8 7.4 %collective-permute-start.8 = (f32[28,1024]{1,0:T(8,128)S(1)}, f32[28,1024]{1,0:T(8,128)S(1)}, u32[]{:S(2)}, u32[]{:S(2)}) collective-permute-start(f32[28,1024]{1,0:T(8,128)S(1)} %slice.64), channel_id=1, source_target_pairs={{0,2},{2,4},{4,6},{6,8},{8,10},{10,12},{12,14},{1,3},{3,5},{5,7},{... | collective-permute-start | bytes 344072
  139.5 17.8 %collective-permute-start.7 = (f32[2,72,128]{2,1,0:T(8,128)S(1)}, f32[2,72,128]{2,1,0:T(8,128)S(1)}, u32[]{:S(2)}, u32[]{:S(2)}) collective-permute-start(f32[2,72,128]{2,1,0:T(8,128)S(1)} %dynamic-slice_bitcast_fusion.1), channel_id=1, source_target_pairs={{0,1},{1,0},{2,3},{3,2},{4,5},{5,4},{6,7},{7,6},{8,9},{9,8},{10,11... | collective-permute-start | bytes 221192 | tf_op jit(solution)/shard_map/ppermute | solution.py:310
  153.0 6.8 %collective-permute-start.6 = (f32[4,72,128]{2,1,0:T(8,128)S(1)}, f32[4,72,128]{2,1,0:T(8,128)S(1)}, u32[]{:S(2)}, u32[]{:S(2)}) collective-permute-start(f32[4,72,128]{2,1,0:T(8,128)S(1)} %dynamic-slice_bitcast_fusion), channel_id=1, source_target_pairs={{0,1},{1,0},{2,3},{3,2},{4,5},{5,4},{6,7},{7,6},{8,9},{9,8},{10,11... | collective-permute-start | bytes 442376 | tf_op jit(solution)/shard_map/ppermute | solution.py:310
Sparse Core Ops, SparseCore 0:
  27.4 42.4 all-gather.2
  104.5 47.5 reduce-scatter.3

commit v6 on v5

--- a/solution.py
+++ b/solution.py
@@ -25,7 +25,7 @@
 GRID = ("y", "zl")
 BATCH = 24
 SLABS = BATCH // SLAB
-VMEM_MIB = 58
+VMEM_MIB = 50
 NEAR = 4
 FAR = SLAB - NEAR
 PITCH = NG + 8

time: 170 us -> 171 us (level)
  waiting for transfers between devices: 26 us -> 28.5 us
  transfers between devices with their start and end apart: 11 -> 11, of which waited for: 8 -> 8; matrix products, arithmetic and copies ran while one was open for 19% -> 18% of each run, Pallas kernels for 0% -> 0%
where the time goes in v6:
time: 171 us; the launch traced here: 169 us
  blocking collectives  47.4 us (28%)
  starting transfers between devices  43.9 us (26%)
  waiting for transfers between devices  28.5 us (17%)
  Pallas kernels  22.5 us (13%)
  between operations  14.4 us (8%)
  local copies, waits for them, and re-layouts  8.68 us (5%)
  other arithmetic  3.81 us (2%)
    unnamed x1, blocking collectives  25.3 us
    pallas_call x1, Pallas kernels, pair_terms(): pl.pallas_call(pairs_kernel, grid_spec=pltpu.PrefetchScalarGridSpec(num_s...  22.5 us
    all_gather x2, blocking collectives, gathered(): return lax.all_gather(block, axis, axis=0, tiled=True)  22.1 us
    ppermute x4, starting transfers between devices, shifted(): return lax.ppermute(part, 'x', [(at, (at + by) % 4) for at in range(4)])  16.3 us
    ppermute x1, starting transfers between devices, exchanged_slabs(): return lax.ppermute(slab, AXES, pairs)  10.7 us
    reduce_scatter x1, waiting for transfers between devices, scattered(): return lax.psum_scatter(terms, 'y', scatter_dimension=0, tiled=True)  9.88 us
    ppermute x4, waiting for transfers between devices, shifted(): return lax.ppermute(part, 'x', [(at, (at + by) % 4) for at in range(4)])  8.63 us
    ppermute x2, starting transfers between devices, both_places(): return mine + lax.ppermute(other, 'zl', [(0, 1), (1, 0)])  7.19 us
  transfers between devices with their start and end apart: 11, of which 8 were waited for; matrix products, arithmetic and copies ran while one was open for 18% of the time, Pallas kernels for 0%

profile of v6, /device:TPU:1, one launch (start us, length us, event | category | flops | bytes accessed | tf_op | source)
XLA Modules:
  0.0 169.2 jit_solution(3401906221258612679)
XLA Ops:
  6.5 1.1 reshape.60
  7.8 10.7 %collective-permute-start = (bf16[432,128]{1,0:T(8,128)(2,1)S(1)}, bf16[432,128]{1,0:T(8,128)(2,1)S(1)}, u32[]{:S(2)}, u32[]{:S(2)}) collective-permute-start(bf16[432,128]{1,0:T(8,128)(2,1)S(1)} %bitcast.28), channel_id=1, source_target_pairs={{0,0},{1,128},{2,256},{3,384},{4,32},{5,160},{6,288},{7,416},{8,64... | collective-permute-start | bytes 331784 | tf_op jit(solution)/shard_map/ppermute | solution.py:277
  18.6 8.7 %all_gather.9 = bf16[864,128]{1,0:T(8,128)(2,1)} all-gather(bf16[432,128]{1,0:T(8,128)(2,1)S(1)} %bitcast.29), channel_id=1, replica_groups=mesh['zh'=4,'x'=4,'core'=2,'y'=8,'zl'=2] {'zl'}, dimensions={0}, use_global_device_ids=true | all-gather | bytes 331776 | tf_op jit(solution)/shard_map/all_gather | solution.py:299
  27.4 13.5 %all-gather = bf16[1728,128]{1,0:T(8,128)(2,1)S(1)} all-gather(bf16[432,128]{1,0:T(8,128)(2,1)S(1)} %collective-permute-done), channel_id=2, replica_groups=mesh['zh'=4,'x'=4,'core'=2,'y'=8,'zl'=2] {'zh'}, dimensions={0}, use_global_device_ids=true | all-gather | bytes 552960 | tf_op jit(solution)/shard_map/all_gather | solution.py:299
  40.8 5.4 %collective-permute-start.1 = (bf16[4,432,128]{2,1,0:T(8,128)(2,1)S(1)}, bf16[4,432,128]{2,1,0:T(8,128)(2,1)S(1)}, u32[]{:S(2)}, u32[]{:S(2)}) collective-permute-start(bf16[4,432,128]{2,1,0:T(8,128)(2,1)S(1)} %bitcast.25), channel_id=1, source_target_pairs={{0,32},{32,64},{64,96},{96,0},{1,33},{33,65},{65,97},{97,1},{2,34}... | collective-permute-start | bytes 1327112 | tf_op jit(solution)/shard_map/ppermute | solution.py:292
  46.3 4.4 %collective-permute-start.2 = (bf16[4,432,128]{2,1,0:T(8,128)(2,1)S(1)}, bf16[4,432,128]{2,1,0:T(8,128)(2,1)S(1)}, u32[]{:S(2)}, u32[]{:S(2)}) collective-permute-start(bf16[4,432,128]{2,1,0:T(8,128)(2,1)S(1)} %bitcast.26), channel_id=1, source_target_pairs={{0,96},{32,0},{64,32},{96,64},{1,97},{33,1},{65,33},{97,65},{2,98}... | collective-permute-start | bytes 1327112 | tf_op jit(solution)/shard_map/ppermute | solution.py:292
  50.7 5.8 %collective-permute-done.1 = bf16[4,432,128]{2,1,0:T(8,128)(2,1)S(1)} collective-permute-done((bf16[4,432,128]{2,1,0:T(8,128)(2,1)S(1)}, bf16[4,432,128]{2,1,0:T(8,128)(2,1)S(1)}, u32[]{:S(2)}, u32[]{:S(2)}) %collective-permute-start.1) | collective-permute-done | bytes 442400 | tf_op jit(solution)/shard_map/ppermute | solution.py:292
  56.5 1.9 %collective-permute-start.3 = (bf16[2,432,128]{2,1,0:T(8,128)(2,1)S(1)}, bf16[2,432,128]{2,1,0:T(8,128)(2,1)S(1)}, u32[]{:S(2)}, u32[]{:S(2)}) collective-permute-start(bf16[2,432,128]{2,1,0:T(8,128)(2,1)S(1)} %slice.56), channel_id=1, source_target_pairs={{0,32},{32,64},{64,96},{96,0},{1,33},{33,65},{65,97},{97,1},{2,34}... | collective-permute-start | bytes 663560 | tf_op jit(solution)/shard_map/ppermute | solution.py:292
  58.4 4.6 %collective-permute-start.4 = (bf16[2,432,128]{2,1,0:T(8,128)(2,1)S(1)}, bf16[2,432,128]{2,1,0:T(8,128)(2,1)S(1)}, u32[]{:S(2)}, u32[]{:S(2)}) collective-permute-start(bf16[2,432,128]{2,1,0:T(8,128)(2,1)S(1)} %slice.57), channel_id=1, source_target_pairs={{0,96},{32,0},{64,32},{96,64},{1,97},{33,1},{65,33},{97,65},{2,98}... | collective-permute-start | bytes 663560 | tf_op jit(solution)/shard_map/ppermute | solution.py:292
  63.0 1.7 %collective-permute-done.3 = bf16[2,432,128]{2,1,0:T(8,128)(2,1)S(1)} collective-permute-done((bf16[2,432,128]{2,1,0:T(8,128)(2,1)S(1)}, bf16[2,432,128]{2,1,0:T(8,128)(2,1)S(1)}, u32[]{:S(2)}, u32[]{:S(2)}) %collective-permute-start.3) | collective-permute-done | bytes 221216 | tf_op jit(solution)/shard_map/ppermute | solution.py:292
  64.7 1.2 collective-permute-done.4
  65.9 4.1 %all-gather.3.cloned.1.call-done = bf16[6912,128]{1,0:T(8,128)(2,1)} async-done(((bf16[864,128]{1,0:T(8,128)(2,1)}), bf16[6912,128]{1,0:T(8,128)(2,1)}) %all-gather.3.cloned.1.call-update) | async-done | bytes 1769488 | tf_op jit(solution)/shard_map/all_gather | solution.py:299
  73.8 6.1 %collective-permute-start.5 = (bf16[96,72,128]{2,1,0:T(8,128)(2,1)}, bf16[96,72,128]{2,1,0:T(8,128)(2,1)}, u32[]{:S(2)}, u32[]{:S(2)}) collective-permute-start(bf16[96,72,128]{2,1,0:T(8,128)(2,1)} %bitcast.6.refs_0_), channel_id=1, source_target_pairs={{0,16},{16,0},{1,17},{17,1},{2,18},{18,2},{3,19},{19,3},{4,20},{20... | collective-permute-start | bytes 5308424 | tf_op jit(solution)/shard_map/ppermute | solution.py:326
  80.3 2.3 %fusion.4.refs_4_ = f32[49,96,128]{2,1,0:T(8,128)} fusion(f32[128]{0:T(128)S(1)} %pad_multiply_fusion, f32[49,96]{1,0:T(8,128)S(1)} %broadcast_add_fusion), kind=kLoop, calls=%fused_computation.5 | loop fusion | flops 6021120 | bytes 2427776 | tf_op jit(solution)/shard_map/mul | solution.py:69
  82.6 1.0 collective-permute-done.5.refs_1_
  83.6 22.5 %pair_terms.1 = (f32[64,72,128]{2,1,0:T(8,128)}, f32[32,72,128]{2,1,0:T(8,128)S(1)}) custom-call(s32[2,5]{1,0:T(2,128)S(1)} %pad_add_fusion.order_ref, bf16[96,72,128]{2,1,0:T(8,128)(2,1)S(1)} %bitcast.23, bf16[96,72,128]{2,1,0:T(8,128)(2,1)} %bitcast.6.refs_0_, bf16[96,72,128]{2,1,0:T(8,128)(2,1)} %collective-permute-done.5.refs_1_, ...), custom_call_target="tpu_custom_call" | custom-call | flops 14495514624 | bytes 17000000 | tf_op jit(solution)/shard_map/pair_terms/pallas_call | solution.py:226
  106.3 25.3 %fusion = f32[40,1024]{1,0:T(8,128)S(1)} fusion(f32[288,1024]{1,0:T(8,128)S(1)} %reshape.66), kind=kCustom, calls=%all-reduce-scatter | all-reduce-scatter fusion | flops 327681 | bytes 1345536
  131.6 3.5 %collective-permute-start.8 = (f32[28,1024]{1,0:T(8,128)S(1)}, f32[28,1024]{1,0:T(8,128)S(1)}, u32[]{:S(2)}, u32[]{:S(2)}) collective-permute-start(f32[28,1024]{1,0:T(8,128)S(1)} %slice.64), channel_id=1, source_target_pairs={{0,2},{2,4},{4,6},{6,8},{8,10},{10,12},{12,14},{1,3},{3,5},{5,7},{... | collective-permute-start | bytes 344072
  135.1 1.3 dynamic-slice.4
  137.0 2.4 %collective-permute-done.8 = f32[28,1024]{1,0:T(8,128)S(1)} collective-permute-done((f32[28,1024]{1,0:T(8,128)S(1)}, f32[28,1024]{1,0:T(8,128)S(1)}, u32[]{:S(2)}, u32[]{:S(2)}) %collective-permute-start.8) | collective-permute-done | bytes 114720
  139.7 3.4 %collective-permute-start.7 = (f32[2,72,128]{2,1,0:T(8,128)S(1)}, f32[2,72,128]{2,1,0:T(8,128)S(1)}, u32[]{:S(2)}, u32[]{:S(2)}) collective-permute-start(f32[2,72,128]{2,1,0:T(8,128)S(1)} %dynamic-slice_bitcast_fusion.1), channel_id=1, source_target_pairs={{0,1},{1,0},{2,3},{3,2},{4,5},{5,4},{6,7},{7,6},{8,9},{9,8},{10,11... | collective-permute-start | bytes 221192 | tf_op jit(solution)/shard_map/ppermute | solution.py:310
  143.1 9.9 %reduce-scatter.4.cloned.1.call-done = f32[576,128]{1,0:T(8,128)} async-done(((f32[4608,128]{1,0:T(8,128)}), f32[576,128]{1,0:T(8,128)}) %reduce-scatter.4.cloned.1.call-update) | async-done | bytes 294928 | tf_op jit(solution)/shard_map/reduce_scatter | solution.py:303
  153.9 3.8 %collective-permute-start.6 = (f32[4,72,128]{2,1,0:T(8,128)S(1)}, f32[4,72,128]{2,1,0:T(8,128)S(1)}, u32[]{:S(2)}, u32[]{:S(2)}) collective-permute-start(f32[4,72,128]{2,1,0:T(8,128)S(1)} %dynamic-slice_bitcast_fusion), channel_id=1, source_target_pairs={{0,1},{1,0},{2,3},{3,2},{4,5},{5,4},{6,7},{7,6},{8,9},{9,8},{10,11... | collective-permute-start | bytes 442376 | tf_op jit(solution)/shard_map/ppermute | solution.py:310
  157.7 2.5 %collective-permute-done.6 = f32[4,72,128]{2,1,0:T(8,128)S(1)} collective-permute-done((f32[4,72,128]{2,1,0:T(8,128)S(1)}, f32[4,72,128]{2,1,0:T(8,128)S(1)}, u32[]{:S(2)}, u32[]{:S(2)}) %collective-permute-start.6) | collective-permute-done | bytes 147488 | tf_op jit(solution)/shard_map/ppermute | solution.py:310
  (44 shorter events, 8.0 us)
Async XLA Ops:
  6.5 63.4 %all-gather.3.cloned.1.call-start = ((), (), s32[]{:S(2)}) async-start(), calls=%async_computation.1 | async-start | bytes 1990656 | tf_op jit(solution)/shard_map/all_gather | solution.py:299
  7.8 19.4 %collective-permute-start = (bf16[432,128]{1,0:T(8,128)(2,1)S(1)}, bf16[432,128]{1,0:T(8,128)(2,1)S(1)}, u32[]{:S(2)}, u32[]{:S(2)}) collective-permute-start(bf16[432,128]{1,0:T(8,128)(2,1)S(1)} %bitcast.28), channel_id=1, source_target_pairs={{0,0},{1,128},{2,256},{3,384},{4,32},{5,160},{6,288},{7,416},{8,64... | collective-permute-start | bytes 331784 | tf_op jit(solution)/shard_map/ppermute | solution.py:277
  27.3 125.7 %reduce-scatter.4.cloned.1.call-start = ((), (), s32[]{:S(2)}) async-start(), calls=%async_computation.2 | async-start | bytes 2654208 | tf_op jit(solution)/shard_map/reduce_scatter | solution.py:303
  40.8 15.6 %collective-permute-start.1 = (bf16[4,432,128]{2,1,0:T(8,128)(2,1)S(1)}, bf16[4,432,128]{2,1,0:T(8,128)(2,1)S(1)}, u32[]{:S(2)}, u32[]{:S(2)}) collective-permute-start(bf16[4,432,128]{2,1,0:T(8,128)(2,1)S(1)} %bitcast.25), channel_id=1, source_target_pairs={{0,32},{32,64},{64,96},{96,0},{1,33},{33,65},{65,97},{97,1},{2,34}... | collective-permute-start | bytes 1327112 | tf_op jit(solution)/shard_map/ppermute | solution.py:292
  46.3 12.1 %collective-permute-start.2 = (bf16[4,432,128]{2,1,0:T(8,128)(2,1)S(1)}, bf16[4,432,128]{2,1,0:T(8,128)(2,1)S(1)}, u32[]{:S(2)}, u32[]{:S(2)}) collective-permute-start(bf16[4,432,128]{2,1,0:T(8,128)(2,1)S(1)} %bitcast.26), channel_id=1, source_target_pairs={{0,96},{32,0},{64,32},{96,64},{1,97},{33,1},{65,33},{97,65},{2,98}... | collective-permute-start | bytes 1327112 | tf_op jit(solution)/shard_map/ppermute | solution.py:292
  56.5 8.2 %collective-permute-start.3 = (bf16[2,432,128]{2,1,0:T(8,128)(2,1)S(1)}, bf16[2,432,128]{2,1,0:T(8,128)(2,1)S(1)}, u32[]{:S(2)}, u32[]{:S(2)}) collective-permute-start(bf16[2,432,128]{2,1,0:T(8,128)(2,1)S(1)} %slice.56), channel_id=1, source_target_pairs={{0,32},{32,64},{64,96},{96,0},{1,33},{33,65},{65,97},{97,1},{2,34}... | collective-permute-start | bytes 663560 | tf_op jit(solution)/shard_map/ppermute | solution.py:292
  58.4 7.4 %collective-permute-start.4 = (bf16[2,432,128]{2,1,0:T(8,128)(2,1)S(1)}, bf16[2,432,128]{2,1,0:T(8,128)(2,1)S(1)}, u32[]{:S(2)}, u32[]{:S(2)}) collective-permute-start(bf16[2,432,128]{2,1,0:T(8,128)(2,1)S(1)} %slice.57), channel_id=1, source_target_pairs={{0,96},{32,0},{64,32},{96,64},{1,97},{33,1},{65,33},{97,65},{2,98}... | collective-permute-start | bytes 663560 | tf_op jit(solution)/shard_map/ppermute | solution.py:292
  72.4 11.2 %copy-start = (bf16[6912,128]{1,0:T(8,128)(2,1)S(1)}, bf16[6912,128]{1,0:T(8,128)(2,1)}, u32[]{:S(2)}) copy-start(bf16[6912,128]{1,0:T(8,128)(2,1)} %all-gather.3.cloned.1.call-done) | copy-start | bytes 5308420
  72.4 11.2 %copy-start.1 = (bf16[256,256]{1,0:T(8,128)(2,1)S(1)}, bf16[256,256]{1,0:T(8,128)(2,1)}, u32[]{:S(2)}) copy-start(bf16[256,256]{1,0:T(8,128)(2,1)} %constant.126.clone.refs_2_) | copy-start | bytes 393220
  72.4 11.2 %copy-start.2 = (bf16[192,192]{1,0:T(8,128)(2,1)S(1)}, bf16[192,192]{1,0:T(8,128)(2,1)}, u32[]{:S(2)}) copy-start(bf16[192,192]{1,0:T(8,128)(2,1)} %constant.127.clone.refs_3_) | copy-start | bytes 221188
  73.8 9.8 %collective-permute-start.5 = (bf16[96,72,128]{2,1,0:T(8,128)(2,1)}, bf16[96,72,128]{2,1,0:T(8,128)(2,1)}, u32[]{:S(2)}, u32[]{:S(2)}) collective-permute-start(bf16[96,72,128]{2,1,0:T(8,128)(2,1)} %bitcast.6.refs_0_), channel_id=1, source_target_pairs={{0,16},{16,0},{1,17},{17,1},{2,18},{18,2},{3,19},{19,3},{4,20},{20... | collective-permute-start | bytes 5308424 | tf_op jit(solution)/shard_map/ppermute | solution.py:326
  131.6 7.8 %collective-permute-start.8 = (f32[28,1024]{1,0:T(8,128)S(1)}, f32[28,1024]{1,0:T(8,128)S(1)}, u32[]{:S(2)}, u32[]{:S(2)}) collective-permute-start(f32[28,1024]{1,0:T(8,128)S(1)} %slice.64), channel_id=1, source_target_pairs={{0,2},{2,4},{4,6},{6,8},{8,10},{10,12},{12,14},{1,3},{3,5},{5,7},{... | collective-permute-start | bytes 344072
  139.7 18.0 %collective-permute-start.7 = (f32[2,72,128]{2,1,0:T(8,128)S(1)}, f32[2,72,128]{2,1,0:T(8,128)S(1)}, u32[]{:S(2)}, u32[]{:S(2)}) collective-permute-start(f32[2,72,128]{2,1,0:T(8,128)S(1)} %dynamic-slice_bitcast_fusion.1), channel_id=1, source_target_pairs={{0,1},{1,0},{2,3},{3,2},{4,5},{5,4},{6,7},{7,6},{8,9},{9,8},{10,11... | collective-permute-start | bytes 221192 | tf_op jit(solution)/shard_map/ppermute | solution.py:310
  153.9 6.3 %collective-permute-start.6 = (f32[4,72,128]{2,1,0:T(8,128)S(1)}, f32[4,72,128]{2,1,0:T(8,128)S(1)}, u32[]{:S(2)}, u32[]{:S(2)}) collective-permute-start(f32[4,72,128]{2,1,0:T(8,128)S(1)} %dynamic-slice_bitcast_fusion), channel_id=1, source_target_pairs={{0,1},{1,0},{2,3},{3,2},{4,5},{5,4},{6,7},{7,6},{8,9},{9,8},{10,11... | collective-permute-start | bytes 442376 | tf_op jit(solution)/shard_map/ppermute | solution.py:310
Sparse Core Ops, SparseCore 0:
  27.4 42.4 all-gather.2
  106.3 46.6 reduce-scatter.3

commit v7 on v5

--- a/solution.py
+++ b/solution.py
@@ -320,7 +320,7 @@
     own = gathered(pair, "y").reshape(CUBE)
     blocks = gathered_x(gathered(visiting[None], "zh"))
     index = jnp.arange(NG, dtype=jnp.int32)
-    own, index, *blocks = lax.optimization_barrier((own, index, *blocks))
+    own, index = lax.optimization_barrier((own, index))
     kernel = kernel_table(index)
     first = jnp.concatenate(blocks).reshape(CUBE)
     second = lax.ppermute(first, "core", [(0, 1), (1, 0)])

time: 170 us -> 170 us (level)
  waiting for transfers between devices: 26 us -> 23.7 us
    all_gather x1, waiting for transfers between devices: 4.1 us -> 0.01 us  [gathered(): return lax.all_gather(block, axis, axis=0, tiled=True)]
    reduce_scatter x1, waiting for transfers between devices: 8.36 us -> 10.3 us  [scattered(): return lax.psum_scatter(terms, 'y', scatter_dimension=0, tiled=True)]
  transfers between devices with their start and end apart: 11 -> 11, of which waited for: 8 -> 7; matrix products, arithmetic and copies ran while one was open for 19% -> 19% of each run, Pallas kernels for 0% -> 0%
where the time goes in v7:
time: 170 us; the launch traced here: 167 us
  blocking collectives  48.1 us (28%)
  starting transfers between devices  45.9 us (27%)
  waiting for transfers between devices  23.7 us (14%)
  Pallas kernels  23.4 us (14%)
  between operations  14.4 us (8%)
  local copies, waits for them, and re-layouts  7.55 us (4%)
  other arithmetic  4.37 us (3%)
    unnamed x1, blocking collectives  26 us
    pallas_call x1, Pallas kernels, pair_terms(): pl.pallas_call(pairs_kernel, grid_spec=pltpu.PrefetchScalarGridSpec(num_s...  23.4 us
    all_gather x2, blocking collectives, gathered(): return lax.all_gather(block, axis, axis=0, tiled=True)  22.1 us
    ppermute x4, starting transfers between devices, shifted(): return lax.ppermute(part, 'x', [(at, (at + by) % 4) for at in range(4)])  16.3 us
    ppermute x1, starting transfers between devices, exchanged_slabs(): return lax.ppermute(slab, AXES, pairs)  10.7 us
    reduce_scatter x1, waiting for transfers between devices, scattered(): return lax.psum_scatter(terms, 'y', scatter_dimension=0, tiled=True)  10.3 us
    ppermute x2, starting transfers between devices, both_places(): return mine + lax.ppermute(other, 'zl', [(0, 1), (1, 0)])  9.61 us
    ppermute x4, waiting for transfers between devices, shifted(): return lax.ppermute(part, 'x', [(at, (at + by) % 4) for at in range(4)])  8.42 us
  transfers between devices with their start and end apart: 11, of which 7 were waited for; matrix products, arithmetic and copies ran while one was open for 19% of the time, Pallas kernels for 0%

profile of v7, /device:TPU:1, one launch (start us, length us, event | category | flops | bytes accessed | tf_op | source)
XLA Modules:
  0.0 167.5 jit_solution(3512034447584263210)
XLA Ops:
  6.5 1.1 reshape.60
  7.8 10.7 %collective-permute-start = (bf16[432,128]{1,0:T(8,128)(2,1)S(1)}, bf16[432,128]{1,0:T(8,128)(2,1)S(1)}, u32[]{:S(2)}, u32[]{:S(2)}) collective-permute-start(bf16[432,128]{1,0:T(8,128)(2,1)S(1)} %bitcast.27), channel_id=1, source_target_pairs={{0,0},{1,128},{2,256},{3,384},{4,32},{5,160},{6,288},{7,416},{8,64... | collective-permute-start | bytes 331784 | tf_op jit(solution)/shard_map/ppermute | solution.py:277
  18.6 8.7 %all_gather.9 = bf16[864,128]{1,0:T(8,128)(2,1)} all-gather(bf16[432,128]{1,0:T(8,128)(2,1)S(1)} %bitcast.28), channel_id=1, replica_groups=mesh['zh'=4,'x'=4,'core'=2,'y'=8,'zl'=2] {'zl'}, dimensions={0}, use_global_device_ids=true | all-gather | bytes 331776 | tf_op jit(solution)/shard_map/all_gather | solution.py:299
  27.4 13.5 %all-gather = bf16[1728,128]{1,0:T(8,128)(2,1)S(1)} all-gather(bf16[432,128]{1,0:T(8,128)(2,1)S(1)} %collective-permute-done), channel_id=2, replica_groups=mesh['zh'=4,'x'=4,'core'=2,'y'=8,'zl'=2] {'zh'}, dimensions={0}, use_global_device_ids=true | all-gather | bytes 552960 | tf_op jit(solution)/shard_map/all_gather | solution.py:299
  40.8 5.4 %collective-permute-start.1 = (bf16[4,432,128]{2,1,0:T(8,128)(2,1)S(1)}, bf16[4,432,128]{2,1,0:T(8,128)(2,1)S(1)}, u32[]{:S(2)}, u32[]{:S(2)}) collective-permute-start(bf16[4,432,128]{2,1,0:T(8,128)(2,1)S(1)} %bitcast.24), channel_id=1, source_target_pairs={{0,32},{32,64},{64,96},{96,0},{1,33},{33,65},{65,97},{97,1},{2,34}... | collective-permute-start | bytes 1327112 | tf_op jit(solution)/shard_map/ppermute | solution.py:292
  46.3 4.4 %collective-permute-start.2 = (bf16[4,432,128]{2,1,0:T(8,128)(2,1)S(1)}, bf16[4,432,128]{2,1,0:T(8,128)(2,1)S(1)}, u32[]{:S(2)}, u32[]{:S(2)}) collective-permute-start(bf16[4,432,128]{2,1,0:T(8,128)(2,1)S(1)} %bitcast.25), channel_id=1, source_target_pairs={{0,96},{32,0},{64,32},{96,64},{1,97},{33,1},{65,33},{97,65},{2,98}... | collective-permute-start | bytes 1327112 | tf_op jit(solution)/shard_map/ppermute | solution.py:292
  50.7 5.7 %collective-permute-done.1 = bf16[4,432,128]{2,1,0:T(8,128)(2,1)S(1)} collective-permute-done((bf16[4,432,128]{2,1,0:T(8,128)(2,1)S(1)}, bf16[4,432,128]{2,1,0:T(8,128)(2,1)S(1)}, u32[]{:S(2)}, u32[]{:S(2)}) %collective-permute-start.1) | collective-permute-done | bytes 442400 | tf_op jit(solution)/shard_map/ppermute | solution.py:292
  56.5 1.9 %collective-permute-start.3 = (bf16[2,432,128]{2,1,0:T(8,128)(2,1)S(1)}, bf16[2,432,128]{2,1,0:T(8,128)(2,1)S(1)}, u32[]{:S(2)}, u32[]{:S(2)}) collective-permute-start(bf16[2,432,128]{2,1,0:T(8,128)(2,1)S(1)} %slice.56), channel_id=1, source_target_pairs={{0,32},{32,64},{64,96},{96,0},{1,33},{33,65},{65,97},{97,1},{2,34}... | collective-permute-start | bytes 663560 | tf_op jit(solution)/shard_map/ppermute | solution.py:292
  58.4 4.6 %collective-permute-start.4 = (bf16[2,432,128]{2,1,0:T(8,128)(2,1)S(1)}, bf16[2,432,128]{2,1,0:T(8,128)(2,1)S(1)}, u32[]{:S(2)}, u32[]{:S(2)}) collective-permute-start(bf16[2,432,128]{2,1,0:T(8,128)(2,1)S(1)} %slice.57), channel_id=1, source_target_pairs={{0,96},{32,0},{64,32},{96,64},{1,97},{33,1},{65,33},{97,65},{2,98}... | collective-permute-start | bytes 663560 | tf_op jit(solution)/shard_map/ppermute | solution.py:292
  63.1 1.6 collective-permute-done.3
  64.7 1.1 collective-permute-done.4
  65.9 6.5 %collective-permute-start.5 = (bf16[96,72,128]{2,1,0:T(8,128)(2,1)S(1)}, bf16[96,72,128]{2,1,0:T(8,128)(2,1)S(1)}, u32[]{:S(2)}, u32[]{:S(2)}) collective-permute-start(bf16[96,72,128]{2,1,0:T(8,128)(2,1)S(1)} %bitcast.31), channel_id=1, source_target_pairs={{0,16},{16,0},{1,17},{17,1},{2,18},{18,2},{3,19},{19,3},{4,20},{20... | collective-permute-start | bytes 5308424 | tf_op jit(solution)/shard_map/ppermute | solution.py:326
  73.3 2.3 %fusion.4.refs_4_ = f32[49,96,128]{2,1,0:T(8,128)} fusion(f32[128]{0:T(128)S(1)} %pad_multiply_fusion, f32[49,96]{1,0:T(8,128)S(1)} %broadcast_add_fusion), kind=kLoop, calls=%fused_computation.5 | loop fusion | flops 6021120 | bytes 2427776 | tf_op jit(solution)/shard_map/mul | solution.py:69
  75.7 1.3 copy-done.2
  76.9 23.4 %pair_terms.1 = (f32[64,72,128]{2,1,0:T(8,128)}, f32[32,72,128]{2,1,0:T(8,128)}) custom-call(s32[2,5]{1,0:T(2,128)} %pad_add_fusion.order_ref, bf16[96,72,128]{2,1,0:T(8,128)(2,1)} %bitcast.34, bf16[96,72,128]{2,1,0:T(8,128)(2,1)} %bitcast.32, bf16[96,72,128]{2,1,0:T(8,128)(2,1)} %copy-done.2, bf16[256,256]{1,0:T(8,128)(2,1)} %constant.126.clone.refs_2_, ...), custom_call_target="tpu_custom_call" | custom-call | flops 14495514624 | bytes 17000000 | tf_op jit(solution)/shard_map/pair_terms/pallas_call | solution.py:226
  100.4 1.2 copy-done
  101.8 26.0 %fusion = f32[40,1024]{1,0:T(8,128)S(1)} fusion(f32[288,1024]{1,0:T(8,128)S(1)} %reshape.66), kind=kCustom, calls=%all-reduce-scatter | all-reduce-scatter fusion | flops 327681 | bytes 1345536
  127.8 2.7 %collective-permute-start.8 = (f32[28,1024]{1,0:T(8,128)S(1)}, f32[28,1024]{1,0:T(8,128)S(1)}, u32[]{:S(2)}, u32[]{:S(2)}) collective-permute-start(f32[28,1024]{1,0:T(8,128)S(1)} %slice.64), channel_id=1, source_target_pairs={{0,2},{2,4},{4,6},{6,8},{8,10},{10,12},{12,14},{1,3},{3,5},{5,7},{... | collective-permute-start | bytes 344072
  130.5 1.3 dynamic-slice.4
  132.4 2.3 %collective-permute-done.8 = f32[28,1024]{1,0:T(8,128)S(1)} collective-permute-done((f32[28,1024]{1,0:T(8,128)S(1)}, f32[28,1024]{1,0:T(8,128)S(1)}, u32[]{:S(2)}, u32[]{:S(2)}) %collective-permute-start.8) | collective-permute-done | bytes 114720
  135.1 4.4 %collective-permute-start.7 = (f32[2,72,128]{2,1,0:T(8,128)S(1)}, f32[2,72,128]{2,1,0:T(8,128)S(1)}, u32[]{:S(2)}, u32[]{:S(2)}) collective-permute-start(f32[2,72,128]{2,1,0:T(8,128)S(1)} %dynamic-slice_bitcast_fusion.1), channel_id=1, source_target_pairs={{0,1},{1,0},{2,3},{3,2},{4,5},{5,4},{6,7},{7,6},{8,9},{9,8},{10,11... | collective-permute-start | bytes 221192 | tf_op jit(solution)/shard_map/ppermute | solution.py:310
  139.5 10.3 %reduce-scatter.4.cloned.1.call-done = f32[576,128]{1,0:T(8,128)} async-done(((f32[4608,128]{1,0:T(8,128)}), f32[576,128]{1,0:T(8,128)}) %reduce-scatter.4.cloned.1.call-update) | async-done | bytes 294928 | tf_op jit(solution)/shard_map/reduce_scatter | solution.py:303
  150.8 5.2 %collective-permute-start.6 = (f32[4,72,128]{2,1,0:T(8,128)S(1)}, f32[4,72,128]{2,1,0:T(8,128)S(1)}, u32[]{:S(2)}, u32[]{:S(2)}) collective-permute-start(f32[4,72,128]{2,1,0:T(8,128)S(1)} %dynamic-slice_bitcast_fusion), channel_id=1, source_target_pairs={{0,1},{1,0},{2,3},{3,2},{4,5},{5,4},{6,7},{7,6},{8,9},{9,8},{10,11... | collective-permute-start | bytes 442376 | tf_op jit(solution)/shard_map/ppermute | solution.py:310
  156.0 2.5 %collective-permute-done.6 = f32[4,72,128]{2,1,0:T(8,128)S(1)} collective-permute-done((f32[4,72,128]{2,1,0:T(8,128)S(1)}, f32[4,72,128]{2,1,0:T(8,128)S(1)}, u32[]{:S(2)}, u32[]{:S(2)}) %collective-permute-start.6) | collective-permute-done | bytes 147488 | tf_op jit(solution)/shard_map/ppermute | solution.py:310
  (44 shorter events, 5.0 us)
Async XLA Ops:
  6.5 66.6 %all-gather.3.cloned.1.call-start = ((), (), s32[]{:S(2)}) async-start(), calls=%async_computation.1 | async-start | bytes 1990656 | tf_op jit(solution)/shard_map/all_gather | solution.py:299
  7.8 19.4 %collective-permute-start = (bf16[432,128]{1,0:T(8,128)(2,1)S(1)}, bf16[432,128]{1,0:T(8,128)(2,1)S(1)}, u32[]{:S(2)}, u32[]{:S(2)}) collective-permute-start(bf16[432,128]{1,0:T(8,128)(2,1)S(1)} %bitcast.27), channel_id=1, source_target_pairs={{0,0},{1,128},{2,256},{3,384},{4,32},{5,160},{6,288},{7,416},{8,64... | collective-permute-start | bytes 331784 | tf_op jit(solution)/shard_map/ppermute | solution.py:277
  27.3 122.5 %reduce-scatter.4.cloned.1.call-start = ((), (), s32[]{:S(2)}) async-start(), calls=%async_computation.2 | async-start | bytes 2654208 | tf_op jit(solution)/shard_map/reduce_scatter | solution.py:303
  40.8 15.6 %collective-permute-start.1 = (bf16[4,432,128]{2,1,0:T(8,128)(2,1)S(1)}, bf16[4,432,128]{2,1,0:T(8,128)(2,1)S(1)}, u32[]{:S(2)}, u32[]{:S(2)}) collective-permute-start(bf16[4,432,128]{2,1,0:T(8,128)(2,1)S(1)} %bitcast.24), channel_id=1, source_target_pairs={{0,32},{32,64},{64,96},{96,0},{1,33},{33,65},{65,97},{97,1},{2,34}... | collective-permute-start | bytes 1327112 | tf_op jit(solution)/shard_map/ppermute | solution.py:292
  46.3 12.1 %collective-permute-start.2 = (bf16[4,432,128]{2,1,0:T(8,128)(2,1)S(1)}, bf16[4,432,128]{2,1,0:T(8,128)(2,1)S(1)}, u32[]{:S(2)}, u32[]{:S(2)}) collective-permute-start(bf16[4,432,128]{2,1,0:T(8,128)(2,1)S(1)} %bitcast.25), channel_id=1, source_target_pairs={{0,96},{32,0},{64,32},{96,64},{1,97},{33,1},{65,33},{97,65},{2,98}... | collective-permute-start | bytes 1327112 | tf_op jit(solution)/shard_map/ppermute | solution.py:292
  56.5 8.2 %collective-permute-start.3 = (bf16[2,432,128]{2,1,0:T(8,128)(2,1)S(1)}, bf16[2,432,128]{2,1,0:T(8,128)(2,1)S(1)}, u32[]{:S(2)}, u32[]{:S(2)}) collective-permute-start(bf16[2,432,128]{2,1,0:T(8,128)(2,1)S(1)} %slice.56), channel_id=1, source_target_pairs={{0,32},{32,64},{64,96},{96,0},{1,33},{33,65},{65,97},{97,1},{2,34}... | collective-permute-start | bytes 663560 | tf_op jit(solution)/shard_map/ppermute | solution.py:292
  58.4 7.4 %collective-permute-start.4 = (bf16[2,432,128]{2,1,0:T(8,128)(2,1)S(1)}, bf16[2,432,128]{2,1,0:T(8,128)(2,1)S(1)}, u32[]{:S(2)}, u32[]{:S(2)}) collective-permute-start(bf16[2,432,128]{2,1,0:T(8,128)(2,1)S(1)} %slice.57), channel_id=1, source_target_pairs={{0,96},{32,0},{64,32},{96,64},{1,97},{33,1},{65,33},{97,65},{2,98}... | collective-permute-start | bytes 663560 | tf_op jit(solution)/shard_map/ppermute | solution.py:292
  65.9 9.8 %copy-start.1 = (bf16[16,432,128]{2,1,0:T(8,128)(2,1)}, bf16[16,432,128]{2,1,0:T(8,128)(2,1)S(1)}, u32[]{:S(2)}) copy-start(bf16[16,432,128]{2,1,0:T(8,128)(2,1)S(1)} %constant_dynamic-update-slice_fusion) | copy-start | bytes 5308420
  65.9 9.8 %collective-permute-start.5 = (bf16[96,72,128]{2,1,0:T(8,128)(2,1)S(1)}, bf16[96,72,128]{2,1,0:T(8,128)(2,1)S(1)}, u32[]{:S(2)}, u32[]{:S(2)}) collective-permute-start(bf16[96,72,128]{2,1,0:T(8,128)(2,1)S(1)} %bitcast.31), channel_id=1, source_target_pairs={{0,16},{16,0},{1,17},{17,1},{2,18},{18,2},{3,19},{19,3},{4,20},{20... | collective-permute-start | bytes 5308424 | tf_op jit(solution)/shard_map/ppermute | solution.py:326
  75.7 1.3 copy-start.2
  100.3 1.3 copy-start
  127.8 7.0 %collective-permute-start.8 = (f32[28,1024]{1,0:T(8,128)S(1)}, f32[28,1024]{1,0:T(8,128)S(1)}, u32[]{:S(2)}, u32[]{:S(2)}) collective-permute-start(f32[28,1024]{1,0:T(8,128)S(1)} %slice.64), channel_id=1, source_target_pairs={{0,2},{2,4},{4,6},{6,8},{8,10},{10,12},{12,14},{1,3},{3,5},{5,7},{... | collective-permute-start | bytes 344072
  135.1 20.9 %collective-permute-start.7 = (f32[2,72,128]{2,1,0:T(8,128)S(1)}, f32[2,72,128]{2,1,0:T(8,128)S(1)}, u32[]{:S(2)}, u32[]{:S(2)}) collective-permute-start(f32[2,72,128]{2,1,0:T(8,128)S(1)} %dynamic-slice_bitcast_fusion.1), channel_id=1, source_target_pairs={{0,1},{1,0},{2,3},{3,2},{4,5},{5,4},{6,7},{7,6},{8,9},{9,8},{10,11... | collective-permute-start | bytes 221192 | tf_op jit(solution)/shard_map/ppermute | solution.py:310
  150.8 7.7 %collective-permute-start.6 = (f32[4,72,128]{2,1,0:T(8,128)S(1)}, f32[4,72,128]{2,1,0:T(8,128)S(1)}, u32[]{:S(2)}, u32[]{:S(2)}) collective-permute-start(f32[4,72,128]{2,1,0:T(8,128)S(1)} %dynamic-slice_bitcast_fusion), channel_id=1, source_target_pairs={{0,1},{1,0},{2,3},{3,2},{4,5},{5,4},{6,7},{7,6},{8,9},{9,8},{10,11... | collective-permute-start | bytes 442376 | tf_op jit(solution)/shard_map/ppermute | solution.py:310
Sparse Core Ops, SparseCore 0:
  27.4 42.4 all-gather.2
  100.5 49.3 reduce-scatter.3

commit v8 on v7

--- a/solution.py
+++ b/solution.py
@@ -240,7 +240,7 @@
                 planes(count * SLABS, lambda i, order: clipped(i, 2 * steps)) for count in (NEAR, FAR)
             ],
             scratch_shapes=[
-                pltpu.VMEM((2 * NG * PITCH, LANES), F32),
+                pltpu.VMEM((2 * NG * PITCH + PITCH, LANES), F32),
                 pltpu.VMEM((NG // 2 + 1, NG, LANES), F32),
                 pltpu.SemaphoreType.DMA,
             ],

time: 170 us -> 170 us (level)
  no operation moved by 1% of the time
where the time goes in v8:
time: 170 us; the launch traced here: 167 us
  blocking collectives  48 us (28%)
  starting transfers between devices  46.1 us (27%)
  waiting for transfers between devices  23.7 us (14%)
  Pallas kernels  23.4 us (14%)
  between operations  14.4 us (8%)
  local copies, waits for them, and re-layouts  7.55 us (4%)
  other arithmetic  4.37 us (3%)
    unnamed x1, blocking collectives  25.8 us
    pallas_call x1, Pallas kernels, pair_terms(): pl.pallas_call(pairs_kernel, grid_spec=pltpu.PrefetchScalarGridSpec(num_s...  23.4 us
    all_gather x2, blocking collectives, gathered(): return lax.all_gather(block, axis, axis=0, tiled=True)  22.1 us
    ppermute x4, starting transfers between devices, shifted(): return lax.ppermute(part, 'x', [(at, (at + by) % 4) for at in range(4)])  16.3 us
    ppermute x1, starting transfers between devices, exchanged_slabs(): return lax.ppermute(slab, AXES, pairs)  10.7 us
    reduce_scatter x1, waiting for transfers between devices, scattered(): return lax.psum_scatter(terms, 'y', scatter_dimension=0, tiled=True)  10.4 us
    ppermute x2, starting transfers between devices, both_places(): return mine + lax.ppermute(other, 'zl', [(0, 1), (1, 0)])  9.86 us
    ppermute x4, waiting for transfers between devices, shifted(): return lax.ppermute(part, 'x', [(at, (at + by) % 4) for at in range(4)])  8.42 us
  transfers between devices with their start and end apart: 11, of which 7 were waited for; matrix products, arithmetic and copies ran while one was open for 19% of the time, Pallas kernels for 0%

profile of v8, /device:TPU:1, one launch (start us, length us, event | category | flops | bytes accessed | tf_op | source)
XLA Modules:
  0.0 167.5 jit_solution(2542801780986102507)
XLA Ops:
  6.5 1.1 reshape.60
  7.8 10.7 %collective-permute-start = (bf16[432,128]{1,0:T(8,128)(2,1)S(1)}, bf16[432,128]{1,0:T(8,128)(2,1)S(1)}, u32[]{:S(2)}, u32[]{:S(2)}) collective-permute-start(bf16[432,128]{1,0:T(8,128)(2,1)S(1)} %bitcast.27), channel_id=1, source_target_pairs={{0,0},{1,128},{2,256},{3,384},{4,32},{5,160},{6,288},{7,416},{8,64... | collective-permute-start | bytes 331784 | tf_op jit(solution)/shard_map/ppermute | solution.py:277
  18.6 8.7 %all_gather.9 = bf16[864,128]{1,0:T(8,128)(2,1)} all-gather(bf16[432,128]{1,0:T(8,128)(2,1)S(1)} %bitcast.28), channel_id=1, replica_groups=mesh['zh'=4,'x'=4,'core'=2,'y'=8,'zl'=2] {'zl'}, dimensions={0}, use_global_device_ids=true | all-gather | bytes 331776 | tf_op jit(solution)/shard_map/all_gather | solution.py:299
  27.4 13.5 %all-gather = bf16[1728,128]{1,0:T(8,128)(2,1)S(1)} all-gather(bf16[432,128]{1,0:T(8,128)(2,1)S(1)} %collective-permute-done), channel_id=2, replica_groups=mesh['zh'=4,'x'=4,'core'=2,'y'=8,'zl'=2] {'zh'}, dimensions={0}, use_global_device_ids=true | all-gather | bytes 552960 | tf_op jit(solution)/shard_map/all_gather | solution.py:299
  40.8 5.4 %collective-permute-start.1 = (bf16[4,432,128]{2,1,0:T(8,128)(2,1)S(1)}, bf16[4,432,128]{2,1,0:T(8,128)(2,1)S(1)}, u32[]{:S(2)}, u32[]{:S(2)}) collective-permute-start(bf16[4,432,128]{2,1,0:T(8,128)(2,1)S(1)} %bitcast.24), channel_id=1, source_target_pairs={{0,32},{32,64},{64,96},{96,0},{1,33},{33,65},{65,97},{97,1},{2,34}... | collective-permute-start | bytes 1327112 | tf_op jit(solution)/shard_map/ppermute | solution.py:292
  46.3 4.4 %collective-permute-start.2 = (bf16[4,432,128]{2,1,0:T(8,128)(2,1)S(1)}, bf16[4,432,128]{2,1,0:T(8,128)(2,1)S(1)}, u32[]{:S(2)}, u32[]{:S(2)}) collective-permute-start(bf16[4,432,128]{2,1,0:T(8,128)(2,1)S(1)} %bitcast.25), channel_id=1, source_target_pairs={{0,96},{32,0},{64,32},{96,64},{1,97},{33,1},{65,33},{97,65},{2,98}... | collective-permute-start | bytes 1327112 | tf_op jit(solution)/shard_map/ppermute | solution.py:292
  50.7 5.7 %collective-permute-done.1 = bf16[4,432,128]{2,1,0:T(8,128)(2,1)S(1)} collective-permute-done((bf16[4,432,128]{2,1,0:T(8,128)(2,1)S(1)}, bf16[4,432,128]{2,1,0:T(8,128)(2,1)S(1)}, u32[]{:S(2)}, u32[]{:S(2)}) %collective-permute-start.1) | collective-permute-done | bytes 442400 | tf_op jit(solution)/shard_map/ppermute | solution.py:292
  56.5 1.9 %collective-permute-start.3 = (bf16[2,432,128]{2,1,0:T(8,128)(2,1)S(1)}, bf16[2,432,128]{2,1,0:T(8,128)(2,1)S(1)}, u32[]{:S(2)}, u32[]{:S(2)}) collective-permute-start(bf16[2,432,128]{2,1,0:T(8,128)(2,1)S(1)} %slice.56), channel_id=1, source_target_pairs={{0,32},{32,64},{64,96},{96,0},{1,33},{33,65},{65,97},{97,1},{2,34}... | collective-permute-start | bytes 663560 | tf_op jit(solution)/shard_map/ppermute | solution.py:292
  58.4 4.6 %collective-permute-start.4 = (bf16[2,432,128]{2,1,0:T(8,128)(2,1)S(1)}, bf16[2,432,128]{2,1,0:T(8,128)(2,1)S(1)}, u32[]{:S(2)}, u32[]{:S(2)}) collective-permute-start(bf16[2,432,128]{2,1,0:T(8,128)(2,1)S(1)} %slice.57), channel_id=1, source_target_pairs={{0,96},{32,0},{64,32},{96,64},{1,97},{33,1},{65,33},{97,65},{2,98}... | collective-permute-start | bytes 663560 | tf_op jit(solution)/shard_map/ppermute | solution.py:292
  63.1 1.6 collective-permute-done.3
  64.7 1.1 collective-permute-done.4
  65.9 6.5 %collective-permute-start.5 = (bf16[96,72,128]{2,1,0:T(8,128)(2,1)S(1)}, bf16[96,72,128]{2,1,0:T(8,128)(2,1)S(1)}, u32[]{:S(2)}, u32[]{:S(2)}) collective-permute-start(bf16[96,72,128]{2,1,0:T(8,128)(2,1)S(1)} %bitcast.31), channel_id=1, source_target_pairs={{0,16},{16,0},{1,17},{17,1},{2,18},{18,2},{3,19},{19,3},{4,20},{20... | collective-permute-start | bytes 5308424 | tf_op jit(solution)/shard_map/ppermute | solution.py:326
  73.3 2.3 %fusion.4.refs_4_ = f32[49,96,128]{2,1,0:T(8,128)} fusion(f32[128]{0:T(128)S(1)} %pad_multiply_fusion, f32[49,96]{1,0:T(8,128)S(1)} %broadcast_add_fusion), kind=kLoop, calls=%fused_computation.5 | loop fusion | flops 6021120 | bytes 2427776 | tf_op jit(solution)/shard_map/mul | solution.py:69
  75.7 1.3 copy-done.2
  76.9 23.4 %pair_terms.1 = (f32[64,72,128]{2,1,0:T(8,128)}, f32[32,72,128]{2,1,0:T(8,128)}) custom-call(s32[2,5]{1,0:T(2,128)} %pad_add_fusion.order_ref, bf16[96,72,128]{2,1,0:T(8,128)(2,1)} %bitcast.34, bf16[96,72,128]{2,1,0:T(8,128)(2,1)} %bitcast.32, bf16[96,72,128]{2,1,0:T(8,128)(2,1)} %copy-done.2, bf16[256,256]{1,0:T(8,128)(2,1)} %constant.126.clone.refs_2_, ...), custom_call_target="tpu_custom_call" | custom-call | flops 14495514624 | bytes 17000000 | tf_op jit(solution)/shard_map/pair_terms/pallas_call | solution.py:226
  100.4 1.2 copy-done
  101.8 25.8 %fusion = f32[40,1024]{1,0:T(8,128)S(1)} fusion(f32[288,1024]{1,0:T(8,128)S(1)} %reshape.66), kind=kCustom, calls=%all-reduce-scatter | all-reduce-scatter fusion | flops 327681 | bytes 1345536
  127.7 2.7 %collective-permute-start.8 = (f32[28,1024]{1,0:T(8,128)S(1)}, f32[28,1024]{1,0:T(8,128)S(1)}, u32[]{:S(2)}, u32[]{:S(2)}) collective-permute-start(f32[28,1024]{1,0:T(8,128)S(1)} %slice.64), channel_id=1, source_target_pairs={{0,2},{2,4},{4,6},{6,8},{8,10},{10,12},{12,14},{1,3},{3,5},{5,7},{... | collective-permute-start | bytes 344072
  130.4 1.3 dynamic-slice.4
  132.3 2.2 %collective-permute-done.8 = f32[28,1024]{1,0:T(8,128)S(1)} collective-permute-done((f32[28,1024]{1,0:T(8,128)S(1)}, f32[28,1024]{1,0:T(8,128)S(1)}, u32[]{:S(2)}, u32[]{:S(2)}) %collective-permute-start.8) | collective-permute-done | bytes 114720
  134.7 4.8 %collective-permute-start.7 = (f32[2,72,128]{2,1,0:T(8,128)S(1)}, f32[2,72,128]{2,1,0:T(8,128)S(1)}, u32[]{:S(2)}, u32[]{:S(2)}) collective-permute-start(f32[2,72,128]{2,1,0:T(8,128)S(1)} %dynamic-slice_bitcast_fusion.1), channel_id=1, source_target_pairs={{0,1},{1,0},{2,3},{3,2},{4,5},{5,4},{6,7},{7,6},{8,9},{9,8},{10,11... | collective-permute-start | bytes 221192 | tf_op jit(solution)/shard_map/ppermute | solution.py:310
  139.5 10.4 %reduce-scatter.4.cloned.1.call-done = f32[576,128]{1,0:T(8,128)} async-done(((f32[4608,128]{1,0:T(8,128)}), f32[576,128]{1,0:T(8,128)}) %reduce-scatter.4.cloned.1.call-update) | async-done | bytes 294928 | tf_op jit(solution)/shard_map/reduce_scatter | solution.py:303
  150.9 5.1 %collective-permute-start.6 = (f32[4,72,128]{2,1,0:T(8,128)S(1)}, f32[4,72,128]{2,1,0:T(8,128)S(1)}, u32[]{:S(2)}, u32[]{:S(2)}) collective-permute-start(f32[4,72,128]{2,1,0:T(8,128)S(1)} %dynamic-slice_bitcast_fusion), channel_id=1, source_target_pairs={{0,1},{1,0},{2,3},{3,2},{4,5},{5,4},{6,7},{7,6},{8,9},{9,8},{10,11... | collective-permute-start | bytes 442376 | tf_op jit(solution)/shard_map/ppermute | solution.py:310
  156.0 2.5 %collective-permute-done.6 = f32[4,72,128]{2,1,0:T(8,128)S(1)} collective-permute-done((f32[4,72,128]{2,1,0:T(8,128)S(1)}, f32[4,72,128]{2,1,0:T(8,128)S(1)}, u32[]{:S(2)}, u32[]{:S(2)}) %collective-permute-start.6) | collective-permute-done | bytes 147488 | tf_op jit(solution)/shard_map/ppermute | solution.py:310
  (44 shorter events, 5.0 us)
Async XLA Ops:
  6.5 66.6 %all-gather.3.cloned.1.call-start = ((), (), s32[]{:S(2)}) async-start(), calls=%async_computation.1 | async-start | bytes 1990656 | tf_op jit(solution)/shard_map/all_gather | solution.py:299
  7.8 19.4 %collective-permute-start = (bf16[432,128]{1,0:T(8,128)(2,1)S(1)}, bf16[432,128]{1,0:T(8,128)(2,1)S(1)}, u32[]{:S(2)}, u32[]{:S(2)}) collective-permute-start(bf16[432,128]{1,0:T(8,128)(2,1)S(1)} %bitcast.27), channel_id=1, source_target_pairs={{0,0},{1,128},{2,256},{3,384},{4,32},{5,160},{6,288},{7,416},{8,64... | collective-permute-start | bytes 331784 | tf_op jit(solution)/shard_map/ppermute | solution.py:277
  27.3 122.6 %reduce-scatter.4.cloned.1.call-start = ((), (), s32[]{:S(2)}) async-start(), calls=%async_computation.2 | async-start | bytes 2654208 | tf_op jit(solution)/shard_map/reduce_scatter | solution.py:303
  40.8 15.6 %collective-permute-start.1 = (bf16[4,432,128]{2,1,0:T(8,128)(2,1)S(1)}, bf16[4,432,128]{2,1,0:T(8,128)(2,1)S(1)}, u32[]{:S(2)}, u32[]{:S(2)}) collective-permute-start(bf16[4,432,128]{2,1,0:T(8,128)(2,1)S(1)} %bitcast.24), channel_id=1, source_target_pairs={{0,32},{32,64},{64,96},{96,0},{1,33},{33,65},{65,97},{97,1},{2,34}... | collective-permute-start | bytes 1327112 | tf_op jit(solution)/shard_map/ppermute | solution.py:292
  46.3 12.1 %collective-permute-start.2 = (bf16[4,432,128]{2,1,0:T(8,128)(2,1)S(1)}, bf16[4,432,128]{2,1,0:T(8,128)(2,1)S(1)}, u32[]{:S(2)}, u32[]{:S(2)}) collective-permute-start(bf16[4,432,128]{2,1,0:T(8,128)(2,1)S(1)} %bitcast.25), channel_id=1, source_target_pairs={{0,96},{32,0},{64,32},{96,64},{1,97},{33,1},{65,33},{97,65},{2,98}... | collective-permute-start | bytes 1327112 | tf_op jit(solution)/shard_map/ppermute | solution.py:292
  56.5 8.2 %collective-permute-start.3 = (bf16[2,432,128]{2,1,0:T(8,128)(2,1)S(1)}, bf16[2,432,128]{2,1,0:T(8,128)(2,1)S(1)}, u32[]{:S(2)}, u32[]{:S(2)}) collective-permute-start(bf16[2,432,128]{2,1,0:T(8,128)(2,1)S(1)} %slice.56), channel_id=1, source_target_pairs={{0,32},{32,64},{64,96},{96,0},{1,33},{33,65},{65,97},{97,1},{2,34}... | collective-permute-start | bytes 663560 | tf_op jit(solution)/shard_map/ppermute | solution.py:292
  58.4 7.4 %collective-permute-start.4 = (bf16[2,432,128]{2,1,0:T(8,128)(2,1)S(1)}, bf16[2,432,128]{2,1,0:T(8,128)(2,1)S(1)}, u32[]{:S(2)}, u32[]{:S(2)}) collective-permute-start(bf16[2,432,128]{2,1,0:T(8,128)(2,1)S(1)} %slice.57), channel_id=1, source_target_pairs={{0,96},{32,0},{64,32},{96,64},{1,97},{33,1},{65,33},{97,65},{2,98}... | collective-permute-start | bytes 663560 | tf_op jit(solution)/shard_map/ppermute | solution.py:292
  65.9 9.8 %copy-start.1 = (bf16[16,432,128]{2,1,0:T(8,128)(2,1)}, bf16[16,432,128]{2,1,0:T(8,128)(2,1)S(1)}, u32[]{:S(2)}) copy-start(bf16[16,432,128]{2,1,0:T(8,128)(2,1)S(1)} %constant_dynamic-update-slice_fusion) | copy-start | bytes 5308420
  65.9 9.8 %collective-permute-start.5 = (bf16[96,72,128]{2,1,0:T(8,128)(2,1)S(1)}, bf16[96,72,128]{2,1,0:T(8,128)(2,1)S(1)}, u32[]{:S(2)}, u32[]{:S(2)}) collective-permute-start(bf16[96,72,128]{2,1,0:T(8,128)(2,1)S(1)} %bitcast.31), channel_id=1, source_target_pairs={{0,16},{16,0},{1,17},{17,1},{2,18},{18,2},{3,19},{19,3},{4,20},{20... | collective-permute-start | bytes 5308424 | tf_op jit(solution)/shard_map/ppermute | solution.py:326
  75.7 1.3 copy-start.2
  100.4 1.3 copy-start
  127.7 6.8 %collective-permute-start.8 = (f32[28,1024]{1,0:T(8,128)S(1)}, f32[28,1024]{1,0:T(8,128)S(1)}, u32[]{:S(2)}, u32[]{:S(2)}) collective-permute-start(f32[28,1024]{1,0:T(8,128)S(1)} %slice.64), channel_id=1, source_target_pairs={{0,2},{2,4},{4,6},{6,8},{8,10},{10,12},{12,14},{1,3},{3,5},{5,7},{... | collective-permute-start | bytes 344072
  134.7 21.2 %collective-permute-start.7 = (f32[2,72,128]{2,1,0:T(8,128)S(1)}, f32[2,72,128]{2,1,0:T(8,128)S(1)}, u32[]{:S(2)}, u32[]{:S(2)}) collective-permute-start(f32[2,72,128]{2,1,0:T(8,128)S(1)} %dynamic-slice_bitcast_fusion.1), channel_id=1, source_target_pairs={{0,1},{1,0},{2,3},{3,2},{4,5},{5,4},{6,7},{7,6},{8,9},{9,8},{10,11... | collective-permute-start | bytes 221192 | tf_op jit(solution)/shard_map/ppermute | solution.py:310
  150.9 7.6 %collective-permute-start.6 = (f32[4,72,128]{2,1,0:T(8,128)S(1)}, f32[4,72,128]{2,1,0:T(8,128)S(1)}, u32[]{:S(2)}, u32[]{:S(2)}) collective-permute-start(f32[4,72,128]{2,1,0:T(8,128)S(1)} %dynamic-slice_bitcast_fusion), channel_id=1, source_target_pairs={{0,1},{1,0},{2,3},{3,2},{4,5},{5,4},{6,7},{7,6},{8,9},{9,8},{10,11... | collective-permute-start | bytes 442376 | tf_op jit(solution)/shard_map/ppermute | solution.py:310
Sparse Core Ops, SparseCore 0:
  27.4 42.4 all-gather.2
  100.5 49.3 reduce-scatter.3
